TPU v7x, 128 devices: a whole 4x4x4 slice. The times are simulated.
128 devices in a mesh: trow: 16 (over x, y), tcol: 8 (over z, core).
Axes of the slice: x: 4, y: 4, z: 4, core: 2. Of those that a mesh axis runs over, the one named last changes fastest.
Arguments:
- ccd_image: bfloat16 [16, 8, 2, 512, 512], P('trow', 'tcol'), may hold values from -6 to 6
- ccd_variance: bfloat16 [16, 8, 2, 512, 512], P('trow', 'tcol'), may hold values from 0.25 to 4
- basis_taps: bfloat16 [6, 2, 21], replicated, may hold values from -1 to 1
- coef_table: float32 [8, 6], replicated, may hold values from -3 to 3
- coef_pick: int32 [16, 8, 2], P('trow', 'tcol'), may hold values from 0 to 7
- block_visit: int32 [16, 8, 2], P('trow', 'tcol'), may hold values from 0 to 7
- visit_weight: int32 [8], replicated, may hold values from 1 to 4
- patch_place: int32 [16, 8, 32], P('trow', 'tcol'), may hold values from 0 to 575, as said below
- psf_taps: float32 [2, 31], replicated, may hold values from 0.01 to 1
Outputs:
- coadd_image: float32 [16384, 8192], P('trow', 'tcol')
- significance: float32 [16384, 8192], P('trow', 'tcol')
Inputs may be any that keep to these rules, and one draw needn't show every extreme that they name: `patch_place`: every entry names a tile on the sky (the target device exists). From one device at most 4 squares go to each of its eight neighbour tiles, and one neighbour gets exactly 4; the rest stay on the device's own tile.
All inputs are finite; a program needn't handle non-finite values.
Results may differ from a plain program's by a relative error of at most 0.0042.
Values may be sent and summed in bfloat16 or wider, within the bound.
No kernel may reach another device: no remote copies, remote signals or barrier semaphores. Data moves between devices by JAX's collectives and lax.ppermute only.
A program may use at most 192 MiB of HBM per device.

v0:
```python
import functools
import jax
import jax.numpy as jnp
from jax import lax
from jax.experimental import pallas as pl
from jax.experimental.pallas import tpu as pltpu
from jax.sharding import PartitionSpec as P

F32 = jnp.float32
BF16 = jnp.bfloat16
BLOCK = 512
PATCH = 128
TAPS = 21
RADIUS = 10
PSF = 31
REACH = 15
NBASIS = 6
NP = 32
CAP = 4
GROUP = CAP * PATCH + 16
TILE = 1024
RIM = 16
STEP = 208
MIB = 1 << 20

SMEM = functools.partial(pl.BlockSpec, memory_space=pltpu.SMEM)


def iotas(shape):
    return (lax.broadcasted_iota(jnp.int32, shape, 0), lax.broadcasted_iota(jnp.int32, shape, 1))


def dot(a, b):
    return jnp.dot(a, b, preferred_element_type=F32)


def split(x):
    high = x.astype(BF16)
    return high, (x - high.astype(F32)).astype(BF16)


def diagonals(read, count, first, step, lanes):
    rows, cols = iotas((16, lanes))
    offset = (cols - rows) & (lanes - 1)
    out = jnp.zeros((16, lanes), F32)
    for t in range(count):
        out = jnp.where(offset == (first + step * t) % lanes, read(t), out)
    return out


def toeplitz(base, m, low, high):
    lanes = base.shape[1]
    turned = pltpu.roll(base, (16 * m) % lanes, 1) if (16 * m) % lanes else base
    rows, cols = iotas(base.shape)
    offset = cols - rows - 16 * m
    return jnp.where((offset >= low) & (offset <= high), turned, 0.0)


def corner(read, count, reach):
    rows, cols = iotas((32, 128))
    left = rows < 16
    tap = rows + 112 - cols + reach - jnp.where(left, 128, 0)
    tap = jnp.where(left == (cols < 64), tap, -1)
    out = jnp.zeros((32, 128), F32)
    for t in range(count):
        out = jnp.where(tap == t, read(t), out)
    return out


def match_kernel(
    squared, table, pick, visit, weight, place, taps, x_ref,
    up_ref, down_ref, left_ref, right_ref, own_ref,
    across, edges, down, rows_ref, total, heading, rank, slots,
):
    block = pl.program_id(0)

    def read(k, axis):
        return lambda t: taps[(2 * k + axis) * TAPS + t]

    def kept(x):
        return (x * x if squared else x).astype(BF16)

    @pl.when(block == 0)
    def _():
        for g in range(8):
            for s in range(CAP):
                slots[g * CAP + s] = -1

        def order(n, counts):
            entry = place[n]
            d = entry >> 6
            heading[n] = d
            r = jnp.int32(0)
            for g in range(9):
                r = jnp.where(d == g, counts[g], r)
            rank[n] = r

            @pl.when(d != 4)
            def _():
                slots[jnp.where(d > 4, d - 1, d) * CAP + r] = entry & 63

            return tuple(counts[g] + (d == g).astype(jnp.int32) for g in range(9))

        lax.fori_loop(0, NP, order, (jnp.int32(0),) * 9)
        _, lanes = iotas((16, 128))
        for g in range(8):
            line = jnp.full((16, 128), -1.0, F32)
            for s in range(CAP):
                line = jnp.where(lanes == s, slots[g * CAP + s].astype(F32), line)
            line = line.astype(BF16)
            last = pl.ds(CAP * PATCH, 16)
            if g < 3:
                up_ref[g, last, :] = line
            elif g == 3:
                left_ref[0, last, :] = line
            elif g == 4:
                right_ref[0, last, :] = line
            else:
                down_ref[g - 5, last, :] = line
        edges[...] = jnp.zeros(edges.shape, BF16)
        for k in range(NBASIS):
            base = diagonals(read(k, 0), TAPS, RADIUS, -1, 256)
            for m in range(16):
                across[k, pl.ds(16 * m, 16), :] = kept(toeplitz(base, m, -RADIUS, RADIUS))
            edges[k // 2, pl.ds(112, 32), pl.ds(k % 2 * 128, 128)] = kept(corner(read(k, 0), TAPS, RADIUS))
            base = diagonals(read(k, 1), TAPS, -26, 1, 256)
            for m in range(18):
                down[k, pl.ds(16 * m, 16), :] = kept(toeplitz(base, m, -26, -6))

    lanes = lax.broadcasted_iota(jnp.int32, (BLOCK, 128), 1)
    for pair in range(NBASIS // 2):
        fix = dot(x_ref[0, :, 128:384], edges[pair])
        for half in range(2):
            k = 2 * pair + half
            part = fix[:, 128 * half : 128 * half + 128]
            first = dot(x_ref[0, :, :256], across[k])
            rows_ref[k, :, 0:128] = first[:, :128].astype(BF16)
            rows_ref[k, :, 128:256] = (first[:, 128:] + jnp.where(lanes >= 64, part, 0.0)).astype(BF16)
            second = dot(x_ref[0, :, 256:], across[k])
            rows_ref[k, :, 256:384] = (second[:, :128] + jnp.where(lanes < 64, part, 0.0)).astype(BF16)
            rows_ref[k, :, 384:512] = second[:, 128:].astype(BF16)
    scale = weight[visit[block]].astype(F32)
    if squared:
        scale = scale * scale
    for side in range(2):
        span = pl.ds(256 * side, 256)
        for k in range(NBASIS):
            coef = table[pick[block], k]
            if squared:
                coef = coef * coef
            top = dot(down[k, 16:288, :], rows_ref[k, 0:256, span])
            low = dot(down[k, 0:272, :], rows_ref[k, 256:512, span])
            middle = top[240:] + low[:32]
            if k == 0:
                total[0:240, span] = coef * top[:240]
                total[240:272, span] = coef * middle
                total[272:512, span] = coef * low[32:]
            else:
                total[0:240, span] += coef * top[:240]
                total[240:272, span] += coef * middle
                total[272:512, span] += coef * low[32:]
    for i in range(4):
        for j in range(4):
            square = (scale * total[128 * i : 128 * i + 128, 128 * j : 128 * j + 128]).astype(BF16)
            n = block * 16 + 4 * i + j
            d = heading[n]
            where = pl.ds(pl.multiple_of(rank[n] * PATCH, PATCH), PATCH)

            @pl.when(d < 3)
            def _():
                up_ref[d, where, :] = square

            @pl.when(d == 3)
            def _():
                left_ref[0, where, :] = square

            @pl.when(d == 4)
            def _():
                own_ref[n] = square

            @pl.when(d == 5)
            def _():
                right_ref[0, where, :] = square

            @pl.when(d > 5)
            def _():
                down_ref[d - 6, where, :] = square


def match(squared, table, pick, visit, weight, place, taps, blocks):
    whole = lambda *shape: pl.BlockSpec(shape, lambda b: (0,) * len(shape))
    return pl.pallas_call(
        functools.partial(match_kernel, squared),
        grid=(2,),
        in_specs=[SMEM()] * 6 + [pl.BlockSpec((1, BLOCK, BLOCK), lambda b: (b, 0, 0))],
        out_specs=[whole(3, GROUP, 128), whole(3, GROUP, 128), whole(1, GROUP, 128), whole(1, GROUP, 128), whole(NP, PATCH, PATCH)],
        out_shape=[
            jax.ShapeDtypeStruct(s, BF16)
            for s in ((3, GROUP, 128), (3, GROUP, 128), (1, GROUP, 128), (1, GROUP, 128), (NP, PATCH, PATCH))
        ],
        scratch_shapes=[
            pltpu.VMEM((NBASIS, 256, 256), BF16),
            pltpu.VMEM((NBASIS // 2, 256, 256), BF16),
            pltpu.VMEM((NBASIS, 288, 256), BF16),
            pltpu.VMEM((NBASIS, BLOCK, BLOCK), BF16),
            pltpu.VMEM((BLOCK, BLOCK), F32),
            pltpu.SMEM((NP,), jnp.int32),
            pltpu.SMEM((NP,), jnp.int32),
            pltpu.SMEM((8 * CAP,), jnp.int32),
        ],
        compiler_params=pltpu.CompilerParams(vmem_limit_bytes=40 * MIB),
        name="match_var" if squared else "match_img",
    )(table, pick, visit, weight, place, taps, blocks)


def ring(value, axis, step):
    count = lax.axis_size(axis)
    return lax.ppermute(value, axis, [(i, (i + step) % count) for i in range(count)])


def exchange(parcels):
    up, down, left, right = parcels
    below = ring(up, "trow", -1)
    above = ring(down, "trow", 1)
    leftward = jnp.concatenate([left, below[0:1], above[0:1]], 0)
    rightward = jnp.concatenate([right, below[2:3], above[2:3]], 0)
    return below, above, ring(leftward, "tcol", -1), ring(rightward, "tcol", 1)


def gather_kernel(place, own_ref, below_ref, above_ref, east_ref, west_ref, tile_ref, top_ref, bottom_ref, lines, spots, sem):
    groups = [(below_ref, 0), (above_ref, 0)] + [(east_ref, g) for g in range(3)] + [(west_ref, g) for g in range(3)]
    for g, (ref, at) in enumerate(groups):
        lines[pl.ds(g, 1), :] = ref[at, CAP * PATCH :, :].astype(F32)[0:1].astype(jnp.int32)
    copy = pltpu.make_async_copy(lines, spots, sem)
    copy.start()
    tile_ref[...] = jnp.zeros(tile_ref.shape, F32)

    def add(spot, square):
        rows = pl.ds(pl.multiple_of((spot >> 3) * PATCH, PATCH), PATCH)
        cols = pl.ds(pl.multiple_of((spot & 7) * PATCH, PATCH), PATCH)
        tile_ref[rows, cols] += square.astype(F32)

    def own(n, _):
        entry = place[n]

        @pl.when((entry >> 6) == 4)
        def _():
            add(entry & 63, own_ref[n])

    lax.fori_loop(0, NP, own, None)
    copy.wait()
    for g, (ref, at) in enumerate(groups):
        for s in range(CAP):
            spot = spots[g, s]

            @pl.when(spot >= 0)
            def _():
                add(spot, ref[at, s * PATCH : (s + 1) * PATCH, :])

    top_ref[...] = tile_ref[0:RIM, :]
    bottom_ref[...] = tile_ref[TILE - RIM :, :]


def gather(name, place, own, below, above, east, west):
    middle = pl.BlockSpec((1, GROUP, 128), lambda i: (1, 0, 0))
    whole = lambda *shape: pl.BlockSpec(shape, lambda i: (0,) * len(shape))
    return pl.pallas_call(
        gather_kernel,
        grid=(1,),
        in_specs=[SMEM(), whole(NP, PATCH, PATCH), middle, middle, whole(3, GROUP, 128), whole(3, GROUP, 128)],
        out_specs=[whole(TILE, TILE), whole(RIM, TILE), whole(RIM, TILE)],
        out_shape=[jax.ShapeDtypeStruct(s, F32) for s in ((TILE, TILE), (RIM, TILE), (RIM, TILE))],
        scratch_shapes=[pltpu.VMEM((8, 128), jnp.int32), pltpu.SMEM((8, 128), jnp.int32), pltpu.SemaphoreType.DMA],
        compiler_params=pltpu.CompilerParams(vmem_limit_bytes=40 * MIB),
        name=name,
    )(place, own, below, above, east, west)


def psf_reader(squared, psf, axis):
    def read(t):
        tap = psf[axis * PSF + t]
        return tap * tap if squared else tap

    return read


def column_kernel(squared, psf, tile_ref, above_ref, below_ref, out_ref, first_ref, last_ref, band, high, low):
    step = pl.program_id(0)
    here, count = lax.axis_index("trow"), lax.axis_size("trow")

    @pl.when(step == 0)
    def _():
        base = diagonals(psf_reader(squared, psf, 1), PSF, 1, 1, 256)
        for m in range(STEP // 16):
            band[0, pl.ds(16 * m, 16), :], band[1, pl.ds(16 * m, 16), :] = split(toeplitz(base, m, 1, PSF))

    def put(at, value):
        high[pl.ds(at, value.shape[0]), :], low[pl.ds(at, value.shape[0]), :] = split(value)

    put(0, jnp.where(here > 0, above_ref[...], 0.0))
    put(RIM, tile_ref[...])
    put(RIM + TILE, jnp.where(here < count - 1, below_ref[...], 0.0))
    put(2 * RIM + TILE, jnp.zeros((32, 256), F32))
    for t in range(5):
        rows = min(STEP, TILE - STEP * t)
        window = pl.ds(STEP * t, 256)
        out_ref[pl.ds(STEP * t, rows), :] = (
            dot(band[0, :rows], high[window, :]) + dot(band[0, :rows], low[window, :]) + dot(band[1, :rows], high[window, :])
        )
    lanes = lax.broadcasted_iota(jnp.int32, (128, 128), 1)

    @pl.when(step == 0)
    def _():
        first_ref[...] = sum(
            pltpu.roll(jnp.where(lanes < RIM, out_ref[128 * g : 128 * g + 128, :128], 0.0), RIM * g, 1) for g in range(8)
        )

    @pl.when(step == 3)
    def _():
        last_ref[...] = sum(
            pltpu.roll(jnp.where(lanes >= 128 - RIM, out_ref[128 * g : 128 * g + 128, 128:], 0.0), (RIM * g + RIM) % 128, 1)
            for g in range(8)
        )


def column_pass(squared, psf, tile, above, below):
    strip = pl.BlockSpec((128, 128), lambda c: (0, 0))
    rim = pl.BlockSpec((RIM, 256), lambda c: (0, c))
    chunk = pl.BlockSpec((TILE, 256), lambda c: (0, c))
    return pl.pallas_call(
        functools.partial(column_kernel, squared),
        grid=(4,),
        in_specs=[SMEM(), chunk, rim, rim],
        out_specs=[chunk, strip, strip],
        out_shape=[jax.ShapeDtypeStruct(s, F32) for s in ((TILE, TILE), (128, 128), (128, 128))],
        scratch_shapes=[pltpu.VMEM((2, STEP, 256), BF16), pltpu.VMEM((1088, 256), BF16), pltpu.VMEM((1088, 256), BF16)],
        compiler_params=pltpu.CompilerParams(vmem_limit_bytes=40 * MIB),
        name="column_var" if squared else "column_img",
    )(psf, tile, above, below)


def row_kernel(squared, psf, v_ref, west_ref, east_ref, *rest):
    if squared:
        smooth_ref, out_ref, band, ends, high, low = rest
    else:
        out_ref, band, ends, high, low = rest
    step = pl.program_id(0)
    here, count = lax.axis_index("tcol"), lax.axis_size("tcol")

    @pl.when(step == 0)
    def _():
        read = psf_reader(squared, psf, 0)
        base = diagonals(read, PSF, REACH, -1, 256)
        for m in range(16):
            band[0, pl.ds(16 * m, 16), :], band[1, pl.ds(16 * m, 16), :] = split(toeplitz(base, m, -REACH, REACH))
        ends[...] = jnp.zeros(ends.shape, BF16)
        ends[pl.ds(112, 32), 0:128], ends[pl.ds(112, 32), 128:256] = split(corner(read, PSF, REACH))

    lanes = lax.broadcasted_iota(jnp.int32, (128, 128), 1)
    high[:, 128 : 128 + TILE], low[:, 128 : 128 + TILE] = split(v_ref[...])
    for part in range(2):
        g = 2 * step + part
        rows = pl.ds(128 * part, 128)
        piece = pltpu.roll(west_ref[...], (112 + 256 - RIM * g) & 127, 1)
        piece = jnp.where((lanes >= 112) & (here > 0), piece, 0.0)
        high[rows, 0:128], low[rows, 0:128] = split(piece)
        piece = pltpu.roll(east_ref[...], (256 - RIM * g) & 127, 1)
        piece = jnp.where((lanes < RIM) & (here < count - 1), piece, 0.0)
        high[rows, 128 + TILE :], low[rows, 128 + TILE :] = split(piece)
    lanes = lax.broadcasted_iota(jnp.int32, (256, 128), 1)
    fixes = []
    for w in range(5):
        window = pl.ds(256 * w, 256)
        both = dot(high[:, window], ends[...])
        fixes.append(both[:, :128] + both[:, 128:] + dot(low[:, window], ends[:, 0:128]))
    for c in range(4):
        window = pl.ds(128 + 256 * c, 256)
        main = dot(high[:, window], band[0]) + dot(low[:, window], band[0]) + dot(high[:, window], band[1])
        for part in range(2):
            fix = jnp.where(lanes >= 64, fixes[c + 1], 0.0) if part else jnp.where(lanes < 64, fixes[c], 0.0)
            value = main[:, 128 * part : 128 * part + 128] + fix
            cols = pl.ds(256 * c + 128 * part, 128)
            if squared:
                value = smooth_ref[:, cols] / jnp.sqrt(value + 1.0)
            out_ref[:, cols] = value


def row_pass(squared, psf, v, west, east, smooth=None):
    strip = pl.BlockSpec((128, 128), lambda r: (0, 0))
    chunk = pl.BlockSpec((256, TILE), lambda r: (r, 0))
    extra = (smooth,) if squared else ()
    return pl.pallas_call(
        functools.partial(row_kernel, squared),
        grid=(4,),
        in_specs=[SMEM(), chunk, strip, strip] + [chunk] * len(extra),
        out_specs=chunk,
        out_shape=jax.ShapeDtypeStruct((TILE, TILE), F32),
        scratch_shapes=[
            pltpu.VMEM((2, 256, 256), BF16),
            pltpu.VMEM((256, 256), BF16),
            pltpu.VMEM((256, TILE + 256), BF16),
            pltpu.VMEM((256, TILE + 256), BF16),
        ],
        compiler_params=pltpu.CompilerParams(vmem_limit_bytes=40 * MIB),
        name="row_var" if squared else "row_img",
    )(psf, v, west, east, *extra)


def shards(ccd_image, ccd_variance, basis_taps, coef_table, coef_pick, block_visit, visit_weight, patch_place, psf_taps):
    place = patch_place.reshape(NP)
    taps = basis_taps.astype(F32).reshape(-1)
    psf = psf_taps.reshape(-1)
    small = (coef_table, coef_pick.reshape(2), block_visit.reshape(2), visit_weight, place, taps)

    *parcels, own_image = match(False, *small, ccd_image.reshape(2, BLOCK, BLOCK))
    *parcels_var, own_var = match(True, *small, ccd_variance.reshape(2, BLOCK, BLOCK))
    tile, top, bottom = gather("gather_img", place, own_image, *exchange(parcels))
    tile_var, top_var, bottom_var = gather("gather_var", place, own_var, *exchange(parcels_var))
    v, first, last = column_pass(False, psf, tile, ring(bottom, "trow", 1), ring(top, "trow", -1))
    smooth = row_pass(False, psf, v, ring(last, "tcol", 1), ring(first, "tcol", -1))
    v, first, last = column_pass(True, psf, tile_var, ring(bottom_var, "trow", 1), ring(top_var, "trow", -1))
    significance = row_pass(True, psf, v, ring(last, "tcol", 1), ring(first, "tcol", -1), smooth)
    return tile, significance


def solution(mesh):
    place = P("trow", "tcol", None)
    blocks = P("trow", "tcol", None, None, None)
    in_specs = (blocks, blocks, P(), P(), place, place, P(), place, P())
    out_specs = (P("trow", "tcol"), P("trow", "tcol"))
    return jax.shard_map(shards, mesh=mesh, in_specs=in_specs, out_specs=out_specs, check_vma=False)
```

profile of v0, /device:TPU:0, one launch (start us, length us, event | category | flops | bytes accessed | tf_op | source)
XLA Modules:
  0.0 103.5 jit_solution(4697138652174918840)
XLA Ops:
  0.6 0.0 copy-start.7
  0.6 0.8 reshape.36.taps
  1.4 0.0 copy-start.3
  1.4 1.2 %copy-done.3 = bf16[1,1,2,512,512]{4,3,2,1,0:T(8,128)(2,1)S(1)} copy-done((bf16[1,1,2,512,512]{4,3,2,1,0:T(8,128)(2,1)S(1)}, bf16[1,1,2,512,512]{4,3,2,1,0:T(8,128)(2,1)}, u32[]{:S(2)}) %copy-start.3) | copy-done | bytes 1048600
  2.7 0.0 copy-start.5
  2.7 0.7 copy-done.5
  3.3 0.7 copy-done.6
  4.0 0.0 copy-start.8
  4.0 0.7 copy-done.8
  4.6 0.0 copy-start.9
  4.7 0.7 copy-done.9
  5.3 0.0 copy-start.10
  5.3 0.7 copy-done.10
  6.0 7.4 %match_var.1 = (bf16[3,528,128]{2,1,0:T(8,128)(2,1)S(1)}, bf16[3,528,128]{2,1,0:T(8,128)(2,1)S(1)}, bf16[1,528,128]{2,1,0:T(8,128)(2,1)S(1)}, bf16[1,528,128]{2,1,0:T(8,128)(2,1)S(1)}, bf16[32,128,128]{2,1,0:T(8,128)(2,1)S(1)}) custom-call(f32[8,6]{1,0:T(8,128)S(1)} %copy-done.5, s32[2]{0:T(128)S(1)} %bitcast.11, s32[2]{0:T(128)S(1)} %bitcast.13, ...), custom_call_target="tpu_custom_call" | custom-call | tf_op jit(solution)/shard_map/match_var/pallas_call | solution.py:192
  13.4 5.4 %collective-permute-start.4 = (bf16[3,528,128]{2,1,0:T(8,128)(2,1)S(1)}, bf16[3,528,128]{2,1,0:T(8,128)(2,1)S(1)}, u32[]{:S(2)}, u32[]{:S(2)}) collective-permute-start(bf16[3,528,128]{2,1,0:T(8,128)(2,1)S(1)} %get-tuple-element.31), channel_id=1, source_target_pairs={{0,120},{8,0},{16,8},{24,16},{32,24},{40,32},{48,40},{56,48},{64,5... | collective-permute-start | bytes 1216520 | tf_op jit(solution)/shard_map/ppermute | solution.py:218
  18.7 0.0 collective-permute-start.5
  18.7 0.0 copy-start.4
  18.7 1.2 %copy-done.4 = bf16[1,1,2,512,512]{4,3,2,1,0:T(8,128)(2,1)S(1)} copy-done((bf16[1,1,2,512,512]{4,3,2,1,0:T(8,128)(2,1)S(1)}, bf16[1,1,2,512,512]{4,3,2,1,0:T(8,128)(2,1)}, u32[]{:S(2)}) %copy-start.4) | copy-done | bytes 1048600
  20.0 7.3 %match_img.1 = (bf16[3,528,128]{2,1,0:T(8,128)(2,1)S(1)}, bf16[3,528,128]{2,1,0:T(8,128)(2,1)S(1)}, bf16[1,528,128]{2,1,0:T(8,128)(2,1)S(1)}, bf16[1,528,128]{2,1,0:T(8,128)(2,1)S(1)}, bf16[32,128,128]{2,1,0:T(8,128)(2,1)S(1)}) custom-call(f32[8,6]{1,0:T(8,128)S(1)} %copy-done.5, s32[2]{0:T(128)S(1)} %bitcast.12, s32[2]{0:T(128)S(1)} %bitcast.14, ...), custom_call_target="tpu_custom_call" | custom-call | tf_op jit(solution)/shard_map/match_img/pallas_call | solution.py:192
  27.3 5.4 %collective-permute-start = (bf16[3,528,128]{2,1,0:T(8,128)(2,1)S(1)}, bf16[3,528,128]{2,1,0:T(8,128)(2,1)S(1)}, u32[]{:S(2)}, u32[]{:S(2)}) collective-permute-start(bf16[3,528,128]{2,1,0:T(8,128)(2,1)S(1)} %get-tuple-element.25), channel_id=1, source_target_pairs={{0,120},{8,0},{16,8},{24,16},{32,24},{40,32},{48,40},{56,48},{64,5... | collective-permute-start | bytes 1216520 | tf_op jit(solution)/shard_map/ppermute | solution.py:218
  32.7 0.0 collective-permute-start.1
  32.7 0.0 collective-permute-done.4.below_ref
  32.7 0.2 collective-permute-done.5.above_ref
  33.0 2.5 %collective-permute-start.6 = (bf16[3,528,128]{2,1,0:T(8,128)(2,1)S(1)}, bf16[3,528,128]{2,1,0:T(8,128)(2,1)S(1)}, u32[]{:S(2)}, u32[]{:S(2)}) collective-permute-start(bf16[3,528,128]{2,1,0:T(8,128)(2,1)S(1)} %pad_maximum_fusion.2), channel_id=1, source_target_pairs={{0,7},{1,0},{2,1},{3,2},{4,3},{5,4},{6,5},{7,6},{8,15},{9,8},{10,9... | collective-permute-start | bytes 1216520 | tf_op jit(solution)/shard_map/ppermute | solution.py:218
  35.5 5.3 %collective-permute-done.below_ref = bf16[3,528,128]{2,1,0:T(8,128)(2,1)S(1)} collective-permute-done((bf16[3,528,128]{2,1,0:T(8,128)(2,1)S(1)}, bf16[3,528,128]{2,1,0:T(8,128)(2,1)S(1)}, u32[]{:S(2)}, u32[]{:S(2)}) %collective-permute-start) | collective-permute-done | bytes 405536 | tf_op jit(solution)/shard_map/ppermute | solution.py:218
  40.8 0.0 copy-start.11
  40.8 5.5 %collective-permute-done.1.above_ref = bf16[3,528,128]{2,1,0:T(8,128)(2,1)S(1)} collective-permute-done((bf16[3,528,128]{2,1,0:T(8,128)(2,1)S(1)}, bf16[3,528,128]{2,1,0:T(8,128)(2,1)S(1)}, u32[]{:S(2)}, u32[]{:S(2)}) %collective-permute-start.1) | collective-permute-done | bytes 405536 | tf_op jit(solution)/shard_map/ppermute | solution.py:218
  46.4 1.7 %collective-permute-start.2 = (bf16[3,528,128]{2,1,0:T(8,128)(2,1)S(1)}, bf16[3,528,128]{2,1,0:T(8,128)(2,1)S(1)}, u32[]{:S(2)}, u32[]{:S(2)}) collective-permute-start(bf16[3,528,128]{2,1,0:T(8,128)(2,1)S(1)} %pad_maximum_fusion), channel_id=1, source_target_pairs={{0,7},{1,0},{2,1},{3,2},{4,3},{5,4},{6,5},{7,6},{8,15},{9,8},{10,9... | collective-permute-start | bytes 1216520 | tf_op jit(solution)/shard_map/ppermute | solution.py:218
  48.2 0.0 collective-permute-start.3
  48.2 0.3 collective-permute-start.7
  48.6 5.0 %collective-permute-done.2.east_ref = bf16[3,528,128]{2,1,0:T(8,128)(2,1)S(1)} collective-permute-done((bf16[3,528,128]{2,1,0:T(8,128)(2,1)S(1)}, bf16[3,528,128]{2,1,0:T(8,128)(2,1)S(1)}, u32[]{:S(2)}, u32[]{:S(2)}) %collective-permute-start.2) | collective-permute-done | bytes 405536 | tf_op jit(solution)/shard_map/ppermute | solution.py:218
  53.5 3.2 %collective-permute-done.3.west_ref = bf16[3,528,128]{2,1,0:T(8,128)(2,1)S(1)} collective-permute-done((bf16[3,528,128]{2,1,0:T(8,128)(2,1)S(1)}, bf16[3,528,128]{2,1,0:T(8,128)(2,1)S(1)}, u32[]{:S(2)}, u32[]{:S(2)}) %collective-permute-start.3) | collective-permute-done | bytes 405536 | tf_op jit(solution)/shard_map/ppermute | solution.py:218
  56.7 0.0 copy-done.7
  56.7 3.9 %gather_img.1 = (f32[1024,1024]{1,0:T(8,128)}, f32[16,1024]{1,0:T(8,128)S(1)}, f32[16,1024]{1,0:T(8,128)S(1)}) custom-call(s32[32]{0:T(128)S(1)} %bitcast.9, bf16[32,128,128]{2,1,0:T(8,128)(2,1)S(1)} %get-tuple-element.24.own_ref, bf16[3,528,128]{2,1,0:T(8,128)(2,1)S(1)} %collective-permute-done.below_ref, ...), custom_call_target="tpu_custom_call" | custom-call | tf_op jit(solution)/shard_map/gather_img/pallas_call | solution.py:267
  60.6 0.1 collective-permute-start.12
  60.7 5.3 %collective-permute-start.13 = (f32[16,1024]{1,0:T(8,128)S(1)}, f32[16,1024]{1,0:T(8,128)S(1)}, u32[]{:S(2)}, u32[]{:S(2)}) collective-permute-start(f32[16,1024]{1,0:T(8,128)S(1)} %get-tuple-element.42), channel_id=1, source_target_pairs={{0,120},{8,0},{16,8},{24,16},{32,24},{40,32},{48,40},{56,48},{64,5... | collective-permute-start | bytes 196616 | tf_op jit(solution)/shard_map/ppermute | solution.py:218
  66.0 0.0 collective-permute-done.6.east_ref
  66.0 0.0 collective-permute-done.7.west_ref
  66.0 1.9 %gather_var.1 = (f32[1024,1024]{1,0:T(8,128)S(1)}, f32[16,1024]{1,0:T(8,128)S(1)}, f32[16,1024]{1,0:T(8,128)S(1)}) custom-call(s32[32]{0:T(128)S(1)} %bitcast.10, bf16[32,128,128]{2,1,0:T(8,128)(2,1)S(1)} %get-tuple-element.30.own_ref, bf16[3,528,128]{2,1,0:T(8,128)(2,1)S(1)} %collective-permute-done.4.below_ref, ...), custom_call_target="tpu_custom_call" | custom-call | tf_op jit(solution)/shard_map/gather_var/pallas_call | solution.py:267
  67.9 0.0 copy-start.1
  67.9 2.0 %copy-done.1 = f32[1024,1024]{1,0:T(8,128)} copy-done((f32[1024,1024]{1,0:T(8,128)}, f32[1024,1024]{1,0:T(8,128)S(1)}, u32[]{:S(2)}) %copy-start.1) | copy-done | bytes 4194328
  69.9 0.0 collective-permute-start.8
  69.9 5.3 %collective-permute-start.9 = (f32[16,1024]{1,0:T(8,128)S(1)}, f32[16,1024]{1,0:T(8,128)S(1)}, u32[]{:S(2)}, u32[]{:S(2)}) collective-permute-start(f32[16,1024]{1,0:T(8,128)S(1)} %get-tuple-element.37), channel_id=1, source_target_pairs={{0,120},{8,0},{16,8},{24,16},{32,24},{40,32},{48,40},{56,48},{64,5... | collective-permute-start | bytes 196616 | tf_op jit(solution)/shard_map/ppermute | solution.py:218
  75.3 0.0 copy-done.11
  75.3 0.1 reshape.33.psf
  75.4 0.0 collective-permute-done.12.above_ref
  75.4 0.0 collective-permute-done.13.below_ref
  75.4 0.0 copy-start
  75.4 2.2 %copy-done = f32[1024,1024]{1,0:T(8,128)S(1)} copy-done((f32[1024,1024]{1,0:T(8,128)S(1)}, f32[1024,1024]{1,0:T(8,128)}, u32[]{:S(2)}) %copy-start) | copy-done | bytes 4194328
  77.5 4.2 %column_img.1 = (f32[1024,1024]{1,0:T(8,128)S(1)}, f32[128,128]{1,0:T(8,128)S(1)}, f32[128,128]{1,0:T(8,128)S(1)}) custom-call(f32[62]{0:T(128)S(1)} %reshape.33.psf, f32[1024,1024]{1,0:T(8,128)S(1)} %copy-done, f32[16,1024]{1,0:T(8,128)S(1)} %collective-permute-done.12.above_ref, f32[16,1024]{1,0:T(8,128)S(1)} %collective-permute-done.13.below_ref), custom_call_target="tpu_custom_call" | custom-call | tf_op jit(solution)/shard_map/column_img/pallas_call | solution.py:330
  81.8 0.0 collective-permute-start.14
  81.8 2.9 %collective-permute-start.15 = (f32[128,128]{1,0:T(8,128)S(1)}, f32[128,128]{1,0:T(8,128)S(1)}, u32[]{:S(2)}, u32[]{:S(2)}) collective-permute-start(f32[128,128]{1,0:T(8,128)S(1)} %get-tuple-element.45), channel_id=1, source_target_pairs={{0,7},{1,0},{2,1},{3,2},{4,3},{5,4},{6,5},{7,6},{8,15},{9,8},{10,9... | collective-permute-start | bytes 196616 | tf_op jit(solution)/shard_map/ppermute | solution.py:218
  84.7 0.0 collective-permute-done.8.above_ref
  84.7 0.0 collective-permute-done.9.below_ref
  84.7 0.0 copy-done.2
  84.7 4.1 %column_var.1 = (f32[1024,1024]{1,0:T(8,128)S(1)}, f32[128,128]{1,0:T(8,128)S(1)}, f32[128,128]{1,0:T(8,128)S(1)}) custom-call(f32[62]{0:T(128)S(1)} %reshape.33.psf, f32[1024,1024]{1,0:T(8,128)S(1)} %copy-done.2, f32[16,1024]{1,0:T(8,128)S(1)} %collective-permute-done.8.above_ref, f32[16,1024]{1,0:T(8,128)S(1)} %collective-permute-done.9.below_ref), custom_call_target="tpu_custom_call" | custom-call | tf_op jit(solution)/shard_map/column_var/pallas_call | solution.py:330
  88.9 0.0 collective-permute-start.10
  88.9 2.9 %collective-permute-start.11 = (f32[128,128]{1,0:T(8,128)S(1)}, f32[128,128]{1,0:T(8,128)S(1)}, u32[]{:S(2)}, u32[]{:S(2)}) collective-permute-start(f32[128,128]{1,0:T(8,128)S(1)} %get-tuple-element.40), channel_id=1, source_target_pairs={{0,7},{1,0},{2,1},{3,2},{4,3},{5,4},{6,5},{7,6},{8,15},{9,8},{10,9... | collective-permute-start | bytes 196616 | tf_op jit(solution)/shard_map/ppermute | solution.py:218
  91.8 0.0 collective-permute-done.14.west_ref
  91.9 0.0 collective-permute-done.15.east_ref
  91.9 4.8 %row_img.1.rest_0_ = f32[1024,1024]{1,0:T(8,128)S(1)} custom-call(f32[62]{0:T(128)S(1)} %reshape.33.psf, f32[1024,1024]{1,0:T(8,128)S(1)} %get-tuple-element.43.v_ref, f32[128,128]{1,0:T(8,128)S(1)} %collective-permute-done.14.west_ref, f32[128,128]{1,0:T(8,128)S(1)} %collective-permute-done.15.east_ref), custom_call_target="tpu_custom_call" | custom-call | tf_op jit(solution)/shard_map/row_img/pallas_call | solution.py:392
  96.6 0.0 collective-permute-done.10.west_ref
  96.6 0.0 collective-permute-done.11.east_ref
  96.6 6.9 %row_var.1 = f32[1024,1024]{1,0:T(8,128)} custom-call(f32[62]{0:T(128)S(1)} %reshape.33.psf, f32[1024,1024]{1,0:T(8,128)S(1)} %get-tuple-element.38.v_ref, f32[128,128]{1,0:T(8,128)S(1)} %collective-permute-done.10.west_ref, f32[128,128]{1,0:T(8,128)S(1)} %collective-permute-done.11.east_ref, f32[1024,1024]{1,0:T(8,128)S(1)} %row_img.1.rest_0_), custom_call_target="tpu_custom_call" | custom-call | tf_op jit(solution)/shard_map/row_var/pallas_call | solution.py:392
  (10 shorter events, 0.3 us)
Async XLA Ops:
  0.6 56.1 %copy-start.7 = (s32[1,1,32]{2,1,0:T(1,128)S(1)}, s32[1,1,32]{2,1,0:T(1,128)}, u32[]{:S(2)}) copy-start(s32[1,1,32]{2,1,0:T(1,128)} %param.16) | copy-start | bytes 388
  1.4 1.2 %copy-start.3 = (bf16[1,1,2,512,512]{4,3,2,1,0:T(8,128)(2,1)S(1)}, bf16[1,1,2,512,512]{4,3,2,1,0:T(8,128)(2,1)}, u32[]{:S(2)}) copy-start(bf16[1,1,2,512,512]{4,3,2,1,0:T(8,128)(2,1)} %param.10) | copy-start | bytes 3145732
  2.7 0.7 copy-start.5
  3.3 0.7 copy-start.6
  4.0 0.7 copy-start.8
  4.6 0.7 copy-start.9
  5.3 0.7 copy-start.10
  13.4 19.3 %collective-permute-start.4 = (bf16[3,528,128]{2,1,0:T(8,128)(2,1)S(1)}, bf16[3,528,128]{2,1,0:T(8,128)(2,1)S(1)}, u32[]{:S(2)}, u32[]{:S(2)}) collective-permute-start(bf16[3,528,128]{2,1,0:T(8,128)(2,1)S(1)} %get-tuple-element.31), channel_id=1, source_target_pairs={{0,120},{8,0},{16,8},{24,16},{32,24},{40,32},{48,40},{56,48},{64,5... | collective-permute-start | bytes 1216520 | tf_op jit(solution)/shard_map/ppermute | solution.py:218
  18.7 14.2 %collective-permute-start.5 = (bf16[3,528,128]{2,1,0:T(8,128)(2,1)S(1)}, bf16[3,528,128]{2,1,0:T(8,128)(2,1)S(1)}, u32[]{:S(2)}, u32[]{:S(2)}) collective-permute-start(bf16[3,528,128]{2,1,0:T(8,128)(2,1)S(1)} %get-tuple-element.32), channel_id=1, source_target_pairs={{0,8},{8,16},{16,24},{24,32},{32,40},{40,48},{48,56},{56,64},{64,7... | collective-permute-start | bytes 1216520 | tf_op jit(solution)/shard_map/ppermute | solution.py:218
  18.7 1.2 %copy-start.4 = (bf16[1,1,2,512,512]{4,3,2,1,0:T(8,128)(2,1)S(1)}, bf16[1,1,2,512,512]{4,3,2,1,0:T(8,128)(2,1)}, u32[]{:S(2)}) copy-start(bf16[1,1,2,512,512]{4,3,2,1,0:T(8,128)(2,1)} %param.9) | copy-start | bytes 3145732
  27.3 13.5 %collective-permute-start = (bf16[3,528,128]{2,1,0:T(8,128)(2,1)S(1)}, bf16[3,528,128]{2,1,0:T(8,128)(2,1)S(1)}, u32[]{:S(2)}, u32[]{:S(2)}) collective-permute-start(bf16[3,528,128]{2,1,0:T(8,128)(2,1)S(1)} %get-tuple-element.25), channel_id=1, source_target_pairs={{0,120},{8,0},{16,8},{24,16},{32,24},{40,32},{48,40},{56,48},{64,5... | collective-permute-start | bytes 1216520 | tf_op jit(solution)/shard_map/ppermute | solution.py:218
  32.7 13.6 %collective-permute-start.1 = (bf16[3,528,128]{2,1,0:T(8,128)(2,1)S(1)}, bf16[3,528,128]{2,1,0:T(8,128)(2,1)S(1)}, u32[]{:S(2)}, u32[]{:S(2)}) collective-permute-start(bf16[3,528,128]{2,1,0:T(8,128)(2,1)S(1)} %get-tuple-element.26), channel_id=1, source_target_pairs={{0,8},{8,16},{16,24},{24,32},{32,40},{40,48},{48,56},{56,64},{64,7... | collective-permute-start | bytes 1216520 | tf_op jit(solution)/shard_map/ppermute | solution.py:218
  33.0 33.1 %collective-permute-start.6 = (bf16[3,528,128]{2,1,0:T(8,128)(2,1)S(1)}, bf16[3,528,128]{2,1,0:T(8,128)(2,1)S(1)}, u32[]{:S(2)}, u32[]{:S(2)}) collective-permute-start(bf16[3,528,128]{2,1,0:T(8,128)(2,1)S(1)} %pad_maximum_fusion.2), channel_id=1, source_target_pairs={{0,7},{1,0},{2,1},{3,2},{4,3},{5,4},{6,5},{7,6},{8,15},{9,8},{10,9... | collective-permute-start | bytes 1216520 | tf_op jit(solution)/shard_map/ppermute | solution.py:218
  40.8 34.5 %copy-start.11 = (f32[2,31]{1,0:T(2,128)S(1)}, f32[2,31]{1,0:T(2,128)}, u32[]{:S(2)}) copy-start(f32[2,31]{1,0:T(2,128)} %param.17) | copy-start | bytes 748
  46.4 7.2 %collective-permute-start.2 = (bf16[3,528,128]{2,1,0:T(8,128)(2,1)S(1)}, bf16[3,528,128]{2,1,0:T(8,128)(2,1)S(1)}, u32[]{:S(2)}, u32[]{:S(2)}) collective-permute-start(bf16[3,528,128]{2,1,0:T(8,128)(2,1)S(1)} %pad_maximum_fusion), channel_id=1, source_target_pairs={{0,7},{1,0},{2,1},{3,2},{4,3},{5,4},{6,5},{7,6},{8,15},{9,8},{10,9... | collective-permute-start | bytes 1216520 | tf_op jit(solution)/shard_map/ppermute | solution.py:218
  48.2 8.6 %collective-permute-start.3 = (bf16[3,528,128]{2,1,0:T(8,128)(2,1)S(1)}, bf16[3,528,128]{2,1,0:T(8,128)(2,1)S(1)}, u32[]{:S(2)}, u32[]{:S(2)}) collective-permute-start(bf16[3,528,128]{2,1,0:T(8,128)(2,1)S(1)} %pad_maximum_fusion.1), channel_id=1, source_target_pairs={{0,1},{1,2},{2,3},{3,4},{4,5},{5,6},{6,7},{7,0},{8,9},{9,10},{10,1... | collective-permute-start | bytes 1216520 | tf_op jit(solution)/shard_map/ppermute | solution.py:218
  48.2 17.8 %collective-permute-start.7 = (bf16[3,528,128]{2,1,0:T(8,128)(2,1)S(1)}, bf16[3,528,128]{2,1,0:T(8,128)(2,1)S(1)}, u32[]{:S(2)}, u32[]{:S(2)}) collective-permute-start(bf16[3,528,128]{2,1,0:T(8,128)(2,1)S(1)} %pad_maximum_fusion.3), channel_id=1, source_target_pairs={{0,1},{1,2},{2,3},{3,4},{4,5},{5,6},{6,7},{7,0},{8,9},{9,10},{10,1... | collective-permute-start | bytes 1216520 | tf_op jit(solution)/shard_map/ppermute | solution.py:218
  60.6 14.7 %collective-permute-start.12 = (f32[16,1024]{1,0:T(8,128)S(1)}, f32[16,1024]{1,0:T(8,128)S(1)}, u32[]{:S(2)}, u32[]{:S(2)}) collective-permute-start(f32[16,1024]{1,0:T(8,128)S(1)} %get-tuple-element.41), channel_id=1, source_target_pairs={{0,8},{8,16},{16,24},{24,32},{32,40},{40,48},{48,56},{56,64},{64,7... | collective-permute-start | bytes 196616 | tf_op jit(solution)/shard_map/ppermute | solution.py:218
  60.7 14.7 %collective-permute-start.13 = (f32[16,1024]{1,0:T(8,128)S(1)}, f32[16,1024]{1,0:T(8,128)S(1)}, u32[]{:S(2)}, u32[]{:S(2)}) collective-permute-start(f32[16,1024]{1,0:T(8,128)S(1)} %get-tuple-element.42), channel_id=1, source_target_pairs={{0,120},{8,0},{16,8},{24,16},{32,24},{40,32},{48,40},{56,48},{64,5... | collective-permute-start | bytes 196616 | tf_op jit(solution)/shard_map/ppermute | solution.py:218
  67.9 2.0 %copy-start.1 = (f32[1024,1024]{1,0:T(8,128)}, f32[1024,1024]{1,0:T(8,128)S(1)}, u32[]{:S(2)}) copy-start(f32[1024,1024]{1,0:T(8,128)S(1)} %get-tuple-element.35.tile_ref) | copy-start | bytes 12582916
  69.9 14.8 %collective-permute-start.8 = (f32[16,1024]{1,0:T(8,128)S(1)}, f32[16,1024]{1,0:T(8,128)S(1)}, u32[]{:S(2)}, u32[]{:S(2)}) collective-permute-start(f32[16,1024]{1,0:T(8,128)S(1)} %get-tuple-element.36), channel_id=1, source_target_pairs={{0,8},{8,16},{16,24},{24,32},{32,40},{40,48},{48,56},{56,64},{64,7... | collective-permute-start | bytes 196616 | tf_op jit(solution)/shard_map/ppermute | solution.py:218
  69.9 14.8 %collective-permute-start.9 = (f32[16,1024]{1,0:T(8,128)S(1)}, f32[16,1024]{1,0:T(8,128)S(1)}, u32[]{:S(2)}, u32[]{:S(2)}) collective-permute-start(f32[16,1024]{1,0:T(8,128)S(1)} %get-tuple-element.37), channel_id=1, source_target_pairs={{0,120},{8,0},{16,8},{24,16},{32,24},{40,32},{48,40},{56,48},{64,5... | collective-permute-start | bytes 196616 | tf_op jit(solution)/shard_map/ppermute | solution.py:218
  75.4 2.2 %copy-start = (f32[1024,1024]{1,0:T(8,128)S(1)}, f32[1024,1024]{1,0:T(8,128)}, u32[]{:S(2)}) copy-start(f32[1024,1024]{1,0:T(8,128)} %get-tuple-element.22.tile_ref) | copy-start | bytes 12582916
  77.5 7.2 %copy-start.2 = (f32[1024,1024]{1,0:T(8,128)S(1)}, f32[1024,1024]{1,0:T(8,128)}, u32[]{:S(2)}) copy-start(f32[1024,1024]{1,0:T(8,128)} %copy-done.1) | copy-start | bytes 12582916
  81.8 10.1 %collective-permute-start.14 = (f32[128,128]{1,0:T(8,128)S(1)}, f32[128,128]{1,0:T(8,128)S(1)}, u32[]{:S(2)}, u32[]{:S(2)}) collective-permute-start(f32[128,128]{1,0:T(8,128)S(1)} %get-tuple-element.44), channel_id=1, source_target_pairs={{0,1},{1,2},{2,3},{3,4},{4,5},{5,6},{6,7},{7,0},{8,9},{9,10},{10,1... | collective-permute-start | bytes 196616 | tf_op jit(solution)/shard_map/ppermute | solution.py:218
  81.8 10.1 %collective-permute-start.15 = (f32[128,128]{1,0:T(8,128)S(1)}, f32[128,128]{1,0:T(8,128)S(1)}, u32[]{:S(2)}, u32[]{:S(2)}) collective-permute-start(f32[128,128]{1,0:T(8,128)S(1)} %get-tuple-element.45), channel_id=1, source_target_pairs={{0,7},{1,0},{2,1},{3,2},{4,3},{5,4},{6,5},{7,6},{8,15},{9,8},{10,9... | collective-permute-start | bytes 196616 | tf_op jit(solution)/shard_map/ppermute | solution.py:218
  88.9 7.8 %collective-permute-start.10 = (f32[128,128]{1,0:T(8,128)S(1)}, f32[128,128]{1,0:T(8,128)S(1)}, u32[]{:S(2)}, u32[]{:S(2)}) collective-permute-start(f32[128,128]{1,0:T(8,128)S(1)} %get-tuple-element.39), channel_id=1, source_target_pairs={{0,1},{1,2},{2,3},{3,4},{4,5},{5,6},{6,7},{7,0},{8,9},{9,10},{10,1... | collective-permute-start | bytes 196616 | tf_op jit(solution)/shard_map/ppermute | solution.py:218
  88.9 7.7 %collective-permute-start.11 = (f32[128,128]{1,0:T(8,128)S(1)}, f32[128,128]{1,0:T(8,128)S(1)}, u32[]{:S(2)}, u32[]{:S(2)}) collective-permute-start(f32[128,128]{1,0:T(8,128)S(1)} %get-tuple-element.40), channel_id=1, source_target_pairs={{0,7},{1,0},{2,1},{3,2},{4,3},{5,4},{6,5},{7,6},{8,15},{9,8},{10,9... | collective-permute-start | bytes 196616 | tf_op jit(solution)/shard_map/ppermute | solution.py:218
where the time goes:
time: 104 us
  Pallas kernels  40.4 us (39%)
  starting transfers between devices  32 us (31%)
  waiting for transfers between devices  19.1 us (18%)
  local copies, waits for them, and re-layouts  10.9 us (10%)
    ppermute x16, starting transfers between devices, ring(): lax.ppermute(value, axis, [(i, (i + step) % count) for i in range(count)])  32 us
    ppermute x16, waiting for transfers between devices, ring(): lax.ppermute(value, axis, [(i, (i + step) % count) for i in range(count)])  19.1 us
    pallas_call x2, Pallas kernels, match(): pl.pallas_call(functools.partial(match_kernel, squared), grid=(2,), in_sp...  14.7 us
    pallas_call x2, Pallas kernels, row_pass(): pl.pallas_call(functools.partial(row_kernel, squared), grid=(4,), in_spec...  11.6 us
    unnamed x24, local copies, waits for them, and re-layouts  9.97 us
    pallas_call x2, Pallas kernels, column_pass(): pl.pallas_call(functools.partial(column_kernel, squared), grid=(4,), in_s...  8.33 us
    pallas_call x2, Pallas kernels, gather(): pl.pallas_call(gather_kernel, grid=(1,), in_specs=[SMEM(), whole(NP, PATC...  5.74 us
  transfers between devices with their start and end apart: 16, of which 5 were waited for; matrix products, arithmetic and copies ran while one was open for 0% of the time, Pallas kernels for 25%

commit v1 on v0

v1 whole, which is shorter than its diff:
```python
import functools
import jax
import jax.numpy as jnp
from jax import lax
from jax.experimental import pallas as pl
from jax.experimental.pallas import tpu as pltpu
from jax.sharding import PartitionSpec as P

F32 = jnp.float32
BF16 = jnp.bfloat16
BLOCK = 512
PATCH = 128
TAPS = 21
RADIUS = 10
PSF = 31
REACH = 15
NBASIS = 6
NP = 32
CAP = 4
GROUP = CAP * PATCH + 16
TILE = 1024
RIM = 16
STEP = 208
MIB = 1 << 20

HBM = pl.BlockSpec(memory_space=pltpu.HBM)
SMEM = functools.partial(pl.BlockSpec, memory_space=pltpu.SMEM)


def iotas(shape):
    return (lax.broadcasted_iota(jnp.int32, shape, 0), lax.broadcasted_iota(jnp.int32, shape, 1))


def dot(a, b):
    return jnp.dot(a, b, preferred_element_type=F32)


def split(x):
    high = x.astype(BF16)
    return high, (x - high.astype(F32)).astype(BF16)


def diagonals(read, count, first, step, lanes):
    rows, cols = iotas((16, lanes))
    offset = (cols - rows) & (lanes - 1)
    out = jnp.zeros((16, lanes), F32)
    for t in range(count):
        out = jnp.where(offset == (first + step * t) % lanes, read(t), out)
    return out


def toeplitz(base, m, low, high):
    lanes = base.shape[1]
    turned = pltpu.roll(base, (16 * m) % lanes, 1) if (16 * m) % lanes else base
    rows, cols = iotas(base.shape)
    offset = cols - rows - 16 * m
    return jnp.where((offset >= low) & (offset <= high), turned, 0.0)


def corner(read, count, reach):
    rows, cols = iotas((32, 128))
    left = rows < 16
    tap = rows + 112 - cols + reach - jnp.where(left, 128, 0)
    tap = jnp.where(left == (cols < 64), tap, -1)
    out = jnp.zeros((32, 128), F32)
    for t in range(count):
        out = jnp.where(tap == t, read(t), out)
    return out


def via(d):
    vertical = ((d * 11) >> 5) - 1
    sideways = d - 3 * ((d * 11) >> 5) - 1
    vertical = jnp.where((lax.axis_index("trow") & 1) == 0, -vertical, vertical)
    sideways = jnp.where((lax.axis_index("tcol") & 1) == 0, -sideways, sideways)
    return 3 * vertical + sideways + 4


def match_kernel(
    squared, table_in, pick_in, visit_in, weight_in, place_in, taps, x_in,
    up_ref, down_ref, left_ref, right_ref, own_ref,
    across, edges, down, rows_ref, total, heading, rank, slots,
    table, pick, visit, weight, place, x_ref, sems, x_sem,
):
    block = pl.program_id(0)
    small = [(table_in, table), (pick_in, pick), (visit_in, visit), (weight_in, weight), (place_in, place)]
    small = [pltpu.make_async_copy(a, b, sems.at[i]) for i, (a, b) in enumerate(small)]
    pixels = [pltpu.make_async_copy(x_in.at[b], x_ref.at[b], x_sem.at[b]) for b in range(2)]

    def read(k, axis):
        return lambda t: taps[(2 * k + axis) * TAPS + t]

    def kept(x):
        return (x * x if squared else x).astype(BF16)

    @pl.when(block == 0)
    def _():
        for copy in small + pixels:
            copy.start()
        edges[...] = jnp.zeros(edges.shape, BF16)
        for k in range(NBASIS):
            base = diagonals(read(k, 0), TAPS, RADIUS, -1, 256)
            for m in range(16):
                across[k, pl.ds(16 * m, 16), :] = kept(toeplitz(base, m, -RADIUS, RADIUS))
            edges[k // 2, pl.ds(112, 32), pl.ds(k % 2 * 128, 128)] = kept(corner(read(k, 0), TAPS, RADIUS))
            base = diagonals(read(k, 1), TAPS, -26, 1, 256)
            for m in range(18):
                down[k, pl.ds(16 * m, 16), :] = kept(toeplitz(base, m, -26, -6))
        for copy in small:
            copy.wait()
        for g in range(8):
            for s in range(CAP):
                slots[g * CAP + s] = -1

        def order(n, counts):
            entry = place[0, 0, n]
            d = via(entry >> 6)
            heading[n] = d
            r = jnp.int32(0)
            for g in range(9):
                r = jnp.where(d == g, counts[g], r)
            rank[n] = r

            @pl.when(d != 4)
            def _():
                slots[jnp.where(d > 4, d - 1, d) * CAP + r] = entry & 63

            return tuple(counts[g] + (d == g).astype(jnp.int32) for g in range(9))

        lax.fori_loop(0, NP, order, (jnp.int32(0),) * 9)
        _, lanes = iotas((16, 128))
        for g in range(8):
            line = jnp.full((16, 128), -1.0, F32)
            for s in range(CAP):
                line = jnp.where(lanes == s, slots[g * CAP + s].astype(F32), line)
            line = line.astype(BF16)
            last = pl.ds(CAP * PATCH, 16)
            if g < 3:
                up_ref[g, last, :] = line
            elif g == 3:
                left_ref[0, last, :] = line
            elif g == 4:
                right_ref[0, last, :] = line
            else:
                down_ref[g - 5, last, :] = line
        pixels[0].wait()

    @pl.when(block == 1)
    def _():
        pixels[1].wait()

    lanes = lax.broadcasted_iota(jnp.int32, (BLOCK, 128), 1)
    for pair in range(NBASIS // 2):
        fix = dot(x_ref[block, :, 128:384], edges[pair])
        for half in range(2):
            k = 2 * pair + half
            part = fix[:, 128 * half : 128 * half + 128]
            first = dot(x_ref[block, :, :256], across[k])
            rows_ref[k, :, 0:128] = first[:, :128].astype(BF16)
            rows_ref[k, :, 128:256] = (first[:, 128:] + jnp.where(lanes >= 64, part, 0.0)).astype(BF16)
            second = dot(x_ref[block, :, 256:], across[k])
            rows_ref[k, :, 256:384] = (second[:, :128] + jnp.where(lanes < 64, part, 0.0)).astype(BF16)
            rows_ref[k, :, 384:512] = second[:, 128:].astype(BF16)
    scale = weight[visit[0, 0, block]].astype(F32)
    if squared:
        scale = scale * scale
    for side in range(2):
        span = pl.ds(256 * side, 256)
        for k in range(NBASIS):
            coef = table[pick[0, 0, block], k]
            if squared:
                coef = coef * coef
            top = dot(down[k, 16:288, :], rows_ref[k, 0:256, span])
            low = dot(down[k, 0:272, :], rows_ref[k, 256:512, span])
            middle = top[240:] + low[:32]
            if k == 0:
                total[0:240, span] = coef * top[:240]
                total[240:272, span] = coef * middle
                total[272:512, span] = coef * low[32:]
            else:
                total[0:240, span] += coef * top[:240]
                total[240:272, span] += coef * middle
                total[272:512, span] += coef * low[32:]
    for i in range(4):
        for j in range(4):
            square = scale * total[128 * i : 128 * i + 128, 128 * j : 128 * j + 128]
            own_ref[block * 16 + 4 * i + j] = square.astype(BF16)

    def leave(i, _):
        n = block * 16 + i
        d = heading[n]
        where = pl.ds(pl.multiple_of(rank[n] * PATCH, PATCH), PATCH)

        @pl.when(d < 3)
        def _():
            up_ref[d, where, :] = own_ref[n]

        @pl.when(d == 3)
        def _():
            left_ref[0, where, :] = own_ref[n]

        @pl.when(d == 5)
        def _():
            right_ref[0, where, :] = own_ref[n]

        @pl.when(d > 5)
        def _():
            down_ref[d - 6, where, :] = own_ref[n]

    lax.fori_loop(0, 16, leave, None)


def match(squared, table, pick, visit, weight, place, taps, blocks):
    whole = lambda *shape: pl.BlockSpec(shape, lambda b: (0,) * len(shape))
    return pl.pallas_call(
        functools.partial(match_kernel, squared),
        grid=(2,),
        in_specs=[HBM] * 5 + [SMEM(), HBM],
        out_specs=[whole(3, GROUP, 128), whole(3, GROUP, 128), whole(1, GROUP, 128), whole(1, GROUP, 128), whole(NP, PATCH, PATCH)],
        out_shape=[
            jax.ShapeDtypeStruct(s, BF16)
            for s in ((3, GROUP, 128), (3, GROUP, 128), (1, GROUP, 128), (1, GROUP, 128), (NP, PATCH, PATCH))
        ],
        scratch_shapes=[
            pltpu.VMEM((NBASIS, 256, 256), BF16),
            pltpu.VMEM((NBASIS // 2, 256, 256), BF16),
            pltpu.VMEM((NBASIS, 288, 256), BF16),
            pltpu.VMEM((NBASIS, BLOCK, BLOCK), BF16),
            pltpu.VMEM((BLOCK, BLOCK), F32),
            pltpu.SMEM((NP,), jnp.int32),
            pltpu.SMEM((NP,), jnp.int32),
            pltpu.SMEM((8 * CAP,), jnp.int32),
            pltpu.SMEM(table.shape, F32),
            pltpu.SMEM(pick.shape, jnp.int32),
            pltpu.SMEM(visit.shape, jnp.int32),
            pltpu.SMEM(weight.shape, jnp.int32),
            pltpu.SMEM(place.shape, jnp.int32),
            pltpu.VMEM((2, BLOCK, BLOCK), BF16),
            pltpu.SemaphoreType.DMA((5,)),
            pltpu.SemaphoreType.DMA((2,)),
        ],
        compiler_params=pltpu.CompilerParams(vmem_limit_bytes=40 * MIB),
        name="match_var" if squared else "match_img",
    )(table, pick, visit, weight, place, taps, blocks)


def swap(value, axis, odd):
    rows, cols = lax.axis_size("trow"), lax.axis_size("tcol")
    pairs = []
    for r in range(rows):
        for c in range(cols):
            at, count = (r, rows) if axis == "trow" else (c, cols)
            to = ((at + 1) ^ 1) - 1 if odd else at ^ 1
            if axis == "trow":
                target = (to, c) if 0 <= to < count else (r, c ^ 1)
            else:
                target = (r, to) if 0 <= to < count else (r ^ 1, c)
            pairs.append((r * cols + c, target[0] * cols + target[1]))
    return lax.ppermute(value, ("trow", "tcol"), pairs)


def first_stage(parcels):
    return swap(parcels[0], "trow", False), swap(parcels[1], "trow", True)


def second_stage(parcels, below, above):
    _, _, left, right = parcels
    leftward = jnp.concatenate([left, below[0:1], above[0:1]], 0)
    rightward = jnp.concatenate([right, below[2:3], above[2:3]], 0)
    return below, above, swap(leftward, "tcol", False), swap(rightward, "tcol", True)


def pack(read, first):
    lanes = lax.broadcasted_iota(jnp.int32, (128, 128), 1)
    out = jnp.zeros((128, 128), F32)
    for g in range(8):
        rows = read(pl.ds(128 * g, 128))
        rows = jnp.where(lanes < RIM if first else lanes >= 128 - RIM, rows, 0.0)
        turn = RIM * g if first else (RIM * g + RIM) % 128
        out = out + (pltpu.roll(rows, turn, 1) if turn else rows)
    return out


def gather_kernel(image, place, own_ref, below_ref, above_ref, east_ref, west_ref, *rest):
    if image:
        tile_ref, up_ref, down_ref, first_ref, last_ref, lines, spots, sem = rest
    else:
        up_in, down_in, first_in, last_in, out_ref, up_ref, down_ref, first_ref, last_ref, lines, spots, sem, tile_ref = rest
    groups = [(below_ref, 0), (above_ref, 0)] + [(east_ref, g) for g in range(3)] + [(west_ref, g) for g in range(3)]
    for g, (ref, at) in enumerate(groups):
        lines[pl.ds(g, 1), :] = ref[at, CAP * PATCH :, :].astype(F32)[0:1].astype(jnp.int32)
    copy = pltpu.make_async_copy(lines, spots, sem)
    copy.start()
    tile_ref[...] = jnp.zeros(tile_ref.shape, F32)

    def add(spot, square):
        rows = pl.ds(pl.multiple_of((spot >> 3) * PATCH, PATCH), PATCH)
        cols = pl.ds(pl.multiple_of((spot & 7) * PATCH, PATCH), PATCH)
        tile_ref[rows, cols] += square.astype(F32)

    def own(n, _):
        entry = place[n]

        @pl.when((entry >> 6) == 4)
        def _():
            add(entry & 63, own_ref[n])

    lax.fori_loop(0, NP, own, None)
    copy.wait()
    for g, (ref, at) in enumerate(groups):
        for s in range(CAP):
            spot = spots[g, s]

            @pl.when(spot >= 0)
            def _():
                add(spot, ref[at, s * PATCH : (s + 1) * PATCH, :])

    first = pack(lambda rows: tile_ref[rows, :128], True)
    last = pack(lambda rows: tile_ref[rows, TILE - 128 :], False)
    even = (lax.axis_index("trow") & 1) == 0
    ends = [tile_ref[pl.ds(pl.multiple_of(jnp.where(even, a, TILE - RIM - a), RIM), RIM), :] for a in (TILE - RIM, 0)]
    if image:
        for ref, value, n in ((up_ref, ends[0], RIM), (down_ref, ends[1], RIM), (first_ref, first, 128), (last_ref, last, 128)):
            ref[pl.ds(0, n), :], ref[pl.ds(n, n), :] = split(value)
    else:
        out_ref[...] = tile_ref[...].astype(BF16)
        for ref, old, value, n in (
            (up_ref, up_in, ends[0], RIM), (down_ref, down_in, ends[1], RIM),
            (first_ref, first_in, first, 128), (last_ref, last_in, last, 128),
        ):
            ref[pl.ds(0, 2 * n), :] = old[...]
            ref[pl.ds(2 * n, n), :] = value.astype(BF16)


def gather(image, place, own, below, above, east, west, rims=()):
    middle = pl.BlockSpec((1, GROUP, 128), lambda i: (1, 0, 0))
    whole = lambda *shape: pl.BlockSpec(shape, lambda i: (0,) * len(shape))
    count = 2 if image else 3
    shapes = [(TILE, TILE), (count * RIM, TILE), (count * RIM, TILE), (count * 128, 128), (count * 128, 128)]
    return pl.pallas_call(
        functools.partial(gather_kernel, image),
        grid=(1,),
        in_specs=[SMEM(), whole(NP, PATCH, PATCH), middle, middle, whole(3, GROUP, 128), whole(3, GROUP, 128)]
        + [whole(*r.shape) for r in rims],
        out_specs=[whole(*s) for s in shapes],
        out_shape=[jax.ShapeDtypeStruct(s, F32 if image and i == 0 else BF16) for i, s in enumerate(shapes)],
        scratch_shapes=[pltpu.VMEM((8, 128), jnp.int32), pltpu.SMEM((8, 128), jnp.int32), pltpu.SemaphoreType.DMA]
        + ([] if image else [pltpu.VMEM((TILE, TILE), F32)]),
        compiler_params=pltpu.CompilerParams(vmem_limit_bytes=40 * MIB),
        name="gather_img" if image else "gather_var",
    )(place, own, below, above, east, west, *rims)


def choose(first, a, b):
    return jnp.where(first, a.astype(F32), b.astype(F32))


def turn_kernel(first_ref, last_ref, even_first, odd_first, even_last, odd_last, even_out, odd_out):
    here, count = lax.axis_index("trow"), lax.axis_size("trow")
    row_odd, col_odd = (here & 1) == 1, (lax.axis_index("tcol") & 1) == 1
    for out, flip in ((even_out, col_odd), (odd_out, jnp.logical_not(col_odd))):
        out[pl.ds(0, 384), :] = choose(flip, first_ref[...], last_ref[...]).astype(BF16)
        met = [choose(flip, a[...], b[...]) for a, b in ((even_first, even_last), (odd_first, odd_last))]
        out[pl.ds(384, 48), :] = jnp.where(here > 0, choose(row_odd, *met), 0.0).astype(BF16)
        out[pl.ds(432, 48), :] = jnp.where(here < count - 1, choose(row_odd, *met[::-1]), 0.0).astype(BF16)


def turn(first, last, even, odd):
    whole = pl.BlockSpec((384, 128), lambda i: (0, 0))
    near = pl.BlockSpec((48, 128), lambda i: (0, 0))
    far = pl.BlockSpec((48, 128), lambda i: (0, 7))
    return pl.pallas_call(
        turn_kernel,
        grid=(1,),
        in_specs=[whole, whole, near, near, far, far],
        out_specs=[pl.BlockSpec((480, 128), lambda i: (0, 0))] * 2,
        out_shape=[jax.ShapeDtypeStruct((480, 128), BF16)] * 2,
        compiler_params=pltpu.CompilerParams(vmem_limit_bytes=8 * MIB),
        name="turn",
    )(first, last, even, odd, even, odd)


def filter_kernel(
    psf, tile_ref, var_ref, row_even, row_odd, col_even, col_odd, out_ref,
    img_in, high, low, var, bands, flats, ends, v_high, v_low, v_var, out, in_sems, out_sems,
):
    row, rows_n = lax.axis_index("trow"), lax.axis_size("trow")
    col, cols_n = lax.axis_index("tcol"), lax.axis_size("tcol")
    copies = []
    for q in range(4):
        rows = pl.ds(256 * q, 256)
        inside = pl.ds(256 * q + RIM, 256)
        copies.append((
            pltpu.make_async_copy(tile_ref.at[rows, :], img_in.at[rows, :], in_sems.at[2 * q]),
            pltpu.make_async_copy(var_ref.at[rows, :], var.at[inside, pl.ds(0, TILE)], in_sems.at[2 * q + 1]),
        ))
    for pair in copies:
        for copy in pair:
            copy.start()

    peaks = []
    for axis in range(2):
        peak = psf[axis * PSF]
        for t in range(1, PSF):
            peak = jnp.maximum(peak, psf[axis * PSF + t])
        peaks.append(peak)
    scale = peaks[0] * peaks[1]

    def read(axis):
        return lambda t: psf[axis * PSF + t]

    over = [1.0 / jnp.full((16, 256), peak, F32) for peak in peaks]
    column = diagonals(read(1), PSF, 1, 1, 256) * over[1]
    flat = diagonals(read(0), PSF, REACH, -1, 256) * over[0]
    edge = corner(read(0), PSF, REACH) * over[0][0:1, :128]
    ends[...] = jnp.zeros(ends.shape, BF16)
    for squared in range(2):
        for m in range(STEP // 16):
            bands[squared, pl.ds(16 * m, 16), :] = toeplitz(column, m, 1, PSF).astype(BF16)
        for m in range(16):
            flats[squared, pl.ds(16 * m, 16), :] = toeplitz(flat, m, -REACH, REACH).astype(BF16)
        for part in range(2):
            span = pl.ds(128 * part, 128)
            ends[squared, pl.ds(128 * part, 16), span] = edge[16:].astype(BF16)
            ends[squared, pl.ds(128 * part + 112, 16), span] = edge[:16].astype(BF16)
        column, flat, edge = column * column, flat * flat, edge * edge

    lanes = lax.broadcasted_iota(jnp.int32, (128, 128), 1)
    side = pl.ds(TILE, 128)
    def met(along, at, start, rows):
        even, odd = (row_even, row_odd) if along is row else (col_even, col_odd)
        parts = even[start : start + rows, :], odd[start : start + rows, :]
        return choose((along & 1) == 1, *(parts[::-1] if at else parts))

    for i, ref in enumerate((high, low, var)):
        ref[pl.ds(0, RIM), pl.ds(0, TILE)] = jnp.where(row > 0, met(row, 0, RIM * i, RIM), 0.0).astype(BF16)
        ref[pl.ds(RIM + TILE, RIM), pl.ds(0, TILE)] = jnp.where(
            row < rows_n - 1, met(row, 1, RIM * i, RIM), 0.0
        ).astype(BF16)
        ref[pl.ds(2 * RIM + TILE, RIM * 2), :] = jnp.zeros((2 * RIM, TILE + 128), BF16)
        west, east = met(col, 0, 128 * i, 128), met(col, 1, 128 * i, 128)
        at_west, at_east = (lanes >= 128 - RIM) & (col > 0), (lanes < RIM) & (col < cols_n - 1)
        for g in range(8):
            near = pltpu.roll(east, 128 - RIM * g, 1) if g else east
            far = pltpu.roll(west, (112 - RIM * g) % 128, 1) if g != 7 else west
            ref[pl.ds(RIM + 128 * g, 128), side] = jnp.where(at_east, near, jnp.where(at_west, far, 0.0)).astype(BF16)
        for at, start in ((0, 384), (RIM + TILE, 432)):
            near, far = met(col, 1, start + RIM * i, RIM), met(col, 0, start + RIM * i, RIM)
            ref[pl.ds(at, RIM), side] = jnp.where(at_east[:RIM], near, jnp.where(at_west[:RIM], far, 0.0)).astype(BF16)

    spans = [(256 * c, 256) for c in range(4)] + [(TILE, 128)]
    ready = 0
    for t in range(5):
        count = min(STEP, TILE - STEP * t)
        while ready < 4 and 256 * ready < STEP * t + 240:
            for copy in copies[ready]:
                copy.wait()
            rows = pl.ds(RIM + 256 * ready, 256)
            high[rows, pl.ds(0, TILE)], low[rows, pl.ds(0, TILE)] = split(img_in[pl.ds(256 * ready, 256), :])
            ready += 1
        window = pl.ds(STEP * t, 256)
        target = pl.ds(STEP * t, count)
        for start, width in spans:
            span = pl.ds(start, width)
            value = dot(bands[0], high[window, span]) + dot(bands[0], low[window, span])
            v_high[target, span], v_low[target, span] = split(value[:count])
            v_var[target, span] = dot(bands[1], var[window, span])[:count].astype(BF16)

    lanes = lax.broadcasted_iota(jnp.int32, (256, 128), 1)
    near = lanes < 64
    for q in range(4):
        rows = pl.ds(256 * q, 256)
        results = []
        for squared, parts in ((0, (v_high, v_low)), (1, (v_var,))):
            def about(ref, w):
                if w == 0:
                    return ref[rows, side]
                return jnp.where(near, ref[rows, pl.ds(256 * w, 128)], ref[rows, pl.ds(256 * w - 128, 128)])

            fixes = []
            for w in (0, 2):
                both = sum(dot(jnp.concatenate([about(ref, w), about(ref, w + 1)], 1), ends[squared]) for ref in parts)
                fixes += [both[:, :128], both[:, 128:]]
            fixes.append(fixes[0])
            values = []
            for c in range(4):
                span = pl.ds(256 * c, 256)
                main = sum(dot(ref[rows, span], flats[squared]) for ref in parts)
                values.append(main[:, :128] + jnp.where(near, fixes[c], 0.0))
                values.append(main[:, 128:] + jnp.where(near, 0.0, fixes[c + 1]))
            results.append(values)
        for c in range(8):
            out[rows, pl.ds(128 * c, 128)] = scale * results[0][c] * lax.rsqrt(scale * scale * results[1][c] + 1.0)
        pltpu.make_async_copy(out.at[rows, :], out_ref.at[rows, :], out_sems.at[q]).start()
    for q in range(4):
        rows = pl.ds(256 * q, 256)
        pltpu.make_async_copy(out.at[rows, :], out_ref.at[rows, :], out_sems.at[q]).wait()


def detect(psf, tile, tile_var, *rims):
    vmem = pl.BlockSpec(memory_space=pltpu.VMEM)
    wide = TILE + 128
    return pl.pallas_call(
        filter_kernel,
        in_specs=[SMEM(), HBM, HBM, vmem, vmem, vmem, vmem],
        out_specs=HBM,
        out_shape=jax.ShapeDtypeStruct((TILE, TILE), F32),
        scratch_shapes=[pltpu.VMEM((TILE, TILE), F32)]
        + [pltpu.VMEM((1088, wide), BF16)] * 3
        + [pltpu.VMEM((2, STEP, 256), BF16), pltpu.VMEM((2, 256, 256), BF16), pltpu.VMEM((2, 256, 256), BF16)]
        + [pltpu.VMEM((TILE, wide), BF16)] * 3
        + [pltpu.VMEM((TILE, TILE), F32), pltpu.SemaphoreType.DMA((8,)), pltpu.SemaphoreType.DMA((4,))],
        compiler_params=pltpu.CompilerParams(vmem_limit_bytes=48 * MIB),
        name="filter",
    )(psf, tile, tile_var, *rims)


def shards(ccd_image, ccd_variance, basis_taps, coef_table, coef_pick, block_visit, visit_weight, patch_place, psf_taps):
    place = patch_place.reshape(NP)
    taps = basis_taps.astype(F32).reshape(-1)
    psf = psf_taps.reshape(-1)
    pin = lambda x: pltpu.with_memory_space_constraint(x, pltpu.HBM)
    small = (*map(pin, (coef_table, coef_pick, block_visit, visit_weight, patch_place)), taps)

    *parcels, own_image = match(False, *small, pin(ccd_image.reshape(2, BLOCK, BLOCK)))
    ahead = first_stage(parcels)
    taps_var, _ = lax.optimization_barrier((taps, own_image))
    *parcels_var, own_var = match(True, *small[:-1], taps_var, pin(ccd_variance.reshape(2, BLOCK, BLOCK)))
    behind = first_stage(parcels_var)
    tile, *rims = gather(True, place, own_image, *second_stage(parcels, *ahead))
    *behind, _ = lax.optimization_barrier((*behind, rims[0]))
    tile_var, up, down, first, last = gather(False, place, own_var, *second_stage(parcels_var, *behind), rims)
    rows = swap(up, "trow", False), swap(down, "trow", True)
    sides = turn(first, last, *rows)
    significance = detect(psf, tile, tile_var, *rows, swap(sides[0], "tcol", False), swap(sides[1], "tcol", True))
    return tile, significance


def solution(mesh):
    place = P("trow", "tcol", None)
    blocks = P("trow", "tcol", None, None, None)
    in_specs = (blocks, blocks, P(), P(), place, place, P(), place, P())
    out_specs = (P("trow", "tcol"), P("trow", "tcol"))
    return jax.shard_map(shards, mesh=mesh, in_specs=in_specs, out_specs=out_specs, check_vma=False)
```

time: 104 us -> 74 us (0.71)
  the two profiles are of different devices: /device:TPU:0 before, /device:TPU:7 now
where the time goes in v1:
time: 74 us; the launch traced here: 73.8 us
  Pallas kernels  32.4 us (44%)
  waiting for transfers between devices  23.6 us (32%)
  starting transfers between devices  15.7 us (21%)
  local copies, waits for them, and re-layouts  0.95 us (1%)
  between operations  0.91 us (1%)
    ppermute x12, waiting for transfers between devices, swap(): return lax.ppermute(value, ('trow', 'tcol'), pairs)  23.6 us
    pallas_call x2, Pallas kernels, match(): pl.pallas_call(functools.partial(match_kernel, squared), grid=(2,), in_sp...  17.1 us
    ppermute x12, starting transfers between devices, swap(): return lax.ppermute(value, ('trow', 'tcol'), pairs)  15.7 us
    pallas_call x1, Pallas kernels, detect(): pl.pallas_call(filter_kernel, in_specs=[SMEM(), HBM, HBM, vmem, vmem, vme...  9 us
    pallas_call x2, Pallas kernels, gather(): pl.pallas_call(functools.partial(gather_kernel, image), grid=(1,), in_spe...  6.2 us
  transfers between devices with their start and end apart: 12, of which 10 were waited for; matrix products, arithmetic and copies ran while one was open for 0% of the time, Pallas kernels for 17%

profile of v1, /device:TPU:7, one launch (start us, length us, event | category | flops | bytes accessed | tf_op | source)
XLA Modules:
  0.0 73.8 jit_solution(1767370316755708945)
XLA Ops:
  0.6 0.0 copy-start
  0.6 0.8 %reshape.28.taps = f32[252]{0:T(256)S(1)} reshape(bf16[6,2,21]{2,1,0:T(2,128)(2,1)} %param.11) | data formatting | bytes 1512 | tf_op jit(solution)/shard_map/reshape | solution.py:520
  1.4 8.5 %match_img.1 = (bf16[3,528,128]{2,1,0:T(8,128)(2,1)S(1)}, bf16[3,528,128]{2,1,0:T(8,128)(2,1)S(1)}, bf16[1,528,128]{2,1,0:T(8,128)(2,1)S(1)}, bf16[1,528,128]{2,1,0:T(8,128)(2,1)S(1)}, bf16[32,128,128]{2,1,0:T(8,128)(2,1)S(1)}) custom-call(f32[8,6]{1,0:T(8,128)} %table_in.3, s32[1,1,2]{2,1,0:T(1,128)} %pick_in.3, s32[1,1,2]{2,1,0:T(1,128)} %visit_in.3, ...), custom_call_target="tpu_custom_call" | custom-call | tf_op jit(solution)/shard_map/match_img/pallas_call | solution.py:215
  10.0 1.4 %collective-permute-start = (bf16[3,528,128]{2,1,0:T(8,128)(2,1)S(1)}, bf16[3,528,128]{2,1,0:T(8,128)(2,1)S(1)}, u32[]{:S(2)}, u32[]{:S(2)}) collective-permute-start(bf16[3,528,128]{2,1,0:T(8,128)(2,1)S(1)} %get-tuple-element.28), channel_id=1, source_target_pairs={{0,8},{1,9},{2,10},{3,11},{4,12},{5,13},{6,14},{7,15},{8,0},{9,1},... | collective-permute-start | bytes 1216520 | tf_op jit(solution)/shard_map/ppermute | solution.py:259
  11.3 2.2 %collective-permute-start.1 = (bf16[3,528,128]{2,1,0:T(8,128)(2,1)S(1)}, bf16[3,528,128]{2,1,0:T(8,128)(2,1)S(1)}, u32[]{:S(2)}, u32[]{:S(2)}) collective-permute-start(bf16[3,528,128]{2,1,0:T(8,128)(2,1)S(1)} %get-tuple-element.29), channel_id=1, source_target_pairs={{0,1},{1,0},{2,3},{3,2},{4,5},{5,4},{6,7},{7,6},{8,16},{9,17},{10,... | collective-permute-start | bytes 1216520 | tf_op jit(solution)/shard_map/ppermute | solution.py:259
  13.5 8.6 %match_var.1 = (bf16[3,528,128]{2,1,0:T(8,128)(2,1)S(1)}, bf16[3,528,128]{2,1,0:T(8,128)(2,1)S(1)}, bf16[1,528,128]{2,1,0:T(8,128)(2,1)S(1)}, bf16[1,528,128]{2,1,0:T(8,128)(2,1)S(1)}, bf16[32,128,128]{2,1,0:T(8,128)(2,1)S(1)}) custom-call(f32[8,6]{1,0:T(8,128)} %table_in.3, s32[1,1,2]{2,1,0:T(1,128)} %pick_in.3, s32[1,1,2]{2,1,0:T(1,128)} %visit_in.3, ...), custom_call_target="tpu_custom_call" | custom-call | tf_op jit(solution)/shard_map/match_var/pallas_call | solution.py:215
  22.1 0.0 collective-permute-done.below_ref
  22.1 1.3 %collective-permute-done.1.above_ref = bf16[3,528,128]{2,1,0:T(8,128)(2,1)S(1)} collective-permute-done((bf16[3,528,128]{2,1,0:T(8,128)(2,1)S(1)}, bf16[3,528,128]{2,1,0:T(8,128)(2,1)S(1)}, u32[]{:S(2)}, u32[]{:S(2)}) %collective-permute-start.1) | collective-permute-done | bytes 405536 | tf_op jit(solution)/shard_map/ppermute | solution.py:259
  23.5 1.9 %collective-permute-start.2 = (bf16[3,528,128]{2,1,0:T(8,128)(2,1)S(1)}, bf16[3,528,128]{2,1,0:T(8,128)(2,1)S(1)}, u32[]{:S(2)}, u32[]{:S(2)}) collective-permute-start(bf16[3,528,128]{2,1,0:T(8,128)(2,1)S(1)} %pad_maximum_fusion), channel_id=1, source_target_pairs={{0,1},{1,0},{2,3},{3,2},{4,5},{5,4},{6,7},{7,6},{8,9},{9,8},{10,11... | collective-permute-start | bytes 1216520 | tf_op jit(solution)/shard_map/ppermute | solution.py:259
  25.4 1.6 %collective-permute-start.3 = (bf16[3,528,128]{2,1,0:T(8,128)(2,1)S(1)}, bf16[3,528,128]{2,1,0:T(8,128)(2,1)S(1)}, u32[]{:S(2)}, u32[]{:S(2)}) collective-permute-start(bf16[3,528,128]{2,1,0:T(8,128)(2,1)S(1)} %pad_maximum_fusion.1), channel_id=1, source_target_pairs={{0,8},{1,2},{2,1},{3,4},{4,3},{5,6},{6,5},{7,15},{8,0},{9,10},{10,... | collective-permute-start | bytes 1216520 | tf_op jit(solution)/shard_map/ppermute | solution.py:259
  27.0 0.0 collective-permute-start.4
  27.0 2.2 %collective-permute-start.5 = (bf16[3,528,128]{2,1,0:T(8,128)(2,1)S(1)}, bf16[3,528,128]{2,1,0:T(8,128)(2,1)S(1)}, u32[]{:S(2)}, u32[]{:S(2)}) collective-permute-start(bf16[3,528,128]{2,1,0:T(8,128)(2,1)S(1)} %get-tuple-element.36), channel_id=1, source_target_pairs={{0,1},{1,0},{2,3},{3,2},{4,5},{5,4},{6,7},{7,6},{8,16},{9,17},{10,... | collective-permute-start | bytes 1216520 | tf_op jit(solution)/shard_map/ppermute | solution.py:259
  29.2 0.0 collective-permute-done.2.east_ref
  29.2 3.9 %collective-permute-done.3.west_ref = bf16[3,528,128]{2,1,0:T(8,128)(2,1)S(1)} collective-permute-done((bf16[3,528,128]{2,1,0:T(8,128)(2,1)S(1)}, bf16[3,528,128]{2,1,0:T(8,128)(2,1)S(1)}, u32[]{:S(2)}, u32[]{:S(2)}) %collective-permute-start.3) | collective-permute-done | bytes 405536 | tf_op jit(solution)/shard_map/ppermute | solution.py:259
  33.1 0.0 copy-done
  33.1 0.0 copy-start.1
  33.1 3.8 %gather_img.1 = (f32[1024,1024]{1,0:T(8,128)}, bf16[32,1024]{1,0:T(8,128)(2,1)S(1)}, bf16[32,1024]{1,0:T(8,128)(2,1)S(1)}, bf16[256,128]{1,0:T(8,128)(2,1)S(1)}, bf16[256,128]{1,0:T(8,128)(2,1)S(1)}) custom-call(s32[32]{0:T(128)S(1)} %bitcast.3, bf16[32,128,128]{2,1,0:T(8,128)(2,1)S(1)} %get-tuple-element.27.own_ref, ...), custom_call_target="tpu_custom_call" | custom-call | tf_op jit(solution)/shard_map/gather_img/pallas_call | solution.py:340
  37.0 1.4 %collective-permute-done.4.below_ref = bf16[3,528,128]{2,1,0:T(8,128)(2,1)S(1)} collective-permute-done((bf16[3,528,128]{2,1,0:T(8,128)(2,1)S(1)}, bf16[3,528,128]{2,1,0:T(8,128)(2,1)S(1)}, u32[]{:S(2)}, u32[]{:S(2)}) %collective-permute-start.4) | collective-permute-done | bytes 405536 | tf_op jit(solution)/shard_map/ppermute | solution.py:259
  38.4 1.1 %collective-permute-done.5.above_ref = bf16[3,528,128]{2,1,0:T(8,128)(2,1)S(1)} collective-permute-done((bf16[3,528,128]{2,1,0:T(8,128)(2,1)S(1)}, bf16[3,528,128]{2,1,0:T(8,128)(2,1)S(1)}, u32[]{:S(2)}, u32[]{:S(2)}) %collective-permute-start.5) | collective-permute-done | bytes 405536 | tf_op jit(solution)/shard_map/ppermute | solution.py:259
  39.6 0.1 fusion
  39.7 2.6 %collective-permute-start.6 = (bf16[3,528,128]{2,1,0:T(8,128)(2,1)S(1)}, bf16[3,528,128]{2,1,0:T(8,128)(2,1)S(1)}, u32[]{:S(2)}, u32[]{:S(2)}) collective-permute-start(bf16[3,528,128]{2,1,0:T(8,128)(2,1)S(1)} %pad_maximum_fusion.2), channel_id=1, source_target_pairs={{0,1},{1,0},{2,3},{3,2},{4,5},{5,4},{6,7},{7,6},{8,9},{9,8},{10,11... | collective-permute-start | bytes 1216520 | tf_op jit(solution)/shard_map/ppermute | solution.py:259
  42.4 0.1 collective-permute-start.7
  42.5 1.2 %collective-permute-done.6.east_ref = bf16[3,528,128]{2,1,0:T(8,128)(2,1)S(1)} collective-permute-done((bf16[3,528,128]{2,1,0:T(8,128)(2,1)S(1)}, bf16[3,528,128]{2,1,0:T(8,128)(2,1)S(1)}, u32[]{:S(2)}, u32[]{:S(2)}) %collective-permute-start.6) | collective-permute-done | bytes 405536 | tf_op jit(solution)/shard_map/ppermute | solution.py:259
  43.7 6.3 %collective-permute-done.7.west_ref = bf16[3,528,128]{2,1,0:T(8,128)(2,1)S(1)} collective-permute-done((bf16[3,528,128]{2,1,0:T(8,128)(2,1)S(1)}, bf16[3,528,128]{2,1,0:T(8,128)(2,1)S(1)}, u32[]{:S(2)}, u32[]{:S(2)}) %collective-permute-start.7) | collective-permute-done | bytes 405536 | tf_op jit(solution)/shard_map/ppermute | solution.py:259
  50.0 2.4 %gather_var.1 = (bf16[1024,1024]{1,0:T(8,128)(2,1)S(1)}, bf16[48,1024]{1,0:T(8,128)(2,1)S(1)}, bf16[48,1024]{1,0:T(8,128)(2,1)S(1)}, bf16[384,128]{1,0:T(8,128)(2,1)S(1)}, bf16[384,128]{1,0:T(8,128)(2,1)S(1)}) custom-call(s32[32]{0:T(128)S(1)} %bitcast.4, bf16[32,128,128]{2,1,0:T(8,128)(2,1)S(1)} %get-tuple-element.34.own_ref, ...), custom_call_target="tpu_custom_call" | custom-call | tf_op jit(solution)/shard_map/gather_var/pallas_call | solution.py:340
  52.3 0.1 collective-permute-start.8
  52.4 2.3 %collective-permute-start.9 = (bf16[48,1024]{1,0:T(8,128)(2,1)S(1)}, bf16[48,1024]{1,0:T(8,128)(2,1)S(1)}, u32[]{:S(2)}, u32[]{:S(2)}) collective-permute-start(bf16[48,1024]{1,0:T(8,128)(2,1)S(1)} %get-tuple-element.47), channel_id=1, source_target_pairs={{0,1},{1,0},{2,3},{3,2},{4,5},{5,4},{6,7},{7,6},{8,16},{9,17},{10,... | collective-permute-start | bytes 294920 | tf_op jit(solution)/shard_map/ppermute | solution.py:259
  54.7 1.6 %collective-permute-done.8.even_first.even_last.row_even = bf16[48,1024]{1,0:T(8,128)(2,1)S(1)} collective-permute-done((bf16[48,1024]{1,0:T(8,128)(2,1)S(1)}, bf16[48,1024]{1,0:T(8,128)(2,1)S(1)}, u32[]{:S(2)}, u32[]{:S(2)}) %collective-permute-start.8) | collective-permute-done | bytes 98336 | tf_op jit(solution)/shard_map/ppermute | solution.py:259
  56.3 2.2 %collective-permute-done.9.odd_first.odd_last.row_odd = bf16[48,1024]{1,0:T(8,128)(2,1)S(1)} collective-permute-done((bf16[48,1024]{1,0:T(8,128)(2,1)S(1)}, bf16[48,1024]{1,0:T(8,128)(2,1)S(1)}, u32[]{:S(2)}, u32[]{:S(2)}) %collective-permute-start.9) | collective-permute-done | bytes 98336 | tf_op jit(solution)/shard_map/ppermute | solution.py:259
  58.5 0.1 turn.1
  58.6 1.4 %collective-permute-start.10 = (bf16[480,128]{1,0:T(8,128)(2,1)S(1)}, bf16[480,128]{1,0:T(8,128)(2,1)S(1)}, u32[]{:S(2)}, u32[]{:S(2)}) collective-permute-start(bf16[480,128]{1,0:T(8,128)(2,1)S(1)} %get-tuple-element.50), channel_id=1, source_target_pairs={{0,1},{1,0},{2,3},{3,2},{4,5},{5,4},{6,7},{7,6},{8,9},{9,8},{10,11... | collective-permute-start | bytes 368648 | tf_op jit(solution)/shard_map/ppermute | solution.py:259
  60.0 0.0 collective-permute-start.11
  60.0 0.0 copy-done.1
  60.0 0.1 reshape.25.psf
  60.1 0.9 %collective-permute-done.10.col_even = bf16[480,128]{1,0:T(8,128)(2,1)S(1)} collective-permute-done((bf16[480,128]{1,0:T(8,128)(2,1)S(1)}, bf16[480,128]{1,0:T(8,128)(2,1)S(1)}, u32[]{:S(2)}, u32[]{:S(2)}) %collective-permute-start.10) | collective-permute-done | bytes 122912 | tf_op jit(solution)/shard_map/ppermute | solution.py:259
  61.0 3.6 %collective-permute-done.11.col_odd = bf16[480,128]{1,0:T(8,128)(2,1)S(1)} collective-permute-done((bf16[480,128]{1,0:T(8,128)(2,1)S(1)}, bf16[480,128]{1,0:T(8,128)(2,1)S(1)}, u32[]{:S(2)}, u32[]{:S(2)}) %collective-permute-start.11) | collective-permute-done | bytes 122912 | tf_op jit(solution)/shard_map/ppermute | solution.py:259
  64.6 9.0 %filter.1 = f32[1024,1024]{1,0:T(8,128)} custom-call(f32[62]{0:T(128)S(1)} %reshape.25.psf, f32[1024,1024]{1,0:T(8,128)} %get-tuple-element.25.tile_ref, bf16[1024,1024]{1,0:T(8,128)(2,1)S(1)} %get-tuple-element.45.var_ref, bf16[48,1024]{1,0:T(8,128)(2,1)S(1)} %collective-permute-done.8.even_first.even_last.row_even, ...), custom_call_target="tpu_custom_call" | custom-call | tf_op jit(solution)/shard_map/filter/pallas_call | solution.py:503
  (6 shorter events, 0.2 us)
Async XLA Ops:
  0.6 32.5 %copy-start = (s32[1,1,32]{2,1,0:T(1,128)S(1)}, s32[1,1,32]{2,1,0:T(1,128)}, u32[]{:S(2)}) copy-start(s32[1,1,32]{2,1,0:T(1,128)} %place_in.3) | copy-start | bytes 388
  10.0 12.1 %collective-permute-start = (bf16[3,528,128]{2,1,0:T(8,128)(2,1)S(1)}, bf16[3,528,128]{2,1,0:T(8,128)(2,1)S(1)}, u32[]{:S(2)}, u32[]{:S(2)}) collective-permute-start(bf16[3,528,128]{2,1,0:T(8,128)(2,1)S(1)} %get-tuple-element.28), channel_id=1, source_target_pairs={{0,8},{1,9},{2,10},{3,11},{4,12},{5,13},{6,14},{7,15},{8,0},{9,1},... | collective-permute-start | bytes 1216520 | tf_op jit(solution)/shard_map/ppermute | solution.py:259
  11.3 12.1 %collective-permute-start.1 = (bf16[3,528,128]{2,1,0:T(8,128)(2,1)S(1)}, bf16[3,528,128]{2,1,0:T(8,128)(2,1)S(1)}, u32[]{:S(2)}, u32[]{:S(2)}) collective-permute-start(bf16[3,528,128]{2,1,0:T(8,128)(2,1)S(1)} %get-tuple-element.29), channel_id=1, source_target_pairs={{0,1},{1,0},{2,3},{3,2},{4,5},{5,4},{6,7},{7,6},{8,16},{9,17},{10,... | collective-permute-start | bytes 1216520 | tf_op jit(solution)/shard_map/ppermute | solution.py:259
  23.5 5.8 %collective-permute-start.2 = (bf16[3,528,128]{2,1,0:T(8,128)(2,1)S(1)}, bf16[3,528,128]{2,1,0:T(8,128)(2,1)S(1)}, u32[]{:S(2)}, u32[]{:S(2)}) collective-permute-start(bf16[3,528,128]{2,1,0:T(8,128)(2,1)S(1)} %pad_maximum_fusion), channel_id=1, source_target_pairs={{0,1},{1,0},{2,3},{3,2},{4,5},{5,4},{6,7},{7,6},{8,9},{9,8},{10,11... | collective-permute-start | bytes 1216520 | tf_op jit(solution)/shard_map/ppermute | solution.py:259
  25.4 7.7 %collective-permute-start.3 = (bf16[3,528,128]{2,1,0:T(8,128)(2,1)S(1)}, bf16[3,528,128]{2,1,0:T(8,128)(2,1)S(1)}, u32[]{:S(2)}, u32[]{:S(2)}) collective-permute-start(bf16[3,528,128]{2,1,0:T(8,128)(2,1)S(1)} %pad_maximum_fusion.1), channel_id=1, source_target_pairs={{0,8},{1,2},{2,1},{3,4},{4,3},{5,6},{6,5},{7,15},{8,0},{9,10},{10,... | collective-permute-start | bytes 1216520 | tf_op jit(solution)/shard_map/ppermute | solution.py:259
  27.0 11.4 %collective-permute-start.4 = (bf16[3,528,128]{2,1,0:T(8,128)(2,1)S(1)}, bf16[3,528,128]{2,1,0:T(8,128)(2,1)S(1)}, u32[]{:S(2)}, u32[]{:S(2)}) collective-permute-start(bf16[3,528,128]{2,1,0:T(8,128)(2,1)S(1)} %get-tuple-element.35), channel_id=1, source_target_pairs={{0,8},{1,9},{2,10},{3,11},{4,12},{5,13},{6,14},{7,15},{8,0},{9,1},... | collective-permute-start | bytes 1216520 | tf_op jit(solution)/shard_map/ppermute | solution.py:259
  27.0 12.5 %collective-permute-start.5 = (bf16[3,528,128]{2,1,0:T(8,128)(2,1)S(1)}, bf16[3,528,128]{2,1,0:T(8,128)(2,1)S(1)}, u32[]{:S(2)}, u32[]{:S(2)}) collective-permute-start(bf16[3,528,128]{2,1,0:T(8,128)(2,1)S(1)} %get-tuple-element.36), channel_id=1, source_target_pairs={{0,1},{1,0},{2,3},{3,2},{4,5},{5,4},{6,7},{7,6},{8,16},{9,17},{10,... | collective-permute-start | bytes 1216520 | tf_op jit(solution)/shard_map/ppermute | solution.py:259
  33.1 26.9 %copy-start.1 = (f32[2,31]{1,0:T(2,128)S(1)}, f32[2,31]{1,0:T(2,128)}, u32[]{:S(2)}) copy-start(f32[2,31]{1,0:T(2,128)} %param.17) | copy-start | bytes 748
  39.7 4.0 %collective-permute-start.6 = (bf16[3,528,128]{2,1,0:T(8,128)(2,1)S(1)}, bf16[3,528,128]{2,1,0:T(8,128)(2,1)S(1)}, u32[]{:S(2)}, u32[]{:S(2)}) collective-permute-start(bf16[3,528,128]{2,1,0:T(8,128)(2,1)S(1)} %pad_maximum_fusion.2), channel_id=1, source_target_pairs={{0,1},{1,0},{2,3},{3,2},{4,5},{5,4},{6,7},{7,6},{8,9},{9,8},{10,11... | collective-permute-start | bytes 1216520 | tf_op jit(solution)/shard_map/ppermute | solution.py:259
  42.4 7.6 %collective-permute-start.7 = (bf16[3,528,128]{2,1,0:T(8,128)(2,1)S(1)}, bf16[3,528,128]{2,1,0:T(8,128)(2,1)S(1)}, u32[]{:S(2)}, u32[]{:S(2)}) collective-permute-start(bf16[3,528,128]{2,1,0:T(8,128)(2,1)S(1)} %pad_maximum_fusion.3), channel_id=1, source_target_pairs={{0,8},{1,2},{2,1},{3,4},{4,3},{5,6},{6,5},{7,15},{8,0},{9,10},{10,... | collective-permute-start | bytes 1216520 | tf_op jit(solution)/shard_map/ppermute | solution.py:259
  52.3 4.0 %collective-permute-start.8 = (bf16[48,1024]{1,0:T(8,128)(2,1)S(1)}, bf16[48,1024]{1,0:T(8,128)(2,1)S(1)}, u32[]{:S(2)}, u32[]{:S(2)}) collective-permute-start(bf16[48,1024]{1,0:T(8,128)(2,1)S(1)} %get-tuple-element.46), channel_id=1, source_target_pairs={{0,8},{1,9},{2,10},{3,11},{4,12},{5,13},{6,14},{7,15},{8,0},{9,1},... | collective-permute-start | bytes 294920 | tf_op jit(solution)/shard_map/ppermute | solution.py:259
  52.4 6.1 %collective-permute-start.9 = (bf16[48,1024]{1,0:T(8,128)(2,1)S(1)}, bf16[48,1024]{1,0:T(8,128)(2,1)S(1)}, u32[]{:S(2)}, u32[]{:S(2)}) collective-permute-start(bf16[48,1024]{1,0:T(8,128)(2,1)S(1)} %get-tuple-element.47), channel_id=1, source_target_pairs={{0,1},{1,0},{2,3},{3,2},{4,5},{5,4},{6,7},{7,6},{8,16},{9,17},{10,... | collective-permute-start | bytes 294920 | tf_op jit(solution)/shard_map/ppermute | solution.py:259
  58.6 2.4 %collective-permute-start.10 = (bf16[480,128]{1,0:T(8,128)(2,1)S(1)}, bf16[480,128]{1,0:T(8,128)(2,1)S(1)}, u32[]{:S(2)}, u32[]{:S(2)}) collective-permute-start(bf16[480,128]{1,0:T(8,128)(2,1)S(1)} %get-tuple-element.50), channel_id=1, source_target_pairs={{0,1},{1,0},{2,3},{3,2},{4,5},{5,4},{6,7},{7,6},{8,9},{9,8},{10,11... | collective-permute-start | bytes 368648 | tf_op jit(solution)/shard_map/ppermute | solution.py:259
  60.0 4.6 %collective-permute-start.11 = (bf16[480,128]{1,0:T(8,128)(2,1)S(1)}, bf16[480,128]{1,0:T(8,128)(2,1)S(1)}, u32[]{:S(2)}, u32[]{:S(2)}) collective-permute-start(bf16[480,128]{1,0:T(8,128)(2,1)S(1)} %get-tuple-element.51), channel_id=1, source_target_pairs={{0,8},{1,2},{2,1},{3,4},{4,3},{5,6},{6,5},{7,15},{8,0},{9,10},{10,... | collective-permute-start | bytes 368648 | tf_op jit(solution)/shard_map/ppermute | solution.py:259

commit v2 on v1

--- a/solution.py
+++ b/solution.py
@@ -24,6 +24,7 @@
 MIB = 1 << 20
 
 HBM = pl.BlockSpec(memory_space=pltpu.HBM)
+VMEM = pl.BlockSpec(memory_space=pltpu.VMEM)
 SMEM = functools.partial(pl.BlockSpec, memory_space=pltpu.SMEM)
 
 
@@ -79,13 +80,14 @@
 def match_kernel(
     squared, table_in, pick_in, visit_in, weight_in, place_in, taps, x_in,
     up_ref, down_ref, left_ref, right_ref, own_ref,
-    across, edges, down, rows_ref, total, heading, rank, slots,
+    across, edges, down, rows_ref, total, leaving, count, slot, slots,
     table, pick, visit, weight, place, x_ref, sems, x_sem,
 ):
-    block = pl.program_id(0)
     small = [(table_in, table), (pick_in, pick), (visit_in, visit), (weight_in, weight), (place_in, place)]
     small = [pltpu.make_async_copy(a, b, sems.at[i]) for i, (a, b) in enumerate(small)]
     pixels = [pltpu.make_async_copy(x_in.at[b], x_ref.at[b], x_sem.at[b]) for b in range(2)]
+    for copy in small + pixels:
+        copy.start()
 
     def read(k, axis):
         return lambda t: taps[(2 * k + axis) * TAPS + t]
@@ -93,143 +95,106 @@
     def kept(x):
         return (x * x if squared else x).astype(BF16)
 
-    @pl.when(block == 0)
-    def _():
-        for copy in small + pixels:
-            copy.start()
-        edges[...] = jnp.zeros(edges.shape, BF16)
-        for k in range(NBASIS):
-            base = diagonals(read(k, 0), TAPS, RADIUS, -1, 256)
-            for m in range(16):
-                across[k, pl.ds(16 * m, 16), :] = kept(toeplitz(base, m, -RADIUS, RADIUS))
-            edges[k // 2, pl.ds(112, 32), pl.ds(k % 2 * 128, 128)] = kept(corner(read(k, 0), TAPS, RADIUS))
-            base = diagonals(read(k, 1), TAPS, -26, 1, 256)
-            for m in range(18):
-                down[k, pl.ds(16 * m, 16), :] = kept(toeplitz(base, m, -26, -6))
-        for copy in small:
-            copy.wait()
-        for g in range(8):
-            for s in range(CAP):
-                slots[g * CAP + s] = -1
-
-        def order(n, counts):
-            entry = place[0, 0, n]
-            d = via(entry >> 6)
-            heading[n] = d
-            r = jnp.int32(0)
-            for g in range(9):
-                r = jnp.where(d == g, counts[g], r)
-            rank[n] = r
-
-            @pl.when(d != 4)
-            def _():
-                slots[jnp.where(d > 4, d - 1, d) * CAP + r] = entry & 63
-
-            return tuple(counts[g] + (d == g).astype(jnp.int32) for g in range(9))
-
-        lax.fori_loop(0, NP, order, (jnp.int32(0),) * 9)
-        _, lanes = iotas((16, 128))
-        for g in range(8):
-            line = jnp.full((16, 128), -1.0, F32)
-            for s in range(CAP):
-                line = jnp.where(lanes == s, slots[g * CAP + s].astype(F32), line)
-            line = line.astype(BF16)
-            last = pl.ds(CAP * PATCH, 16)
-            if g < 3:
-                up_ref[g, last, :] = line
-            elif g == 3:
-                left_ref[0, last, :] = line
-            elif g == 4:
-                right_ref[0, last, :] = line
-            else:
-                down_ref[g - 5, last, :] = line
-        pixels[0].wait()
-
-    @pl.when(block == 1)
-    def _():
-        pixels[1].wait()
-
-    lanes = lax.broadcasted_iota(jnp.int32, (BLOCK, 128), 1)
-    for pair in range(NBASIS // 2):
-        fix = dot(x_ref[block, :, 128:384], edges[pair])
-        for half in range(2):
-            k = 2 * pair + half
-            part = fix[:, 128 * half : 128 * half + 128]
-            first = dot(x_ref[block, :, :256], across[k])
-            rows_ref[k, :, 0:128] = first[:, :128].astype(BF16)
-            rows_ref[k, :, 128:256] = (first[:, 128:] + jnp.where(lanes >= 64, part, 0.0)).astype(BF16)
-            second = dot(x_ref[block, :, 256:], across[k])
-            rows_ref[k, :, 256:384] = (second[:, :128] + jnp.where(lanes < 64, part, 0.0)).astype(BF16)
-            rows_ref[k, :, 384:512] = second[:, 128:].astype(BF16)
-    scale = weight[visit[0, 0, block]].astype(F32)
-    if squared:
-        scale = scale * scale
-    for side in range(2):
-        span = pl.ds(256 * side, 256)
-        for k in range(NBASIS):
-            coef = table[pick[0, 0, block], k]
-            if squared:
-                coef = coef * coef
-            top = dot(down[k, 16:288, :], rows_ref[k, 0:256, span])
-            low = dot(down[k, 0:272, :], rows_ref[k, 256:512, span])
-            middle = top[240:] + low[:32]
-            if k == 0:
-                total[0:240, span] = coef * top[:240]
-                total[240:272, span] = coef * middle
-                total[272:512, span] = coef * low[32:]
-            else:
-                total[0:240, span] += coef * top[:240]
-                total[240:272, span] += coef * middle
-                total[272:512, span] += coef * low[32:]
-    for i in range(4):
-        for j in range(4):
-            square = scale * total[128 * i : 128 * i + 128, 128 * j : 128 * j + 128]
-            own_ref[block * 16 + 4 * i + j] = square.astype(BF16)
-
-    def leave(i, _):
-        n = block * 16 + i
-        d = heading[n]
-        where = pl.ds(pl.multiple_of(rank[n] * PATCH, PATCH), PATCH)
-
-        @pl.when(d < 3)
-        def _():
-            up_ref[d, where, :] = own_ref[n]
-
-        @pl.when(d == 3)
-        def _():
-            left_ref[0, where, :] = own_ref[n]
-
-        @pl.when(d == 5)
-        def _():
-            right_ref[0, where, :] = own_ref[n]
-
-        @pl.when(d > 5)
-        def _():
-            down_ref[d - 6, where, :] = own_ref[n]
-
-    lax.fori_loop(0, 16, leave, None)
+    def build(k):
+        base = diagonals(read(k, 0), TAPS, RADIUS, -1, 256)
+        for m in range(16):
+            across[k, pl.ds(16 * m, 16), :] = kept(toeplitz(base, m, -RADIUS, RADIUS))
+        edges[k // 2, pl.ds(112, 32), pl.ds(k % 2 * 128, 128)] = kept(corner(read(k, 0), TAPS, RADIUS))
+        base = diagonals(read(k, 1), TAPS, -26, 1, 256)
+        for m in range(18):
+            down[k, pl.ds(16 * m, 16), :] = kept(toeplitz(base, m, -26, -6))
+
+    for g in range(9):
+        count[g] = 0
+    for s in range(8 * CAP):
+        slots[s] = -1
+    edges[...] = jnp.zeros(edges.shape, BF16)
+    for k in range(NBASIS // 2):
+        build(k)
+    for copy in small:
+        copy.wait()
+    for n in range(NP):
+        entry = place[0, 0, n]
+        d = via(entry >> 6)
+        r = count[d]
+        count[d] = r + 1
+        s = jnp.where(d == 4, 8 * CAP, jnp.where(d > 4, d - 1, d) * CAP + r)
+        slot[n] = s
+        slots[s] = entry & 63
+    for k in range(NBASIS // 2, NBASIS):
+        build(k)
+    _, lanes = iotas((16, 128))
+    parcels = [(up_ref, 0), (up_ref, 1), (up_ref, 2), (left_ref, 0), (right_ref, 0), (down_ref, 0), (down_ref, 1), (down_ref, 2)]
+    for g, (ref, at) in enumerate(parcels):
+        line = jnp.full((16, 128), -1.0, F32)
+        for s in range(CAP):
+            line = jnp.where(lanes == s, slots[g * CAP + s].astype(F32), line)
+        ref[at, pl.ds(CAP * PATCH, 16), :] = line.astype(BF16)
+
+    def one(block, _):
+        pltpu.make_async_copy(x_in.at[block], x_ref.at[block], x_sem.at[block]).wait()
+        lanes = lax.broadcasted_iota(jnp.int32, (BLOCK, 128), 1)
+        for pair in range(NBASIS // 2):
+            fix = dot(x_ref[block, :, 128:384], edges[pair])
+            for half in range(2):
+                k = 2 * pair + half
+                part = fix[:, 128 * half : 128 * half + 128]
+                first = dot(x_ref[block, :, :256], across[k])
+                rows_ref[k, :, 0:128] = first[:, :128].astype(BF16)
+                rows_ref[k, :, 128:256] = (first[:, 128:] + jnp.where(lanes >= 64, part, 0.0)).astype(BF16)
+                second = dot(x_ref[block, :, 256:], across[k])
+                rows_ref[k, :, 256:384] = (second[:, :128] + jnp.where(lanes < 64, part, 0.0)).astype(BF16)
+                rows_ref[k, :, 384:512] = second[:, 128:].astype(BF16)
+        scale = weight[visit[0, 0, block]].astype(F32)
+        if squared:
+            scale = scale * scale
+        for side in range(2):
+            span = pl.ds(256 * side, 256)
+            for k in range(NBASIS):
+                coef = table[pick[0, 0, block], k]
+                if squared:
+                    coef = coef * coef
+                top = dot(down[k, 16:288, :], rows_ref[k, 0:256, span])
+                low = dot(down[k, 0:272, :], rows_ref[k, 256:512, span])
+                middle = top[240:] + low[:32]
+                if k == 0:
+                    total[0:240, span] = coef * top[:240]
+                    total[240:272, span] = coef * middle
+                    total[272:512, span] = coef * low[32:]
+                else:
+                    total[0:240, span] += coef * top[:240]
+                    total[240:272, span] += coef * middle
+                    total[272:512, span] += coef * low[32:]
+        for i in range(4):
+            for j in range(4):
+                n = block * 16 + 4 * i + j
+                square = (scale * total[128 * i : 128 * i + 128, 128 * j : 128 * j + 128]).astype(BF16)
+                own_ref[n] = square
+                leaving[slot[n]] = square
+
+    lax.fori_loop(0, 2, one, None)
+    for g, (ref, at) in enumerate(parcels):
+        for s in range(CAP):
+            ref[at, pl.ds(s * PATCH, PATCH), :] = leaving[g * CAP + s]
 
 
 def match(squared, table, pick, visit, weight, place, taps, blocks):
-    whole = lambda *shape: pl.BlockSpec(shape, lambda b: (0,) * len(shape))
+    shapes = ((3, GROUP, 128), (3, GROUP, 128), (1, GROUP, 128), (1, GROUP, 128), (NP, PATCH, PATCH))
     return pl.pallas_call(
         functools.partial(match_kernel, squared),
-        grid=(2,),
         in_specs=[HBM] * 5 + [SMEM(), HBM],
-        out_specs=[whole(3, GROUP, 128), whole(3, GROUP, 128), whole(1, GROUP, 128), whole(1, GROUP, 128), whole(NP, PATCH, PATCH)],
-        out_shape=[
-            jax.ShapeDtypeStruct(s, BF16)
-            for s in ((3, GROUP, 128), (3, GROUP, 128), (1, GROUP, 128), (1, GROUP, 128), (NP, PATCH, PATCH))
-        ],
+        out_specs=[VMEM] * 5,
+        out_shape=[jax.ShapeDtypeStruct(s, BF16) for s in shapes],
         scratch_shapes=[
             pltpu.VMEM((NBASIS, 256, 256), BF16),
             pltpu.VMEM((NBASIS // 2, 256, 256), BF16),
             pltpu.VMEM((NBASIS, 288, 256), BF16),
             pltpu.VMEM((NBASIS, BLOCK, BLOCK), BF16),
             pltpu.VMEM((BLOCK, BLOCK), F32),
+            pltpu.VMEM((8 * CAP + 1, PATCH, PATCH), BF16),
+            pltpu.SMEM((9,), jnp.int32),
             pltpu.SMEM((NP,), jnp.int32),
-            pltpu.SMEM((NP,), jnp.int32),
-            pltpu.SMEM((8 * CAP,), jnp.int32),
+            pltpu.SMEM((8 * CAP + 1,), jnp.int32),
             pltpu.SMEM(table.shape, F32),
             pltpu.SMEM(pick.shape, jnp.int32),
             pltpu.SMEM(visit.shape, jnp.int32),
@@ -239,7 +204,7 @@
             pltpu.SemaphoreType.DMA((5,)),
             pltpu.SemaphoreType.DMA((2,)),
         ],
-        compiler_params=pltpu.CompilerParams(vmem_limit_bytes=40 * MIB),
+        compiler_params=pltpu.CompilerParams(vmem_limit_bytes=24 * MIB),
         name="match_var" if squared else "match_img",
     )(table, pick, visit, weight, place, taps, blocks)
 
@@ -281,31 +246,50 @@
     return out
 
 
-def gather_kernel(image, place, own_ref, below_ref, above_ref, east_ref, west_ref, *rest):
+def add(tile_ref, spot, square):
+    rows = pl.ds(pl.multiple_of((spot >> 3) * PATCH, PATCH), PATCH)
+    cols = pl.ds(pl.multiple_of((spot & 7) * PATCH, PATCH), PATCH)
+    tile_ref[rows, cols] += square.astype(F32)
+
+
+def add_own(place, own_ref, tile_ref):
+    tile_ref[...] = jnp.zeros(tile_ref.shape, F32)
+
+    def own(n, _):
+        entry = place[n]
+
+        @pl.when((entry >> 6) == 4)
+        def _():
+            add(tile_ref, entry & 63, own_ref[n])
+
+    lax.fori_loop(0, NP, own, None)
+
+
+def own_sum(name, place, own):
+    return pl.pallas_call(
+        add_own,
+        in_specs=[SMEM(), VMEM],
+        out_specs=VMEM,
+        out_shape=jax.ShapeDtypeStruct((TILE, TILE), F32),
+        compiler_params=pltpu.CompilerParams(vmem_limit_bytes=12 * MIB),
+        name=name,
+    )(place, own)
+
+
+def gather_kernel(image, place, start_ref, below_ref, above_ref, east_ref, west_ref, *rest):
     if image:
         tile_ref, up_ref, down_ref, first_ref, last_ref, lines, spots, sem = rest
     else:
         up_in, down_in, first_in, last_in, out_ref, up_ref, down_ref, first_ref, last_ref, lines, spots, sem, tile_ref = rest
-    groups = [(below_ref, 0), (above_ref, 0)] + [(east_ref, g) for g in range(3)] + [(west_ref, g) for g in range(3)]
+    groups = [(below_ref, 1), (above_ref, 1)] + [(east_ref, g) for g in range(3)] + [(west_ref, g) for g in range(3)]
     for g, (ref, at) in enumerate(groups):
         lines[pl.ds(g, 1), :] = ref[at, CAP * PATCH :, :].astype(F32)[0:1].astype(jnp.int32)
     copy = pltpu.make_async_copy(lines, spots, sem)
     copy.start()
-    tile_ref[...] = jnp.zeros(tile_ref.shape, F32)
-
-    def add(spot, square):
-        rows = pl.ds(pl.multiple_of((spot >> 3) * PATCH, PATCH), PATCH)
-        cols = pl.ds(pl.multiple_of((spot & 7) * PATCH, PATCH), PATCH)
-        tile_ref[rows, cols] += square.astype(F32)
-
-    def own(n, _):
-        entry = place[n]
-
-        @pl.when((entry >> 6) == 4)
-        def _():
-            add(entry & 63, own_ref[n])
-
-    lax.fori_loop(0, NP, own, None)
+    if image:
+        add_own(place, start_ref, tile_ref)
+    else:
+        tile_ref[...] = start_ref[...]
     copy.wait()
     for g, (ref, at) in enumerate(groups):
         for s in range(CAP):
@@ -313,7 +297,7 @@
 
             @pl.when(spot >= 0)
             def _():
-                add(spot, ref[at, s * PATCH : (s + 1) * PATCH, :])
+                add(tile_ref, spot, ref[at, s * PATCH : (s + 1) * PATCH, :])
 
     first = pack(lambda rows: tile_ref[rows, :128], True)
     last = pack(lambda rows: tile_ref[rows, TILE - 128 :], False)
@@ -332,23 +316,19 @@
             ref[pl.ds(2 * n, n), :] = value.astype(BF16)
 
 
-def gather(image, place, own, below, above, east, west, rims=()):
-    middle = pl.BlockSpec((1, GROUP, 128), lambda i: (1, 0, 0))
-    whole = lambda *shape: pl.BlockSpec(shape, lambda i: (0,) * len(shape))
+def gather(image, place, start, below, above, east, west, rims=()):
     count = 2 if image else 3
     shapes = [(TILE, TILE), (count * RIM, TILE), (count * RIM, TILE), (count * 128, 128), (count * 128, 128)]
     return pl.pallas_call(
         functools.partial(gather_kernel, image),
-        grid=(1,),
-        in_specs=[SMEM(), whole(NP, PATCH, PATCH), middle, middle, whole(3, GROUP, 128), whole(3, GROUP, 128)]
-        + [whole(*r.shape) for r in rims],
-        out_specs=[whole(*s) for s in shapes],
+        in_specs=[SMEM()] + [VMEM] * (5 + len(rims)),
+        out_specs=[VMEM] * len(shapes),
         out_shape=[jax.ShapeDtypeStruct(s, F32 if image and i == 0 else BF16) for i, s in enumerate(shapes)],
         scratch_shapes=[pltpu.VMEM((8, 128), jnp.int32), pltpu.SMEM((8, 128), jnp.int32), pltpu.SemaphoreType.DMA]
         + ([] if image else [pltpu.VMEM((TILE, TILE), F32)]),
-        compiler_params=pltpu.CompilerParams(vmem_limit_bytes=40 * MIB),
+        compiler_params=pltpu.CompilerParams(vmem_limit_bytes=20 * MIB),
         name="gather_img" if image else "gather_var",
-    )(place, own, below, above, east, west, *rims)
+    )(place, start, below, above, east, west, *rims)
 
 
 def choose(first, a, b):
@@ -510,7 +490,7 @@
         + [pltpu.VMEM((2, STEP, 256), BF16), pltpu.VMEM((2, 256, 256), BF16), pltpu.VMEM((2, 256, 256), BF16)]
         + [pltpu.VMEM((TILE, wide), BF16)] * 3
         + [pltpu.VMEM((TILE, TILE), F32), pltpu.SemaphoreType.DMA((8,)), pltpu.SemaphoreType.DMA((4,))],
-        compiler_params=pltpu.CompilerParams(vmem_limit_bytes=48 * MIB),
+        compiler_params=pltpu.CompilerParams(vmem_limit_bytes=32 * MIB),
         name="filter",
     )(psf, tile, tile_var, *rims)
 
@@ -524,15 +504,19 @@
 
     *parcels, own_image = match(False, *small, pin(ccd_image.reshape(2, BLOCK, BLOCK)))
     ahead = first_stage(parcels)
-    taps_var, _ = lax.optimization_barrier((taps, own_image))
+    taps_var, own_image = lax.optimization_barrier((taps, own_image))
     *parcels_var, own_var = match(True, *small[:-1], taps_var, pin(ccd_variance.reshape(2, BLOCK, BLOCK)))
     behind = first_stage(parcels_var)
-    tile, *rims = gather(True, place, own_image, *second_stage(parcels, *ahead))
-    *behind, _ = lax.optimization_barrier((*behind, rims[0]))
-    tile_var, up, down, first, last = gather(False, place, own_var, *second_stage(parcels_var, *behind), rims)
+    base_var = own_sum("own_var", place, own_var)
+    *ahead, base_var = lax.optimization_barrier((*ahead, base_var))
+    arrived = second_stage(parcels, *ahead)
+    *behind, east, west = lax.optimization_barrier((*behind, *arrived[2:]))
+    arrived_var = second_stage(parcels_var, *behind)
+    tile, *rims = gather(True, place, own_image, *arrived[:2], east, west)
+    tile_var, up, down, first, last = gather(False, place, base_var, *arrived_var, rims)
     rows = swap(up, "trow", False), swap(down, "trow", True)
     sides = turn(first, last, *rows)
-    significance = detect(psf, tile, tile_var, *rows, swap(sides[0], "tcol", False), swap(sides[1], "tcol", True))
+    significance = detect(psf, pin(tile), tile_var, *rows, swap(sides[0], "tcol", False), swap(sides[1], "tcol", True))
     return tile, significance
 
 

time: 74 us -> 65.8 us (0.89)
  waiting for transfers between devices: 23.6 us -> 18.3 us
  Pallas kernels: 32.4 us -> 29.2 us
    ppermute x12, waiting for transfers between devices: 23.6 us -> 18.3 us  [swap(): return lax.ppermute(value, ('trow', 'tcol'), pairs)]
    pallas_call x4 -> x5, Pallas kernels: 23.3 us -> 20.1 us  [the longest x2 12.8 us: match(): pl.pallas_call(functools.partial(match_kernel, squared), in_specs=[HBM] *...]
  transfers between devices with their start and end apart: 12 -> 12, of which waited for: 10 -> 8; matrix products, arithmetic and copies ran while one was open for 0% -> 0% of each run, Pallas kernels for 17% -> 18%
where the time goes in v2:
time: 65.8 us; the launch traced here: 65.6 us
  Pallas kernels  29.2 us (44%)
  waiting for transfers between devices  18.3 us (28%)
  starting transfers between devices  15.4 us (23%)
  local copies, waits for them, and re-layouts  1.61 us (2%)
  between operations  0.93 us (1%)
    ppermute x12, waiting for transfers between devices, swap(): return lax.ppermute(value, ('trow', 'tcol'), pairs)  18.3 us
    ppermute x12, starting transfers between devices, swap(): return lax.ppermute(value, ('trow', 'tcol'), pairs)  15.4 us
    pallas_call x2, Pallas kernels, match(): pl.pallas_call(functools.partial(match_kernel, squared), in_specs=[HBM] *...  12.8 us
    pallas_call x1, Pallas kernels, detect(): pl.pallas_call(filter_kernel, in_specs=[SMEM(), HBM, HBM, vmem, vmem, vme...  9 us
    pallas_call x2, Pallas kernels, gather(): pl.pallas_call(functools.partial(gather_kernel, image), in_specs=[SMEM()]...  5.94 us
    pallas_call x1, Pallas kernels, own_sum(): pl.pallas_call(add_own, in_specs=[SMEM(), VMEM], out_specs=VMEM, out_shap...  1.34 us
  transfers between devices with their start and end apart: 12, of which 8 were waited for; matrix products, arithmetic and copies ran while one was open for 0% of the time, Pallas kernels for 18%

profile of v2, /device:TPU:7, one launch (start us, length us, event | category | flops | bytes accessed | tf_op | source)
XLA Modules:
  0.0 65.6 jit_solution(9955181956485819312)
XLA Ops:
  0.6 0.8 %reshape.28.taps = f32[252]{0:T(256)S(1)} reshape(bf16[6,2,21]{2,1,0:T(2,128)(2,1)} %param.11) | data formatting | bytes 1512 | tf_op jit(solution)/shard_map/reshape | solution.py:500
  1.4 6.4 %match_img.1 = (bf16[3,528,128]{2,1,0:T(8,128)(2,1)S(1)}, bf16[3,528,128]{2,1,0:T(8,128)(2,1)S(1)}, bf16[1,528,128]{2,1,0:T(8,128)(2,1)S(1)}, bf16[1,528,128]{2,1,0:T(8,128)(2,1)S(1)}, bf16[32,128,128]{2,1,0:T(8,128)(2,1)S(1)}) custom-call(f32[8,6]{1,0:T(8,128)} %table_in.3, s32[1,1,2]{2,1,0:T(1,128)} %pick_in.3, s32[1,1,2]{2,1,0:T(1,128)} %visit_in.3, ...), custom_call_target="tpu_custom_call" | custom-call | tf_op jit(solution)/shard_map/match_img/pallas_call | solution.py:183
  7.8 1.4 %collective-permute-start = (bf16[3,528,128]{2,1,0:T(8,128)(2,1)S(1)}, bf16[3,528,128]{2,1,0:T(8,128)(2,1)S(1)}, u32[]{:S(2)}, u32[]{:S(2)}) collective-permute-start(bf16[3,528,128]{2,1,0:T(8,128)(2,1)S(1)} %get-tuple-element.35), channel_id=1, source_target_pairs={{0,8},{1,9},{2,10},{3,11},{4,12},{5,13},{6,14},{7,15},{8,0},{9,1},... | collective-permute-start | bytes 1216520 | tf_op jit(solution)/shard_map/ppermute | solution.py:224
  9.2 2.2 %collective-permute-start.1 = (bf16[3,528,128]{2,1,0:T(8,128)(2,1)S(1)}, bf16[3,528,128]{2,1,0:T(8,128)(2,1)S(1)}, u32[]{:S(2)}, u32[]{:S(2)}) collective-permute-start(bf16[3,528,128]{2,1,0:T(8,128)(2,1)S(1)} %get-tuple-element.36), channel_id=1, source_target_pairs={{0,1},{1,0},{2,3},{3,2},{4,5},{5,4},{6,7},{7,6},{8,16},{9,17},{10,... | collective-permute-start | bytes 1216520 | tf_op jit(solution)/shard_map/ppermute | solution.py:224
  11.3 6.4 %match_var.1 = (bf16[3,528,128]{2,1,0:T(8,128)(2,1)S(1)}, bf16[3,528,128]{2,1,0:T(8,128)(2,1)S(1)}, bf16[1,528,128]{2,1,0:T(8,128)(2,1)S(1)}, bf16[1,528,128]{2,1,0:T(8,128)(2,1)S(1)}, bf16[32,128,128]{2,1,0:T(8,128)(2,1)S(1)}) custom-call(f32[8,6]{1,0:T(8,128)} %table_in.3, s32[1,1,2]{2,1,0:T(1,128)} %pick_in.3, s32[1,1,2]{2,1,0:T(1,128)} %visit_in.3, ...), custom_call_target="tpu_custom_call" | custom-call | tf_op jit(solution)/shard_map/match_var/pallas_call | solution.py:183
  17.8 0.2 collective-permute-start.2
  18.0 1.4 %collective-permute-start.3 = (bf16[3,528,128]{2,1,0:T(8,128)(2,1)S(1)}, bf16[3,528,128]{2,1,0:T(8,128)(2,1)S(1)}, u32[]{:S(2)}, u32[]{:S(2)}) collective-permute-start(bf16[3,528,128]{2,1,0:T(8,128)(2,1)S(1)} %get-tuple-element.42), channel_id=1, source_target_pairs={{0,1},{1,0},{2,3},{3,2},{4,5},{5,4},{6,7},{7,6},{8,16},{9,17},{10,... | collective-permute-start | bytes 1216520 | tf_op jit(solution)/shard_map/ppermute | solution.py:224
  19.4 0.0 copy-start
  19.4 0.7 copy-done
  20.0 1.3 %own_var.1.start_ref = f32[1024,1024]{1,0:T(8,128)S(1)} custom-call(s32[32]{0:T(128)S(1)} %bitcast.3, bf16[32,128,128]{2,1,0:T(8,128)(2,1)S(1)} %get-tuple-element.38.own_ref), custom_call_target="tpu_custom_call" | custom-call | tf_op jit(solution)/shard_map/own_var/pallas_call | solution.py:269
  21.4 0.0 copy-start.1
  21.4 0.0 collective-permute-done.below_ref
  21.4 0.0 collective-permute-done.1.above_ref
  21.4 0.1 fusion.2
  21.5 1.7 %collective-permute-start.4 = (bf16[3,528,128]{2,1,0:T(8,128)(2,1)S(1)}, bf16[3,528,128]{2,1,0:T(8,128)(2,1)S(1)}, u32[]{:S(2)}, u32[]{:S(2)}) collective-permute-start(bf16[3,528,128]{2,1,0:T(8,128)(2,1)S(1)} %pad_maximum_fusion), channel_id=1, source_target_pairs={{0,1},{1,0},{2,3},{3,2},{4,5},{5,4},{6,7},{7,6},{8,9},{9,8},{10,11... | collective-permute-start | bytes 1216520 | tf_op jit(solution)/shard_map/ppermute | solution.py:224
  23.3 1.6 %collective-permute-start.5 = (bf16[3,528,128]{2,1,0:T(8,128)(2,1)S(1)}, bf16[3,528,128]{2,1,0:T(8,128)(2,1)S(1)}, u32[]{:S(2)}, u32[]{:S(2)}) collective-permute-start(bf16[3,528,128]{2,1,0:T(8,128)(2,1)S(1)} %pad_maximum_fusion.1), channel_id=1, source_target_pairs={{0,8},{1,2},{2,1},{3,4},{4,3},{5,6},{6,5},{7,15},{8,0},{9,10},{10,... | collective-permute-start | bytes 1216520 | tf_op jit(solution)/shard_map/ppermute | solution.py:224
  24.9 2.6 %collective-permute-done.2.below_ref = bf16[3,528,128]{2,1,0:T(8,128)(2,1)S(1)} collective-permute-done((bf16[3,528,128]{2,1,0:T(8,128)(2,1)S(1)}, bf16[3,528,128]{2,1,0:T(8,128)(2,1)S(1)}, u32[]{:S(2)}, u32[]{:S(2)}) %collective-permute-start.2) | collective-permute-done | bytes 405536 | tf_op jit(solution)/shard_map/ppermute | solution.py:224
  27.5 2.0 %collective-permute-done.3.above_ref = bf16[3,528,128]{2,1,0:T(8,128)(2,1)S(1)} collective-permute-done((bf16[3,528,128]{2,1,0:T(8,128)(2,1)S(1)}, bf16[3,528,128]{2,1,0:T(8,128)(2,1)S(1)}, u32[]{:S(2)}, u32[]{:S(2)}) %collective-permute-start.3) | collective-permute-done | bytes 405536 | tf_op jit(solution)/shard_map/ppermute | solution.py:224
  29.5 0.0 collective-permute-done.4.east_ref
  29.5 1.5 %collective-permute-done.5.west_ref = bf16[3,528,128]{2,1,0:T(8,128)(2,1)S(1)} collective-permute-done((bf16[3,528,128]{2,1,0:T(8,128)(2,1)S(1)}, bf16[3,528,128]{2,1,0:T(8,128)(2,1)S(1)}, u32[]{:S(2)}, u32[]{:S(2)}) %collective-permute-start.5) | collective-permute-done | bytes 405536 | tf_op jit(solution)/shard_map/ppermute | solution.py:224
  31.1 3.1 %collective-permute-start.6 = (bf16[3,528,128]{2,1,0:T(8,128)(2,1)S(1)}, bf16[3,528,128]{2,1,0:T(8,128)(2,1)S(1)}, u32[]{:S(2)}, u32[]{:S(2)}) collective-permute-start(bf16[3,528,128]{2,1,0:T(8,128)(2,1)S(1)} %pad_maximum_fusion.2), channel_id=1, source_target_pairs={{0,1},{1,0},{2,3},{3,2},{4,5},{5,4},{6,7},{7,6},{8,9},{9,8},{10,11... | collective-permute-start | bytes 1216520 | tf_op jit(solution)/shard_map/ppermute | solution.py:224
  34.2 0.0 copy-start.2
  34.2 0.1 collective-permute-start.7
  34.3 3.8 %gather_img.1 = (f32[1024,1024]{1,0:T(8,128)}, bf16[32,1024]{1,0:T(8,128)(2,1)S(1)}, bf16[32,1024]{1,0:T(8,128)(2,1)S(1)}, bf16[256,128]{1,0:T(8,128)(2,1)S(1)}, bf16[256,128]{1,0:T(8,128)(2,1)S(1)}) custom-call(s32[32]{0:T(128)S(1)} %bitcast.4, bf16[32,128,128]{2,1,0:T(8,128)(2,1)S(1)} %get-tuple-element.34.start_ref, ...), custom_call_target="tpu_custom_call" | custom-call | tf_op jit(solution)/shard_map/gather_img/pallas_call | solution.py:322
  38.2 0.0 collective-permute-done.6.east_ref
  38.2 3.7 %collective-permute-done.7.west_ref = bf16[3,528,128]{2,1,0:T(8,128)(2,1)S(1)} collective-permute-done((bf16[3,528,128]{2,1,0:T(8,128)(2,1)S(1)}, bf16[3,528,128]{2,1,0:T(8,128)(2,1)S(1)}, u32[]{:S(2)}, u32[]{:S(2)}) %collective-permute-start.7) | collective-permute-done | bytes 405536 | tf_op jit(solution)/shard_map/ppermute | solution.py:224
  41.9 0.0 copy-done.1
  41.9 2.1 %gather_var.1 = (bf16[1024,1024]{1,0:T(8,128)(2,1)S(1)}, bf16[48,1024]{1,0:T(8,128)(2,1)S(1)}, bf16[48,1024]{1,0:T(8,128)(2,1)S(1)}, bf16[384,128]{1,0:T(8,128)(2,1)S(1)}, bf16[384,128]{1,0:T(8,128)(2,1)S(1)}) custom-call(s32[32]{0:T(128)S(1)} %bitcast.5, f32[1024,1024]{1,0:T(8,128)S(1)} %own_var.1.start_ref, ...), custom_call_target="tpu_custom_call" | custom-call | tf_op jit(solution)/shard_map/gather_var/pallas_call | solution.py:322
  44.0 0.2 collective-permute-start.8
  44.2 2.0 %collective-permute-start.9 = (bf16[48,1024]{1,0:T(8,128)(2,1)S(1)}, bf16[48,1024]{1,0:T(8,128)(2,1)S(1)}, u32[]{:S(2)}, u32[]{:S(2)}) collective-permute-start(bf16[48,1024]{1,0:T(8,128)(2,1)S(1)} %get-tuple-element.59), channel_id=1, source_target_pairs={{0,1},{1,0},{2,3},{3,2},{4,5},{5,4},{6,7},{7,6},{8,16},{9,17},{10,... | collective-permute-start | bytes 294920 | tf_op jit(solution)/shard_map/ppermute | solution.py:224
  46.3 1.8 %collective-permute-done.8.even_first.even_last.row_even = bf16[48,1024]{1,0:T(8,128)(2,1)S(1)} collective-permute-done((bf16[48,1024]{1,0:T(8,128)(2,1)S(1)}, bf16[48,1024]{1,0:T(8,128)(2,1)S(1)}, u32[]{:S(2)}, u32[]{:S(2)}) %collective-permute-start.8) | collective-permute-done | bytes 98336 | tf_op jit(solution)/shard_map/ppermute | solution.py:224
  48.1 2.2 %collective-permute-done.9.odd_first.odd_last.row_odd = bf16[48,1024]{1,0:T(8,128)(2,1)S(1)} collective-permute-done((bf16[48,1024]{1,0:T(8,128)(2,1)S(1)}, bf16[48,1024]{1,0:T(8,128)(2,1)S(1)}, u32[]{:S(2)}, u32[]{:S(2)}) %collective-permute-start.9) | collective-permute-done | bytes 98336 | tf_op jit(solution)/shard_map/ppermute | solution.py:224
  50.3 0.1 turn.1
  50.4 1.5 %collective-permute-start.10 = (bf16[480,128]{1,0:T(8,128)(2,1)S(1)}, bf16[480,128]{1,0:T(8,128)(2,1)S(1)}, u32[]{:S(2)}, u32[]{:S(2)}) collective-permute-start(bf16[480,128]{1,0:T(8,128)(2,1)S(1)} %get-tuple-element.62), channel_id=1, source_target_pairs={{0,1},{1,0},{2,3},{3,2},{4,5},{5,4},{6,7},{7,6},{8,9},{9,8},{10,11... | collective-permute-start | bytes 368648 | tf_op jit(solution)/shard_map/ppermute | solution.py:224
  51.8 0.0 collective-permute-start.11
  51.8 0.0 copy-done.2
  51.8 0.1 reshape.26.psf
  51.9 0.9 %collective-permute-done.10.col_even = bf16[480,128]{1,0:T(8,128)(2,1)S(1)} collective-permute-done((bf16[480,128]{1,0:T(8,128)(2,1)S(1)}, bf16[480,128]{1,0:T(8,128)(2,1)S(1)}, u32[]{:S(2)}, u32[]{:S(2)}) %collective-permute-start.10) | collective-permute-done | bytes 122912 | tf_op jit(solution)/shard_map/ppermute | solution.py:224
  52.8 3.6 %collective-permute-done.11.col_odd = bf16[480,128]{1,0:T(8,128)(2,1)S(1)} collective-permute-done((bf16[480,128]{1,0:T(8,128)(2,1)S(1)}, bf16[480,128]{1,0:T(8,128)(2,1)S(1)}, u32[]{:S(2)}, u32[]{:S(2)}) %collective-permute-start.11) | collective-permute-done | bytes 122912 | tf_op jit(solution)/shard_map/ppermute | solution.py:224
  56.4 9.0 %filter.1 = f32[1024,1024]{1,0:T(8,128)} custom-call(f32[62]{0:T(128)S(1)} %reshape.26.psf, f32[1024,1024]{1,0:T(8,128)} %get-tuple-element.31.tile_ref, bf16[1024,1024]{1,0:T(8,128)(2,1)S(1)} %get-tuple-element.57.var_ref, bf16[48,1024]{1,0:T(8,128)(2,1)S(1)} %collective-permute-done.8.even_first.even_last.row_even, ...), custom_call_target="tpu_custom_call" | custom-call | tf_op jit(solution)/shard_map/filter/pallas_call | solution.py:483
  (6 shorter events, 0.2 us)
Async XLA Ops:
  7.8 13.6 %collective-permute-start = (bf16[3,528,128]{2,1,0:T(8,128)(2,1)S(1)}, bf16[3,528,128]{2,1,0:T(8,128)(2,1)S(1)}, u32[]{:S(2)}, u32[]{:S(2)}) collective-permute-start(bf16[3,528,128]{2,1,0:T(8,128)(2,1)S(1)} %get-tuple-element.35), channel_id=1, source_target_pairs={{0,8},{1,9},{2,10},{3,11},{4,12},{5,13},{6,14},{7,15},{8,0},{9,1},... | collective-permute-start | bytes 1216520 | tf_op jit(solution)/shard_map/ppermute | solution.py:224
  9.2 12.2 %collective-permute-start.1 = (bf16[3,528,128]{2,1,0:T(8,128)(2,1)S(1)}, bf16[3,528,128]{2,1,0:T(8,128)(2,1)S(1)}, u32[]{:S(2)}, u32[]{:S(2)}) collective-permute-start(bf16[3,528,128]{2,1,0:T(8,128)(2,1)S(1)} %get-tuple-element.36), channel_id=1, source_target_pairs={{0,1},{1,0},{2,3},{3,2},{4,5},{5,4},{6,7},{7,6},{8,16},{9,17},{10,... | collective-permute-start | bytes 1216520 | tf_op jit(solution)/shard_map/ppermute | solution.py:224
  17.8 9.7 %collective-permute-start.2 = (bf16[3,528,128]{2,1,0:T(8,128)(2,1)S(1)}, bf16[3,528,128]{2,1,0:T(8,128)(2,1)S(1)}, u32[]{:S(2)}, u32[]{:S(2)}) collective-permute-start(bf16[3,528,128]{2,1,0:T(8,128)(2,1)S(1)} %get-tuple-element.41), channel_id=1, source_target_pairs={{0,8},{1,9},{2,10},{3,11},{4,12},{5,13},{6,14},{7,15},{8,0},{9,1},... | collective-permute-start | bytes 1216520 | tf_op jit(solution)/shard_map/ppermute | solution.py:224
  18.0 11.5 %collective-permute-start.3 = (bf16[3,528,128]{2,1,0:T(8,128)(2,1)S(1)}, bf16[3,528,128]{2,1,0:T(8,128)(2,1)S(1)}, u32[]{:S(2)}, u32[]{:S(2)}) collective-permute-start(bf16[3,528,128]{2,1,0:T(8,128)(2,1)S(1)} %get-tuple-element.42), channel_id=1, source_target_pairs={{0,1},{1,0},{2,3},{3,2},{4,5},{5,4},{6,7},{7,6},{8,16},{9,17},{10,... | collective-permute-start | bytes 1216520 | tf_op jit(solution)/shard_map/ppermute | solution.py:224
  19.4 0.7 copy-start
  21.4 20.5 %copy-start.1 = (s32[1,1,32]{2,1,0:T(1,128)S(1)}, s32[1,1,32]{2,1,0:T(1,128)}, u32[]{:S(2)}) copy-start(s32[1,1,32]{2,1,0:T(1,128)} %place_in.3) | copy-start | bytes 388
  21.5 8.0 %collective-permute-start.4 = (bf16[3,528,128]{2,1,0:T(8,128)(2,1)S(1)}, bf16[3,528,128]{2,1,0:T(8,128)(2,1)S(1)}, u32[]{:S(2)}, u32[]{:S(2)}) collective-permute-start(bf16[3,528,128]{2,1,0:T(8,128)(2,1)S(1)} %pad_maximum_fusion), channel_id=1, source_target_pairs={{0,1},{1,0},{2,3},{3,2},{4,5},{5,4},{6,7},{7,6},{8,9},{9,8},{10,11... | collective-permute-start | bytes 1216520 | tf_op jit(solution)/shard_map/ppermute | solution.py:224
  23.3 7.7 %collective-permute-start.5 = (bf16[3,528,128]{2,1,0:T(8,128)(2,1)S(1)}, bf16[3,528,128]{2,1,0:T(8,128)(2,1)S(1)}, u32[]{:S(2)}, u32[]{:S(2)}) collective-permute-start(bf16[3,528,128]{2,1,0:T(8,128)(2,1)S(1)} %pad_maximum_fusion.1), channel_id=1, source_target_pairs={{0,8},{1,2},{2,1},{3,4},{4,3},{5,6},{6,5},{7,15},{8,0},{9,10},{10,... | collective-permute-start | bytes 1216520 | tf_op jit(solution)/shard_map/ppermute | solution.py:224
  31.1 7.1 %collective-permute-start.6 = (bf16[3,528,128]{2,1,0:T(8,128)(2,1)S(1)}, bf16[3,528,128]{2,1,0:T(8,128)(2,1)S(1)}, u32[]{:S(2)}, u32[]{:S(2)}) collective-permute-start(bf16[3,528,128]{2,1,0:T(8,128)(2,1)S(1)} %pad_maximum_fusion.2), channel_id=1, source_target_pairs={{0,1},{1,0},{2,3},{3,2},{4,5},{5,4},{6,7},{7,6},{8,9},{9,8},{10,11... | collective-permute-start | bytes 1216520 | tf_op jit(solution)/shard_map/ppermute | solution.py:224
  34.2 17.6 %copy-start.2 = (f32[2,31]{1,0:T(2,128)S(1)}, f32[2,31]{1,0:T(2,128)}, u32[]{:S(2)}) copy-start(f32[2,31]{1,0:T(2,128)} %param.17) | copy-start | bytes 748
  34.2 7.6 %collective-permute-start.7 = (bf16[3,528,128]{2,1,0:T(8,128)(2,1)S(1)}, bf16[3,528,128]{2,1,0:T(8,128)(2,1)S(1)}, u32[]{:S(2)}, u32[]{:S(2)}) collective-permute-start(bf16[3,528,128]{2,1,0:T(8,128)(2,1)S(1)} %pad_maximum_fusion.3), channel_id=1, source_target_pairs={{0,8},{1,2},{2,1},{3,4},{4,3},{5,6},{6,5},{7,15},{8,0},{9,10},{10,... | collective-permute-start | bytes 1216520 | tf_op jit(solution)/shard_map/ppermute | solution.py:224
  44.0 4.1 %collective-permute-start.8 = (bf16[48,1024]{1,0:T(8,128)(2,1)S(1)}, bf16[48,1024]{1,0:T(8,128)(2,1)S(1)}, u32[]{:S(2)}, u32[]{:S(2)}) collective-permute-start(bf16[48,1024]{1,0:T(8,128)(2,1)S(1)} %get-tuple-element.58), channel_id=1, source_target_pairs={{0,8},{1,9},{2,10},{3,11},{4,12},{5,13},{6,14},{7,15},{8,0},{9,1},... | collective-permute-start | bytes 294920 | tf_op jit(solution)/shard_map/ppermute | solution.py:224
  44.2 6.1 %collective-permute-start.9 = (bf16[48,1024]{1,0:T(8,128)(2,1)S(1)}, bf16[48,1024]{1,0:T(8,128)(2,1)S(1)}, u32[]{:S(2)}, u32[]{:S(2)}) collective-permute-start(bf16[48,1024]{1,0:T(8,128)(2,1)S(1)} %get-tuple-element.59), channel_id=1, source_target_pairs={{0,1},{1,0},{2,3},{3,2},{4,5},{5,4},{6,7},{7,6},{8,16},{9,17},{10,... | collective-permute-start | bytes 294920 | tf_op jit(solution)/shard_map/ppermute | solution.py:224
  50.4 2.4 %collective-permute-start.10 = (bf16[480,128]{1,0:T(8,128)(2,1)S(1)}, bf16[480,128]{1,0:T(8,128)(2,1)S(1)}, u32[]{:S(2)}, u32[]{:S(2)}) collective-permute-start(bf16[480,128]{1,0:T(8,128)(2,1)S(1)} %get-tuple-element.62), channel_id=1, source_target_pairs={{0,1},{1,0},{2,3},{3,2},{4,5},{5,4},{6,7},{7,6},{8,9},{9,8},{10,11... | collective-permute-start | bytes 368648 | tf_op jit(solution)/shard_map/ppermute | solution.py:224
  51.8 4.6 %collective-permute-start.11 = (bf16[480,128]{1,0:T(8,128)(2,1)S(1)}, bf16[480,128]{1,0:T(8,128)(2,1)S(1)}, u32[]{:S(2)}, u32[]{:S(2)}) collective-permute-start(bf16[480,128]{1,0:T(8,128)(2,1)S(1)} %get-tuple-element.63), channel_id=1, source_target_pairs={{0,8},{1,2},{2,1},{3,4},{4,3},{5,6},{6,5},{7,15},{8,0},{9,10},{10,... | collective-permute-start | bytes 368648 | tf_op jit(solution)/shard_map/ppermute | solution.py:224

commit v3 on v2

--- a/solution.py
+++ b/solution.py
@@ -360,112 +360,166 @@
     )(first, last, even, odd, even, odd)
 
 
-def filter_kernel(
-    psf, tile_ref, var_ref, row_even, row_odd, col_even, col_odd, out_ref,
-    img_in, high, low, var, bands, flats, ends, v_high, v_low, v_var, out, in_sems, out_sems,
-):
-    row, rows_n = lax.axis_index("trow"), lax.axis_size("trow")
-    col, cols_n = lax.axis_index("tcol"), lax.axis_size("tcol")
+def tap(psf, axis):
+    return lambda t: psf[axis * PSF + t]
+
+
+def largest(psf, axis):
+    peak = psf[axis * PSF]
+    for t in range(1, PSF):
+        peak = jnp.maximum(peak, psf[axis * PSF + t])
+    return peak
+
+
+def column_bands(psf, bands):
+    column = diagonals(tap(psf, 1), PSF, 1, 1, 256) / jnp.full((16, 256), largest(psf, 1), F32)
+    for squared in range(2):
+        for m in range(STEP // 16):
+            bands[squared, pl.ds(16 * m, 16), :] = toeplitz(column, m, 1, PSF).astype(BF16)
+        column = column * column
+
+
+def column_kernel(psf, tile_ref, var_ref, v_high, v_low, v_var, img_in, high, low, var, bands, in_sems):
     copies = []
     for q in range(4):
         rows = pl.ds(256 * q, 256)
         inside = pl.ds(256 * q + RIM, 256)
         copies.append((
             pltpu.make_async_copy(tile_ref.at[rows, :], img_in.at[rows, :], in_sems.at[2 * q]),
-            pltpu.make_async_copy(var_ref.at[rows, :], var.at[inside, pl.ds(0, TILE)], in_sems.at[2 * q + 1]),
+            pltpu.make_async_copy(var_ref.at[rows, :], var.at[inside, :], in_sems.at[2 * q + 1]),
         ))
     for pair in copies:
         for copy in pair:
             copy.start()
-
-    peaks = []
-    for axis in range(2):
-        peak = psf[axis * PSF]
-        for t in range(1, PSF):
-            peak = jnp.maximum(peak, psf[axis * PSF + t])
-        peaks.append(peak)
-    scale = peaks[0] * peaks[1]
-
-    def read(axis):
-        return lambda t: psf[axis * PSF + t]
-
-    over = [1.0 / jnp.full((16, 256), peak, F32) for peak in peaks]
-    column = diagonals(read(1), PSF, 1, 1, 256) * over[1]
-    flat = diagonals(read(0), PSF, REACH, -1, 256) * over[0]
-    edge = corner(read(0), PSF, REACH) * over[0][0:1, :128]
+    column_bands(psf, bands)
+    for ref in (high, low, var):
+        ref[pl.ds(0, RIM), :] = jnp.zeros((RIM, TILE), BF16)
+        ref[pl.ds(RIM + TILE, 3 * RIM), :] = jnp.zeros((3 * RIM, TILE), BF16)
+    ready = 0
+    for t in range(5):
+        count = min(STEP, TILE - STEP * t)
+        while ready < 4 and 256 * ready < STEP * t + 240:
+            for copy in copies[ready]:
+                copy.wait()
+            high[pl.ds(RIM + 256 * ready, 256), :], low[pl.ds(RIM + 256 * ready, 256), :] = split(img_in[pl.ds(256 * ready, 256), :])
+            ready += 1
+        window = pl.ds(STEP * t, 256)
+        target = pl.ds(STEP * t, count)
+        for c in range(4):
+            span = pl.ds(256 * c, 256)
+            value = dot(bands[0], high[window, span]) + dot(bands[0], low[window, span])
+            v_high[target, span], v_low[target, span] = split(value[:count])
+            v_var[target, span] = dot(bands[1], var[window, span])[:count].astype(BF16)
+
+
+def column_pass(psf, tile, tile_var):
+    return pl.pallas_call(
+        column_kernel,
+        in_specs=[SMEM(), HBM, HBM],
+        out_specs=[VMEM] * 3,
+        out_shape=[jax.ShapeDtypeStruct((TILE, TILE), BF16)] * 3,
+        scratch_shapes=[pltpu.VMEM((TILE, TILE), F32)]
+        + [pltpu.VMEM((1088, TILE), BF16)] * 3
+        + [pltpu.VMEM((2, STEP, 256), BF16), pltpu.SemaphoreType.DMA((8,))],
+        compiler_params=pltpu.CompilerParams(vmem_limit_bytes=22 * MIB),
+        name="column",
+    )(psf, tile, tile_var)
+
+
+def filter_kernel(
+    psf, tile_ref, var_ref, v_high, v_low, v_var, row_even, row_odd, col_even, col_odd, out_ref,
+    img_in, var_in, frame, sides, bands, flats, ends, v_rim, v_side, out, in_sems, out_sems,
+):
+    row, rows_n = lax.axis_index("trow"), lax.axis_size("trow")
+    col, cols_n = lax.axis_index("tcol"), lax.axis_size("tcol")
+    copies = []
+    for i, start in enumerate((0, TILE - 2 * RIM)):
+        rows = pl.ds(start, 2 * RIM)
+        copies.append(pltpu.make_async_copy(tile_ref.at[rows, :], img_in.at[i], in_sems.at[2 * i]))
+        copies.append(pltpu.make_async_copy(var_ref.at[rows, :], var_in.at[i], in_sems.at[2 * i + 1]))
+    for copy in copies:
+        copy.start()
+    scale = largest(psf, 0) * largest(psf, 1)
+    column_bands(psf, bands)
+    over = 1.0 / jnp.full((16, 256), largest(psf, 0), F32)
+    flat = diagonals(tap(psf, 0), PSF, REACH, -1, 256) * over
+    edge = corner(tap(psf, 0), PSF, REACH) * over[0:1, :128]
     ends[...] = jnp.zeros(ends.shape, BF16)
     for squared in range(2):
-        for m in range(STEP // 16):
-            bands[squared, pl.ds(16 * m, 16), :] = toeplitz(column, m, 1, PSF).astype(BF16)
         for m in range(16):
             flats[squared, pl.ds(16 * m, 16), :] = toeplitz(flat, m, -REACH, REACH).astype(BF16)
         for part in range(2):
             span = pl.ds(128 * part, 128)
             ends[squared, pl.ds(128 * part, 16), span] = edge[16:].astype(BF16)
             ends[squared, pl.ds(128 * part + 112, 16), span] = edge[:16].astype(BF16)
-        column, flat, edge = column * column, flat * flat, edge * edge
-
-    lanes = lax.broadcasted_iota(jnp.int32, (128, 128), 1)
-    side = pl.ds(TILE, 128)
+        flat, edge = flat * flat, edge * edge
+
     def met(along, at, start, rows):
         even, odd = (row_even, row_odd) if along is row else (col_even, col_odd)
         parts = even[start : start + rows, :], odd[start : start + rows, :]
         return choose((along & 1) == 1, *(parts[::-1] if at else parts))
 
-    for i, ref in enumerate((high, low, var)):
-        ref[pl.ds(0, RIM), pl.ds(0, TILE)] = jnp.where(row > 0, met(row, 0, RIM * i, RIM), 0.0).astype(BF16)
-        ref[pl.ds(RIM + TILE, RIM), pl.ds(0, TILE)] = jnp.where(
-            row < rows_n - 1, met(row, 1, RIM * i, RIM), 0.0
-        ).astype(BF16)
-        ref[pl.ds(2 * RIM + TILE, RIM * 2), :] = jnp.zeros((2 * RIM, TILE + 128), BF16)
+    lanes = lax.broadcasted_iota(jnp.int32, (128, 128), 1)
+    at_west, at_east = (lanes >= 128 - RIM) & (col > 0), (lanes < RIM) & (col < cols_n - 1)
+    for i in range(3):
+        sides[i, pl.ds(2 * RIM + TILE, 2 * RIM), :] = jnp.zeros((2 * RIM, 128), BF16)
         west, east = met(col, 0, 128 * i, 128), met(col, 1, 128 * i, 128)
-        at_west, at_east = (lanes >= 128 - RIM) & (col > 0), (lanes < RIM) & (col < cols_n - 1)
         for g in range(8):
             near = pltpu.roll(east, 128 - RIM * g, 1) if g else east
             far = pltpu.roll(west, (112 - RIM * g) % 128, 1) if g != 7 else west
-            ref[pl.ds(RIM + 128 * g, 128), side] = jnp.where(at_east, near, jnp.where(at_west, far, 0.0)).astype(BF16)
+            sides[i, pl.ds(RIM + 128 * g, 128), :] = jnp.where(at_east, near, jnp.where(at_west, far, 0.0)).astype(BF16)
         for at, start in ((0, 384), (RIM + TILE, 432)):
             near, far = met(col, 1, start + RIM * i, RIM), met(col, 0, start + RIM * i, RIM)
-            ref[pl.ds(at, RIM), side] = jnp.where(at_east[:RIM], near, jnp.where(at_west[:RIM], far, 0.0)).astype(BF16)
-
-    spans = [(256 * c, 256) for c in range(4)] + [(TILE, 128)]
-    ready = 0
+            sides[i, pl.ds(at, RIM), :] = jnp.where(at_east[:RIM], near, jnp.where(at_west[:RIM], far, 0.0)).astype(BF16)
     for t in range(5):
         count = min(STEP, TILE - STEP * t)
-        while ready < 4 and 256 * ready < STEP * t + 240:
-            for copy in copies[ready]:
-                copy.wait()
-            rows = pl.ds(RIM + 256 * ready, 256)
-            high[rows, pl.ds(0, TILE)], low[rows, pl.ds(0, TILE)] = split(img_in[pl.ds(256 * ready, 256), :])
-            ready += 1
         window = pl.ds(STEP * t, 256)
         target = pl.ds(STEP * t, count)
-        for start, width in spans:
-            span = pl.ds(start, width)
-            value = dot(bands[0], high[window, span]) + dot(bands[0], low[window, span])
-            v_high[target, span], v_low[target, span] = split(value[:count])
-            v_var[target, span] = dot(bands[1], var[window, span])[:count].astype(BF16)
-
-    lanes = lax.broadcasted_iota(jnp.int32, (256, 128), 1)
-    near = lanes < 64
+        value = dot(bands[0], sides[0, window, :]) + dot(bands[0], sides[1, window, :])
+        v_side[0, target, :], v_side[1, target, :] = split(value[:count])
+        v_side[2, target, :] = dot(bands[1], sides[2, window, :])[:count].astype(BF16)
+    for copy in copies:
+        copy.wait()
+    for i in range(2):
+        mine, theirs = (pl.ds(RIM, 2 * RIM), pl.ds(0, RIM)) if i == 0 else (pl.ds(0, 2 * RIM), pl.ds(2 * RIM, RIM))
+        frame[0, mine, :], frame[1, mine, :] = split(img_in[i])
+        frame[2, mine, :] = var_in[i]
+        inside = row < rows_n - 1 if i else row > 0
+        for j in range(3):
+            frame[j, theirs, :] = jnp.where(inside, met(row, i, RIM * j, RIM), 0.0).astype(BF16)
+            frame[j, pl.ds(3 * RIM, RIM), :] = jnp.zeros((RIM, TILE), BF16)
+        value = dot(bands[0, :RIM, 0:64], frame[0]) + dot(bands[0, :RIM, 0:64], frame[1])
+        v_rim[0, i], v_rim[1, i] = split(value)
+        v_rim[2, i] = dot(bands[1, :RIM, 0:64], frame[2]).astype(BF16)
+
+    columns = (v_high, v_low, v_var)
+
+    def read(i, q, start, width):
+        span = pl.ds(start, width)
+        if q == 0:
+            return jnp.concatenate([v_rim[i, 0, :, span], columns[i][RIM:256, span]], 0)
+        if q == 3:
+            return jnp.concatenate([columns[i][768 : TILE - RIM, span], v_rim[i, 1, :, span]], 0)
+        return columns[i][256 * q : 256 * q + 256, span]
+
+    near = lax.broadcasted_iota(jnp.int32, (256, 128), 1) < 64
     for q in range(4):
         rows = pl.ds(256 * q, 256)
         results = []
-        for squared, parts in ((0, (v_high, v_low)), (1, (v_var,))):
-            def about(ref, w):
+        for squared, parts in ((0, (0, 1)), (1, (2,))):
+            def about(i, w):
                 if w == 0:
-                    return ref[rows, side]
-                return jnp.where(near, ref[rows, pl.ds(256 * w, 128)], ref[rows, pl.ds(256 * w - 128, 128)])
+                    return v_side[i, rows, :]
+                return jnp.where(near, read(i, q, 256 * w, 128), read(i, q, 256 * w - 128, 128))
 
             fixes = []
             for w in (0, 2):
-                both = sum(dot(jnp.concatenate([about(ref, w), about(ref, w + 1)], 1), ends[squared]) for ref in parts)
+                both = sum(dot(jnp.concatenate([about(i, w), about(i, w + 1)], 1), ends[squared]) for i in parts)
                 fixes += [both[:, :128], both[:, 128:]]
             fixes.append(fixes[0])
             values = []
             for c in range(4):
-                span = pl.ds(256 * c, 256)
-                main = sum(dot(ref[rows, span], flats[squared]) for ref in parts)
+                main = sum(dot(read(i, q, 256 * c, 256), flats[squared]) for i in parts)
                 values.append(main[:, :128] + jnp.where(near, fixes[c], 0.0))
                 values.append(main[:, 128:] + jnp.where(near, 0.0, fixes[c + 1]))
             results.append(values)
@@ -477,22 +531,29 @@
         pltpu.make_async_copy(out.at[rows, :], out_ref.at[rows, :], out_sems.at[q]).wait()
 
 
-def detect(psf, tile, tile_var, *rims):
-    vmem = pl.BlockSpec(memory_space=pltpu.VMEM)
-    wide = TILE + 128
+def detect(psf, tile, tile_var, columns, *rims):
     return pl.pallas_call(
         filter_kernel,
-        in_specs=[SMEM(), HBM, HBM, vmem, vmem, vmem, vmem],
+        in_specs=[SMEM(), HBM, HBM] + [VMEM] * 7,
         out_specs=HBM,
         out_shape=jax.ShapeDtypeStruct((TILE, TILE), F32),
-        scratch_shapes=[pltpu.VMEM((TILE, TILE), F32)]
-        + [pltpu.VMEM((1088, wide), BF16)] * 3
-        + [pltpu.VMEM((2, STEP, 256), BF16), pltpu.VMEM((2, 256, 256), BF16), pltpu.VMEM((2, 256, 256), BF16)]
-        + [pltpu.VMEM((TILE, wide), BF16)] * 3
-        + [pltpu.VMEM((TILE, TILE), F32), pltpu.SemaphoreType.DMA((8,)), pltpu.SemaphoreType.DMA((4,))],
-        compiler_params=pltpu.CompilerParams(vmem_limit_bytes=32 * MIB),
+        scratch_shapes=[
+            pltpu.VMEM((2, 2 * RIM, TILE), F32),
+            pltpu.VMEM((2, 2 * RIM, TILE), BF16),
+            pltpu.VMEM((3, 4 * RIM, TILE), BF16),
+            pltpu.VMEM((3, 1088, 128), BF16),
+            pltpu.VMEM((2, STEP, 256), BF16),
+            pltpu.VMEM((2, 256, 256), BF16),
+            pltpu.VMEM((2, 256, 256), BF16),
+            pltpu.VMEM((3, 2, RIM, TILE), BF16),
+            pltpu.VMEM((3, TILE, 128), BF16),
+            pltpu.VMEM((TILE, TILE), F32),
+            pltpu.SemaphoreType.DMA((4,)),
+            pltpu.SemaphoreType.DMA((4,)),
+        ],
+        compiler_params=pltpu.CompilerParams(vmem_limit_bytes=24 * MIB),
         name="filter",
-    )(psf, tile, tile_var, *rims)
+    )(psf, tile, tile_var, *columns, *rims)
 
 
 def shards(ccd_image, ccd_variance, basis_taps, coef_table, coef_pick, block_visit, visit_weight, patch_place, psf_taps):
@@ -515,8 +576,11 @@
     tile, *rims = gather(True, place, own_image, *arrived[:2], east, west)
     tile_var, up, down, first, last = gather(False, place, base_var, *arrived_var, rims)
     rows = swap(up, "trow", False), swap(down, "trow", True)
+    tile_read = pin(tile)
+    columns = list(column_pass(psf, tile_read, tile_var))
+    *rows, columns[0] = lax.optimization_barrier((*rows, columns[0]))
     sides = turn(first, last, *rows)
-    significance = detect(psf, pin(tile), tile_var, *rows, swap(sides[0], "tcol", False), swap(sides[1], "tcol", True))
+    significance = detect(psf, tile_read, tile_var, columns, *rows, swap(sides[0], "tcol", False), swap(sides[1], "tcol", True))
     return tile, significance
 
 

time: 65.8 us -> 63.3 us (0.962)
  waiting for transfers between devices: 18.3 us -> 14.9 us
  Pallas kernels: 29.2 us -> 31 us
  local copies, waits for them, and re-layouts: 1.61 us -> 0.95 us
    ppermute x12, waiting for transfers between devices: 18.3 us -> 14.9 us  [swap(): return lax.ppermute(value, ('trow', 'tcol'), pairs)]
    pallas_call x1 -> x2, Pallas kernels: 9 us -> 10.8 us  [the longest x1 6.49 us: detect(): pl.pallas_call(filter_kernel, in_specs=[SMEM(), HBM, HBM] + [VMEM] * 7, o...]
  transfers between devices with their start and end apart: 12 -> 12, of which waited for: 8 -> 7; matrix products, arithmetic and copies ran while one was open for 0% -> 0% of each run, Pallas kernels for 18% -> 25%
where the time goes in v3:
time: 63.3 us; the launch traced here: 63.1 us
  Pallas kernels  31 us (49%)
  starting transfers between devices  15.2 us (24%)
  waiting for transfers between devices  14.9 us (24%)
  local copies, waits for them, and re-layouts  0.95 us (2%)
  between operations  0.95 us (2%)
    ppermute x12, starting transfers between devices, swap(): return lax.ppermute(value, ('trow', 'tcol'), pairs)  15.2 us
    ppermute x12, waiting for transfers between devices, swap(): return lax.ppermute(value, ('trow', 'tcol'), pairs)  14.9 us
    pallas_call x2, Pallas kernels, match(): pl.pallas_call(functools.partial(match_kernel, squared), in_specs=[HBM] *...  12.8 us
    pallas_call x1, Pallas kernels, detect(): pl.pallas_call(filter_kernel, in_specs=[SMEM(), HBM, HBM] + [VMEM] * 7, o...  6.49 us
    pallas_call x2, Pallas kernels, gather(): pl.pallas_call(functools.partial(gather_kernel, image), in_specs=[SMEM()]...  5.94 us
    pallas_call x1, Pallas kernels, column_pass(): pl.pallas_call(column_kernel, in_specs=[SMEM(), HBM, HBM], out_specs=[VME...  4.32 us
    pallas_call x1, Pallas kernels, own_sum(): pl.pallas_call(add_own, in_specs=[SMEM(), VMEM], out_specs=VMEM, out_shap...  1.31 us
  transfers between devices with their start and end apart: 12, of which 7 were waited for; matrix products, arithmetic and copies ran while one was open for 0% of the time, Pallas kernels for 25%

profile of v3, /device:TPU:7, one launch (start us, length us, event | category | flops | bytes accessed | tf_op | source)
XLA Modules:
  0.0 63.1 jit_solution(14304005398599941699)
XLA Ops:
  0.6 0.0 copy-start
  0.6 0.8 %reshape.28.taps = f32[252]{0:T(256)S(1)} reshape(bf16[6,2,21]{2,1,0:T(2,128)(2,1)} %param.11) | data formatting | bytes 1512 | tf_op jit(solution)/shard_map/reshape | solution.py:561
  1.4 6.4 %match_img.1 = (bf16[3,528,128]{2,1,0:T(8,128)(2,1)S(1)}, bf16[3,528,128]{2,1,0:T(8,128)(2,1)S(1)}, bf16[1,528,128]{2,1,0:T(8,128)(2,1)S(1)}, bf16[1,528,128]{2,1,0:T(8,128)(2,1)S(1)}, bf16[32,128,128]{2,1,0:T(8,128)(2,1)S(1)}) custom-call(f32[8,6]{1,0:T(8,128)} %table_in.3, s32[1,1,2]{2,1,0:T(1,128)} %pick_in.3, s32[1,1,2]{2,1,0:T(1,128)} %visit_in.3, ...), custom_call_target="tpu_custom_call" | custom-call | tf_op jit(solution)/shard_map/match_img/pallas_call | solution.py:183
  7.8 1.4 %collective-permute-start = (bf16[3,528,128]{2,1,0:T(8,128)(2,1)S(1)}, bf16[3,528,128]{2,1,0:T(8,128)(2,1)S(1)}, u32[]{:S(2)}, u32[]{:S(2)}) collective-permute-start(bf16[3,528,128]{2,1,0:T(8,128)(2,1)S(1)} %get-tuple-element.41), channel_id=1, source_target_pairs={{0,8},{1,9},{2,10},{3,11},{4,12},{5,13},{6,14},{7,15},{8,0},{9,1},... | collective-permute-start | bytes 1216520 | tf_op jit(solution)/shard_map/ppermute | solution.py:224
  9.2 2.2 %collective-permute-start.1 = (bf16[3,528,128]{2,1,0:T(8,128)(2,1)S(1)}, bf16[3,528,128]{2,1,0:T(8,128)(2,1)S(1)}, u32[]{:S(2)}, u32[]{:S(2)}) collective-permute-start(bf16[3,528,128]{2,1,0:T(8,128)(2,1)S(1)} %get-tuple-element.42), channel_id=1, source_target_pairs={{0,1},{1,0},{2,3},{3,2},{4,5},{5,4},{6,7},{7,6},{8,16},{9,17},{10,... | collective-permute-start | bytes 1216520 | tf_op jit(solution)/shard_map/ppermute | solution.py:224
  11.3 6.4 %match_var.1 = (bf16[3,528,128]{2,1,0:T(8,128)(2,1)S(1)}, bf16[3,528,128]{2,1,0:T(8,128)(2,1)S(1)}, bf16[1,528,128]{2,1,0:T(8,128)(2,1)S(1)}, bf16[1,528,128]{2,1,0:T(8,128)(2,1)S(1)}, bf16[32,128,128]{2,1,0:T(8,128)(2,1)S(1)}) custom-call(f32[8,6]{1,0:T(8,128)} %table_in.3, s32[1,1,2]{2,1,0:T(1,128)} %pick_in.3, s32[1,1,2]{2,1,0:T(1,128)} %visit_in.3, ...), custom_call_target="tpu_custom_call" | custom-call | tf_op jit(solution)/shard_map/match_var/pallas_call | solution.py:183
  17.8 0.2 collective-permute-start.2
  18.0 1.4 %collective-permute-start.3 = (bf16[3,528,128]{2,1,0:T(8,128)(2,1)S(1)}, bf16[3,528,128]{2,1,0:T(8,128)(2,1)S(1)}, u32[]{:S(2)}, u32[]{:S(2)}) collective-permute-start(bf16[3,528,128]{2,1,0:T(8,128)(2,1)S(1)} %get-tuple-element.48), channel_id=1, source_target_pairs={{0,1},{1,0},{2,3},{3,2},{4,5},{5,4},{6,7},{7,6},{8,16},{9,17},{10,... | collective-permute-start | bytes 1216520 | tf_op jit(solution)/shard_map/ppermute | solution.py:224
  19.4 0.0 copy-done
  19.4 1.3 %own_var.1.start_ref = f32[1024,1024]{1,0:T(8,128)S(1)} custom-call(s32[32]{0:T(128)S(1)} %bitcast.3, bf16[32,128,128]{2,1,0:T(8,128)(2,1)S(1)} %get-tuple-element.44.own_ref), custom_call_target="tpu_custom_call" | custom-call | tf_op jit(solution)/shard_map/own_var/pallas_call | solution.py:269
  20.7 0.0 collective-permute-done.below_ref
  20.7 0.5 collective-permute-done.1.above_ref
  21.2 0.1 fusion.2
  21.3 1.9 %collective-permute-start.4 = (bf16[3,528,128]{2,1,0:T(8,128)(2,1)S(1)}, bf16[3,528,128]{2,1,0:T(8,128)(2,1)S(1)}, u32[]{:S(2)}, u32[]{:S(2)}) collective-permute-start(bf16[3,528,128]{2,1,0:T(8,128)(2,1)S(1)} %pad_maximum_fusion), channel_id=1, source_target_pairs={{0,1},{1,0},{2,3},{3,2},{4,5},{5,4},{6,7},{7,6},{8,9},{9,8},{10,11... | collective-permute-start | bytes 1216520 | tf_op jit(solution)/shard_map/ppermute | solution.py:224
  23.3 1.6 %collective-permute-start.5 = (bf16[3,528,128]{2,1,0:T(8,128)(2,1)S(1)}, bf16[3,528,128]{2,1,0:T(8,128)(2,1)S(1)}, u32[]{:S(2)}, u32[]{:S(2)}) collective-permute-start(bf16[3,528,128]{2,1,0:T(8,128)(2,1)S(1)} %pad_maximum_fusion.1), channel_id=1, source_target_pairs={{0,8},{1,2},{2,1},{3,4},{4,3},{5,6},{6,5},{7,15},{8,0},{9,10},{10,... | collective-permute-start | bytes 1216520 | tf_op jit(solution)/shard_map/ppermute | solution.py:224
  24.9 2.6 %collective-permute-done.2.below_ref = bf16[3,528,128]{2,1,0:T(8,128)(2,1)S(1)} collective-permute-done((bf16[3,528,128]{2,1,0:T(8,128)(2,1)S(1)}, bf16[3,528,128]{2,1,0:T(8,128)(2,1)S(1)}, u32[]{:S(2)}, u32[]{:S(2)}) %collective-permute-start.2) | collective-permute-done | bytes 405536 | tf_op jit(solution)/shard_map/ppermute | solution.py:224
  27.5 2.0 %collective-permute-done.3.above_ref = bf16[3,528,128]{2,1,0:T(8,128)(2,1)S(1)} collective-permute-done((bf16[3,528,128]{2,1,0:T(8,128)(2,1)S(1)}, bf16[3,528,128]{2,1,0:T(8,128)(2,1)S(1)}, u32[]{:S(2)}, u32[]{:S(2)}) %collective-permute-start.3) | collective-permute-done | bytes 405536 | tf_op jit(solution)/shard_map/ppermute | solution.py:224
  29.5 0.0 collective-permute-done.4.east_ref
  29.5 1.5 %collective-permute-done.5.west_ref = bf16[3,528,128]{2,1,0:T(8,128)(2,1)S(1)} collective-permute-done((bf16[3,528,128]{2,1,0:T(8,128)(2,1)S(1)}, bf16[3,528,128]{2,1,0:T(8,128)(2,1)S(1)}, u32[]{:S(2)}, u32[]{:S(2)}) %collective-permute-start.5) | collective-permute-done | bytes 405536 | tf_op jit(solution)/shard_map/ppermute | solution.py:224
  31.1 3.1 %collective-permute-start.6 = (bf16[3,528,128]{2,1,0:T(8,128)(2,1)S(1)}, bf16[3,528,128]{2,1,0:T(8,128)(2,1)S(1)}, u32[]{:S(2)}, u32[]{:S(2)}) collective-permute-start(bf16[3,528,128]{2,1,0:T(8,128)(2,1)S(1)} %pad_maximum_fusion.2), channel_id=1, source_target_pairs={{0,1},{1,0},{2,3},{3,2},{4,5},{5,4},{6,7},{7,6},{8,9},{9,8},{10,11... | collective-permute-start | bytes 1216520 | tf_op jit(solution)/shard_map/ppermute | solution.py:224
  34.3 0.1 collective-permute-start.7
  34.3 3.8 %gather_img.1 = (f32[1024,1024]{1,0:T(8,128)}, bf16[32,1024]{1,0:T(8,128)(2,1)S(1)}, bf16[32,1024]{1,0:T(8,128)(2,1)S(1)}, bf16[256,128]{1,0:T(8,128)(2,1)S(1)}, bf16[256,128]{1,0:T(8,128)(2,1)S(1)}) custom-call(s32[32]{0:T(128)S(1)} %bitcast.4, bf16[32,128,128]{2,1,0:T(8,128)(2,1)S(1)} %get-tuple-element.40.start_ref, ...), custom_call_target="tpu_custom_call" | custom-call | tf_op jit(solution)/shard_map/gather_img/pallas_call | solution.py:322
  38.2 0.0 collective-permute-done.6.east_ref
  38.2 3.7 %collective-permute-done.7.west_ref = bf16[3,528,128]{2,1,0:T(8,128)(2,1)S(1)} collective-permute-done((bf16[3,528,128]{2,1,0:T(8,128)(2,1)S(1)}, bf16[3,528,128]{2,1,0:T(8,128)(2,1)S(1)}, u32[]{:S(2)}, u32[]{:S(2)}) %collective-permute-start.7) | collective-permute-done | bytes 405536 | tf_op jit(solution)/shard_map/ppermute | solution.py:224
  41.9 0.0 copy-start.1
  41.9 2.1 %gather_var.1 = (bf16[1024,1024]{1,0:T(8,128)(2,1)S(1)}, bf16[48,1024]{1,0:T(8,128)(2,1)S(1)}, bf16[48,1024]{1,0:T(8,128)(2,1)S(1)}, bf16[384,128]{1,0:T(8,128)(2,1)S(1)}, bf16[384,128]{1,0:T(8,128)(2,1)S(1)}) custom-call(s32[32]{0:T(128)S(1)} %bitcast.5, f32[1024,1024]{1,0:T(8,128)S(1)} %own_var.1.start_ref, ...), custom_call_target="tpu_custom_call" | custom-call | tf_op jit(solution)/shard_map/gather_var/pallas_call | solution.py:322
  44.0 0.3 collective-permute-start.8
  44.3 2.0 %collective-permute-start.9 = (bf16[48,1024]{1,0:T(8,128)(2,1)S(1)}, bf16[48,1024]{1,0:T(8,128)(2,1)S(1)}, u32[]{:S(2)}, u32[]{:S(2)}) collective-permute-start(bf16[48,1024]{1,0:T(8,128)(2,1)S(1)} %get-tuple-element.65), channel_id=1, source_target_pairs={{0,1},{1,0},{2,3},{3,2},{4,5},{5,4},{6,7},{7,6},{8,16},{9,17},{10,... | collective-permute-start | bytes 294920 | tf_op jit(solution)/shard_map/ppermute | solution.py:224
  46.3 0.0 copy-done.1
  46.3 0.1 reshape.26.psf
  46.3 4.3 %column.1 = (bf16[1024,1024]{1,0:T(8,128)(2,1)S(1)}, bf16[1024,1024]{1,0:T(8,128)(2,1)S(1)}, bf16[1024,1024]{1,0:T(8,128)(2,1)S(1)}) custom-call(f32[62]{0:T(128)S(1)} %reshape.26.psf, f32[1024,1024]{1,0:T(8,128)} %get-tuple-element.37.tile_ref, bf16[1024,1024]{1,0:T(8,128)(2,1)S(1)} %get-tuple-element.63.var_ref), custom_call_target="tpu_custom_call" | custom-call | tf_op jit(solution)/shard_map/column/pallas_call | solution.py:416
  50.7 0.0 collective-permute-done.8.even_first.even_last.row_even
  50.7 0.0 collective-permute-done.9.odd_first.odd_last.row_odd
  50.7 0.1 turn.1
  50.8 1.1 %collective-permute-start.10 = (bf16[480,128]{1,0:T(8,128)(2,1)S(1)}, bf16[480,128]{1,0:T(8,128)(2,1)S(1)}, u32[]{:S(2)}, u32[]{:S(2)}) collective-permute-start(bf16[480,128]{1,0:T(8,128)(2,1)S(1)} %get-tuple-element.74), channel_id=1, source_target_pairs={{0,1},{1,0},{2,3},{3,2},{4,5},{5,4},{6,7},{7,6},{8,9},{9,8},{10,11... | collective-permute-start | bytes 368648 | tf_op jit(solution)/shard_map/ppermute | solution.py:224
  51.8 0.0 collective-permute-start.11
  51.9 1.0 %collective-permute-done.10.col_even = bf16[480,128]{1,0:T(8,128)(2,1)S(1)} collective-permute-done((bf16[480,128]{1,0:T(8,128)(2,1)S(1)}, bf16[480,128]{1,0:T(8,128)(2,1)S(1)}, u32[]{:S(2)}, u32[]{:S(2)}) %collective-permute-start.10) | collective-permute-done | bytes 122912 | tf_op jit(solution)/shard_map/ppermute | solution.py:224
  52.8 3.6 %collective-permute-done.11.col_odd = bf16[480,128]{1,0:T(8,128)(2,1)S(1)} collective-permute-done((bf16[480,128]{1,0:T(8,128)(2,1)S(1)}, bf16[480,128]{1,0:T(8,128)(2,1)S(1)}, u32[]{:S(2)}, u32[]{:S(2)}) %collective-permute-start.11) | collective-permute-done | bytes 122912 | tf_op jit(solution)/shard_map/ppermute | solution.py:224
  56.4 6.5 %filter.1 = f32[1024,1024]{1,0:T(8,128)} custom-call(f32[62]{0:T(128)S(1)} %reshape.26.psf, f32[1024,1024]{1,0:T(8,128)} %get-tuple-element.37.tile_ref, bf16[1024,1024]{1,0:T(8,128)(2,1)S(1)} %get-tuple-element.63.var_ref, bf16[1024,1024]{1,0:T(8,128)(2,1)S(1)} %get-tuple-element.67.v_high, bf16[1024,1024]{1,0:T(8,128)(2,1)S(1)} %get-tuple-element.68.v_low, ...), custom_call_target="tpu_custom_call" | custom-call | tf_op jit(solution)/shard_map/filter/pallas_call | solution.py:535
  (6 shorter events, 0.2 us)
Async XLA Ops:
  0.6 18.8 %copy-start = (s32[1,1,32]{2,1,0:T(1,128)S(1)}, s32[1,1,32]{2,1,0:T(1,128)}, u32[]{:S(2)}) copy-start(s32[1,1,32]{2,1,0:T(1,128)} %place_in.3) | copy-start | bytes 388
  7.8 12.9 %collective-permute-start = (bf16[3,528,128]{2,1,0:T(8,128)(2,1)S(1)}, bf16[3,528,128]{2,1,0:T(8,128)(2,1)S(1)}, u32[]{:S(2)}, u32[]{:S(2)}) collective-permute-start(bf16[3,528,128]{2,1,0:T(8,128)(2,1)S(1)} %get-tuple-element.41), channel_id=1, source_target_pairs={{0,8},{1,9},{2,10},{3,11},{4,12},{5,13},{6,14},{7,15},{8,0},{9,1},... | collective-permute-start | bytes 1216520 | tf_op jit(solution)/shard_map/ppermute | solution.py:224
  9.2 12.0 %collective-permute-start.1 = (bf16[3,528,128]{2,1,0:T(8,128)(2,1)S(1)}, bf16[3,528,128]{2,1,0:T(8,128)(2,1)S(1)}, u32[]{:S(2)}, u32[]{:S(2)}) collective-permute-start(bf16[3,528,128]{2,1,0:T(8,128)(2,1)S(1)} %get-tuple-element.42), channel_id=1, source_target_pairs={{0,1},{1,0},{2,3},{3,2},{4,5},{5,4},{6,7},{7,6},{8,16},{9,17},{10,... | collective-permute-start | bytes 1216520 | tf_op jit(solution)/shard_map/ppermute | solution.py:224
  17.8 9.7 %collective-permute-start.2 = (bf16[3,528,128]{2,1,0:T(8,128)(2,1)S(1)}, bf16[3,528,128]{2,1,0:T(8,128)(2,1)S(1)}, u32[]{:S(2)}, u32[]{:S(2)}) collective-permute-start(bf16[3,528,128]{2,1,0:T(8,128)(2,1)S(1)} %get-tuple-element.47), channel_id=1, source_target_pairs={{0,8},{1,9},{2,10},{3,11},{4,12},{5,13},{6,14},{7,15},{8,0},{9,1},... | collective-permute-start | bytes 1216520 | tf_op jit(solution)/shard_map/ppermute | solution.py:224
  18.0 11.5 %collective-permute-start.3 = (bf16[3,528,128]{2,1,0:T(8,128)(2,1)S(1)}, bf16[3,528,128]{2,1,0:T(8,128)(2,1)S(1)}, u32[]{:S(2)}, u32[]{:S(2)}) collective-permute-start(bf16[3,528,128]{2,1,0:T(8,128)(2,1)S(1)} %get-tuple-element.48), channel_id=1, source_target_pairs={{0,1},{1,0},{2,3},{3,2},{4,5},{5,4},{6,7},{7,6},{8,16},{9,17},{10,... | collective-permute-start | bytes 1216520 | tf_op jit(solution)/shard_map/ppermute | solution.py:224
  21.3 8.2 %collective-permute-start.4 = (bf16[3,528,128]{2,1,0:T(8,128)(2,1)S(1)}, bf16[3,528,128]{2,1,0:T(8,128)(2,1)S(1)}, u32[]{:S(2)}, u32[]{:S(2)}) collective-permute-start(bf16[3,528,128]{2,1,0:T(8,128)(2,1)S(1)} %pad_maximum_fusion), channel_id=1, source_target_pairs={{0,1},{1,0},{2,3},{3,2},{4,5},{5,4},{6,7},{7,6},{8,9},{9,8},{10,11... | collective-permute-start | bytes 1216520 | tf_op jit(solution)/shard_map/ppermute | solution.py:224
  23.3 7.7 %collective-permute-start.5 = (bf16[3,528,128]{2,1,0:T(8,128)(2,1)S(1)}, bf16[3,528,128]{2,1,0:T(8,128)(2,1)S(1)}, u32[]{:S(2)}, u32[]{:S(2)}) collective-permute-start(bf16[3,528,128]{2,1,0:T(8,128)(2,1)S(1)} %pad_maximum_fusion.1), channel_id=1, source_target_pairs={{0,8},{1,2},{2,1},{3,4},{4,3},{5,6},{6,5},{7,15},{8,0},{9,10},{10,... | collective-permute-start | bytes 1216520 | tf_op jit(solution)/shard_map/ppermute | solution.py:224
  31.1 7.0 %collective-permute-start.6 = (bf16[3,528,128]{2,1,0:T(8,128)(2,1)S(1)}, bf16[3,528,128]{2,1,0:T(8,128)(2,1)S(1)}, u32[]{:S(2)}, u32[]{:S(2)}) collective-permute-start(bf16[3,528,128]{2,1,0:T(8,128)(2,1)S(1)} %pad_maximum_fusion.2), channel_id=1, source_target_pairs={{0,1},{1,0},{2,3},{3,2},{4,5},{5,4},{6,7},{7,6},{8,9},{9,8},{10,11... | collective-permute-start | bytes 1216520 | tf_op jit(solution)/shard_map/ppermute | solution.py:224
  34.3 7.6 %collective-permute-start.7 = (bf16[3,528,128]{2,1,0:T(8,128)(2,1)S(1)}, bf16[3,528,128]{2,1,0:T(8,128)(2,1)S(1)}, u32[]{:S(2)}, u32[]{:S(2)}) collective-permute-start(bf16[3,528,128]{2,1,0:T(8,128)(2,1)S(1)} %pad_maximum_fusion.3), channel_id=1, source_target_pairs={{0,8},{1,2},{2,1},{3,4},{4,3},{5,6},{6,5},{7,15},{8,0},{9,10},{10,... | collective-permute-start | bytes 1216520 | tf_op jit(solution)/shard_map/ppermute | solution.py:224
  41.9 4.4 %copy-start.1 = (f32[2,31]{1,0:T(2,128)S(1)}, f32[2,31]{1,0:T(2,128)}, u32[]{:S(2)}) copy-start(f32[2,31]{1,0:T(2,128)} %param.17) | copy-start | bytes 748
  44.0 6.7 %collective-permute-start.8 = (bf16[48,1024]{1,0:T(8,128)(2,1)S(1)}, bf16[48,1024]{1,0:T(8,128)(2,1)S(1)}, u32[]{:S(2)}, u32[]{:S(2)}) collective-permute-start(bf16[48,1024]{1,0:T(8,128)(2,1)S(1)} %get-tuple-element.64), channel_id=1, source_target_pairs={{0,8},{1,9},{2,10},{3,11},{4,12},{5,13},{6,14},{7,15},{8,0},{9,1},... | collective-permute-start | bytes 294920 | tf_op jit(solution)/shard_map/ppermute | solution.py:224
  44.3 6.4 %collective-permute-start.9 = (bf16[48,1024]{1,0:T(8,128)(2,1)S(1)}, bf16[48,1024]{1,0:T(8,128)(2,1)S(1)}, u32[]{:S(2)}, u32[]{:S(2)}) collective-permute-start(bf16[48,1024]{1,0:T(8,128)(2,1)S(1)} %get-tuple-element.65), channel_id=1, source_target_pairs={{0,1},{1,0},{2,3},{3,2},{4,5},{5,4},{6,7},{7,6},{8,16},{9,17},{10,... | collective-permute-start | bytes 294920 | tf_op jit(solution)/shard_map/ppermute | solution.py:224
  50.8 2.0 %collective-permute-start.10 = (bf16[480,128]{1,0:T(8,128)(2,1)S(1)}, bf16[480,128]{1,0:T(8,128)(2,1)S(1)}, u32[]{:S(2)}, u32[]{:S(2)}) collective-permute-start(bf16[480,128]{1,0:T(8,128)(2,1)S(1)} %get-tuple-element.74), channel_id=1, source_target_pairs={{0,1},{1,0},{2,3},{3,2},{4,5},{5,4},{6,7},{7,6},{8,9},{9,8},{10,11... | collective-permute-start | bytes 368648 | tf_op jit(solution)/shard_map/ppermute | solution.py:224
  51.8 4.6 %collective-permute-start.11 = (bf16[480,128]{1,0:T(8,128)(2,1)S(1)}, bf16[480,128]{1,0:T(8,128)(2,1)S(1)}, u32[]{:S(2)}, u32[]{:S(2)}) collective-permute-start(bf16[480,128]{1,0:T(8,128)(2,1)S(1)} %get-tuple-element.75), channel_id=1, source_target_pairs={{0,8},{1,2},{2,1},{3,4},{4,3},{5,6},{6,5},{7,15},{8,0},{9,10},{10,... | collective-permute-start | bytes 368648 | tf_op jit(solution)/shard_map/ppermute | solution.py:224

commit v4 on v3

--- a/solution.py
+++ b/solution.py
@@ -426,12 +426,35 @@
     )(psf, tile, tile_var)
 
 
-def filter_kernel(
-    psf, tile_ref, var_ref, v_high, v_low, v_var, row_even, row_odd, col_even, col_odd, out_ref,
-    img_in, var_in, frame, sides, bands, flats, ends, v_rim, v_side, out, in_sems, out_sems,
+def row_bands(psf, flats, ends):
+    over = 1.0 / jnp.full((16, 256), largest(psf, 0), F32)
+    flat = diagonals(tap(psf, 0), PSF, REACH, -1, 256) * over
+    edge = corner(tap(psf, 0), PSF, REACH) * over[0:1, :128]
+    ends[...] = jnp.zeros(ends.shape, BF16)
+    for squared in range(2):
+        for m in range(16 if flats is not None else 0):
+            flats[squared, pl.ds(16 * m, 16), :] = toeplitz(flat, m, -REACH, REACH).astype(BF16)
+        for part in range(ends.shape[1] // 128):
+            span = pl.ds(128 * part, 128)
+            ends[squared, pl.ds(128 * part, 16), span] = edge[16:].astype(BF16)
+            ends[squared, pl.ds(128 * part + 112, 16), span] = edge[:16].astype(BF16)
+        flat, edge = flat * flat, edge * edge
+
+
+def met(along, even, odd, at, start, rows):
+    parts = even[start : start + rows, :], odd[start : start + rows, :]
+    return choose((along & 1) == 1, *(parts[::-1] if at else parts))
+
+
+def significance(scale, smooth, variance):
+    return scale * smooth * lax.rsqrt(scale * scale * variance + 1.0)
+
+
+def row_kernel(
+    psf, tile_ref, var_ref, v_high, v_low, v_var, row_even, row_odd, out_ref, part_ref,
+    img_in, var_in, frame, bands, flats, ends, v_rim, out, in_sems, out_sems,
 ):
     row, rows_n = lax.axis_index("trow"), lax.axis_size("trow")
-    col, cols_n = lax.axis_index("tcol"), lax.axis_size("tcol")
     copies = []
     for i, start in enumerate((0, TILE - 2 * RIM)):
         rows = pl.ds(start, 2 * RIM)
@@ -441,35 +464,98 @@
         copy.start()
     scale = largest(psf, 0) * largest(psf, 1)
     column_bands(psf, bands)
-    over = 1.0 / jnp.full((16, 256), largest(psf, 0), F32)
-    flat = diagonals(tap(psf, 0), PSF, REACH, -1, 256) * over
-    edge = corner(tap(psf, 0), PSF, REACH) * over[0:1, :128]
-    ends[...] = jnp.zeros(ends.shape, BF16)
-    for squared in range(2):
-        for m in range(16):
-            flats[squared, pl.ds(16 * m, 16), :] = toeplitz(flat, m, -REACH, REACH).astype(BF16)
-        for part in range(2):
-            span = pl.ds(128 * part, 128)
-            ends[squared, pl.ds(128 * part, 16), span] = edge[16:].astype(BF16)
-            ends[squared, pl.ds(128 * part + 112, 16), span] = edge[:16].astype(BF16)
-        flat, edge = flat * flat, edge * edge
-
-    def met(along, at, start, rows):
-        even, odd = (row_even, row_odd) if along is row else (col_even, col_odd)
-        parts = even[start : start + rows, :], odd[start : start + rows, :]
-        return choose((along & 1) == 1, *(parts[::-1] if at else parts))
-
+    row_bands(psf, flats, ends)
+    for copy in copies:
+        copy.wait()
+    for i in range(2):
+        mine, theirs = (pl.ds(RIM, 2 * RIM), pl.ds(0, RIM)) if i == 0 else (pl.ds(0, 2 * RIM), pl.ds(2 * RIM, RIM))
+        frame[0, mine, :], frame[1, mine, :] = split(img_in[i])
+        frame[2, mine, :] = var_in[i]
+        inside = row < rows_n - 1 if i else row > 0
+        for j in range(3):
+            frame[j, theirs, :] = jnp.where(inside, met(row, row_even, row_odd, i, RIM * j, RIM), 0.0).astype(BF16)
+            frame[j, pl.ds(3 * RIM, RIM), :] = jnp.zeros((RIM, TILE), BF16)
+        value = dot(bands[0, :RIM, 0:64], frame[0]) + dot(bands[0, :RIM, 0:64], frame[1])
+        v_rim[0, i], v_rim[1, i] = split(value)
+        v_rim[2, i] = dot(bands[1, :RIM, 0:64], frame[2]).astype(BF16)
+
+    columns = (v_high, v_low, v_var)
+
+    def read(i, q, start, width):
+        span = pl.ds(start, width)
+        if q == 0:
+            return jnp.concatenate([v_rim[i, 0, :, span], columns[i][RIM:256, span]], 0)
+        if q == 3:
+            return jnp.concatenate([columns[i][768 : TILE - RIM, span], v_rim[i, 1, :, span]], 0)
+        return columns[i][256 * q : 256 * q + 256, span]
+
+    near = lax.broadcasted_iota(jnp.int32, (256, 128), 1) < 64
+    inner = pl.ds(128, TILE - 256)
+    for q in range(4):
+        rows = pl.ds(256 * q, 256)
+        results = []
+        for squared, parts in ((0, (0, 1)), (1, (2,))):
+            def about(i, w):
+                return jnp.where(near, read(i, q, 256 * w, 128), read(i, q, 256 * w - 128, 128))
+
+            both = sum(dot(jnp.concatenate([about(i, 1), about(i, 2)], 1), ends[squared]) for i in parts)
+            last = sum(dot(about(i, 3), ends[squared, 0:128, 0:128]) for i in parts)
+            fixes = [None, both[:, :128], both[:, 128:], last, None]
+            values = []
+            for c in range(4):
+                main = sum(dot(read(i, q, 256 * c, 256), flats[squared]) for i in parts)
+                values.append(main[:, :128] + jnp.where(near, fixes[c], 0.0) if c > 0 else main[:, :128])
+                values.append(main[:, 128:] + jnp.where(near, 0.0, fixes[c + 1]) if c < 3 else main[:, 128:])
+            results.append(values)
+            part_ref[squared, rows, 0:128] = values[0]
+            part_ref[squared, rows, 128:256] = values[7]
+        for c in range(1, 7):
+            out[rows, pl.ds(128 * c, 128)] = significance(scale, results[0][c], results[1][c])
+        pltpu.make_async_copy(out.at[rows, inner], out_ref.at[rows, inner], out_sems.at[q]).start()
+    for q in range(4):
+        rows = pl.ds(256 * q, 256)
+        pltpu.make_async_copy(out.at[rows, inner], out_ref.at[rows, inner], out_sems.at[q]).wait()
+
+
+def row_pass(psf, tile, tile_var, columns, *rims):
+    return pl.pallas_call(
+        row_kernel,
+        in_specs=[SMEM(), HBM, HBM] + [VMEM] * 5,
+        out_specs=[HBM, VMEM],
+        out_shape=[jax.ShapeDtypeStruct((TILE, TILE), F32), jax.ShapeDtypeStruct((2, TILE, 256), F32)],
+        scratch_shapes=[
+            pltpu.VMEM((2, 2 * RIM, TILE), F32),
+            pltpu.VMEM((2, 2 * RIM, TILE), BF16),
+            pltpu.VMEM((3, 4 * RIM, TILE), BF16),
+            pltpu.VMEM((2, STEP, 256), BF16),
+            pltpu.VMEM((2, 256, 256), BF16),
+            pltpu.VMEM((2, 256, 256), BF16),
+            pltpu.VMEM((3, 2, RIM, TILE), BF16),
+            pltpu.VMEM((TILE, TILE), F32),
+            pltpu.SemaphoreType.DMA((4,)),
+            pltpu.SemaphoreType.DMA((4,)),
+        ],
+        compiler_params=pltpu.CompilerParams(vmem_limit_bytes=24 * MIB),
+        name="row",
+    )(psf, tile, tile_var, *columns, *rims)
+
+
+def side_kernel(psf, held, part_ref, col_even, col_odd, out_ref, sides, bands, ends, v_side, out, out_sems):
+    col, cols_n = lax.axis_index("tcol"), lax.axis_size("tcol")
+    scale = largest(psf, 0) * largest(psf, 1)
+    column_bands(psf, bands)
+    row_bands(psf, None, ends)
     lanes = lax.broadcasted_iota(jnp.int32, (128, 128), 1)
     at_west, at_east = (lanes >= 128 - RIM) & (col > 0), (lanes < RIM) & (col < cols_n - 1)
     for i in range(3):
         sides[i, pl.ds(2 * RIM + TILE, 2 * RIM), :] = jnp.zeros((2 * RIM, 128), BF16)
-        west, east = met(col, 0, 128 * i, 128), met(col, 1, 128 * i, 128)
+        west, east = (met(col, col_even, col_odd, at, 128 * i, 128) for at in range(2))
         for g in range(8):
             near = pltpu.roll(east, 128 - RIM * g, 1) if g else east
             far = pltpu.roll(west, (112 - RIM * g) % 128, 1) if g != 7 else west
             sides[i, pl.ds(RIM + 128 * g, 128), :] = jnp.where(at_east, near, jnp.where(at_west, far, 0.0)).astype(BF16)
         for at, start in ((0, 384), (RIM + TILE, 432)):
-            near, far = met(col, 1, start + RIM * i, RIM), met(col, 0, start + RIM * i, RIM)
+            far, near = (met(col, col_even, col_odd, side, start + RIM * i, RIM) for side in range(2))
             sides[i, pl.ds(at, RIM), :] = jnp.where(at_east[:RIM], near, jnp.where(at_west[:RIM], far, 0.0)).astype(BF16)
     for t in range(5):
         count = min(STEP, TILE - STEP * t)
@@ -478,82 +564,42 @@
         value = dot(bands[0], sides[0, window, :]) + dot(bands[0], sides[1, window, :])
         v_side[0, target, :], v_side[1, target, :] = split(value[:count])
         v_side[2, target, :] = dot(bands[1], sides[2, window, :])[:count].astype(BF16)
+    near = lax.broadcasted_iota(jnp.int32, (256, 128), 1) < 64
+    copies = []
+    for q in range(4):
+        rows = pl.ds(256 * q, 256)
+        smooth = dot(v_side[0, rows, :], ends[0]) + dot(v_side[1, rows, :], ends[0])
+        variance = dot(v_side[2, rows, :], ends[1])
+        for side, start in ((0, 0), (1, TILE - 128)):
+            fixes = [jnp.where(near, 0.0, x) if side else jnp.where(near, x, 0.0) for x in (smooth, variance)]
+            span = pl.ds(128 * side, 128)
+            sums = [part_ref[squared, rows, span] + fixes[squared] for squared in range(2)]
+            out[rows, span] = significance(scale, *sums)
+            copy = pltpu.make_async_copy(out.at[rows, span], out_ref.at[rows, pl.ds(start, 128)], out_sems.at[2 * q + side])
+            copy.start()
+            copies.append(copy)
     for copy in copies:
         copy.wait()
-    for i in range(2):
-        mine, theirs = (pl.ds(RIM, 2 * RIM), pl.ds(0, RIM)) if i == 0 else (pl.ds(0, 2 * RIM), pl.ds(2 * RIM, RIM))
-        frame[0, mine, :], frame[1, mine, :] = split(img_in[i])
-        frame[2, mine, :] = var_in[i]
-        inside = row < rows_n - 1 if i else row > 0
-        for j in range(3):
-            frame[j, theirs, :] = jnp.where(inside, met(row, i, RIM * j, RIM), 0.0).astype(BF16)
-            frame[j, pl.ds(3 * RIM, RIM), :] = jnp.zeros((RIM, TILE), BF16)
-        value = dot(bands[0, :RIM, 0:64], frame[0]) + dot(bands[0, :RIM, 0:64], frame[1])
-        v_rim[0, i], v_rim[1, i] = split(value)
-        v_rim[2, i] = dot(bands[1, :RIM, 0:64], frame[2]).astype(BF16)
-
-    columns = (v_high, v_low, v_var)
-
-    def read(i, q, start, width):
-        span = pl.ds(start, width)
-        if q == 0:
-            return jnp.concatenate([v_rim[i, 0, :, span], columns[i][RIM:256, span]], 0)
-        if q == 3:
-            return jnp.concatenate([columns[i][768 : TILE - RIM, span], v_rim[i, 1, :, span]], 0)
-        return columns[i][256 * q : 256 * q + 256, span]
-
-    near = lax.broadcasted_iota(jnp.int32, (256, 128), 1) < 64
-    for q in range(4):
-        rows = pl.ds(256 * q, 256)
-        results = []
-        for squared, parts in ((0, (0, 1)), (1, (2,))):
-            def about(i, w):
-                if w == 0:
-                    return v_side[i, rows, :]
-                return jnp.where(near, read(i, q, 256 * w, 128), read(i, q, 256 * w - 128, 128))
-
-            fixes = []
-            for w in (0, 2):
-                both = sum(dot(jnp.concatenate([about(i, w), about(i, w + 1)], 1), ends[squared]) for i in parts)
-                fixes += [both[:, :128], both[:, 128:]]
-            fixes.append(fixes[0])
-            values = []
-            for c in range(4):
-                main = sum(dot(read(i, q, 256 * c, 256), flats[squared]) for i in parts)
-                values.append(main[:, :128] + jnp.where(near, fixes[c], 0.0))
-                values.append(main[:, 128:] + jnp.where(near, 0.0, fixes[c + 1]))
-            results.append(values)
-        for c in range(8):
-            out[rows, pl.ds(128 * c, 128)] = scale * results[0][c] * lax.rsqrt(scale * scale * results[1][c] + 1.0)
-        pltpu.make_async_copy(out.at[rows, :], out_ref.at[rows, :], out_sems.at[q]).start()
-    for q in range(4):
-        rows = pl.ds(256 * q, 256)
-        pltpu.make_async_copy(out.at[rows, :], out_ref.at[rows, :], out_sems.at[q]).wait()
-
-
-def detect(psf, tile, tile_var, columns, *rims):
+
+
+def side_pass(psf, held, part, *rims):
     return pl.pallas_call(
-        filter_kernel,
-        in_specs=[SMEM(), HBM, HBM] + [VMEM] * 7,
+        side_kernel,
+        in_specs=[SMEM(), HBM] + [VMEM] * 3,
         out_specs=HBM,
         out_shape=jax.ShapeDtypeStruct((TILE, TILE), F32),
         scratch_shapes=[
-            pltpu.VMEM((2, 2 * RIM, TILE), F32),
-            pltpu.VMEM((2, 2 * RIM, TILE), BF16),
-            pltpu.VMEM((3, 4 * RIM, TILE), BF16),
             pltpu.VMEM((3, 1088, 128), BF16),
             pltpu.VMEM((2, STEP, 256), BF16),
-            pltpu.VMEM((2, 256, 256), BF16),
-            pltpu.VMEM((2, 256, 256), BF16),
-            pltpu.VMEM((3, 2, RIM, TILE), BF16),
+            pltpu.VMEM((2, 128, 128), BF16),
             pltpu.VMEM((3, TILE, 128), BF16),
-            pltpu.VMEM((TILE, TILE), F32),
-            pltpu.SemaphoreType.DMA((4,)),
-            pltpu.SemaphoreType.DMA((4,)),
+            pltpu.VMEM((TILE, 256), F32),
+            pltpu.SemaphoreType.DMA((8,)),
         ],
-        compiler_params=pltpu.CompilerParams(vmem_limit_bytes=24 * MIB),
-        name="filter",
-    )(psf, tile, tile_var, *columns, *rims)
+        input_output_aliases={1: 0},
+        compiler_params=pltpu.CompilerParams(vmem_limit_bytes=12 * MIB),
+        name="side",
+    )(psf, held, part, *rims)
 
 
 def shards(ccd_image, ccd_variance, basis_taps, coef_table, coef_pick, block_visit, visit_weight, patch_place, psf_taps):
@@ -580,8 +626,10 @@
     columns = list(column_pass(psf, tile_read, tile_var))
     *rows, columns[0] = lax.optimization_barrier((*rows, columns[0]))
     sides = turn(first, last, *rows)
-    significance = detect(psf, tile_read, tile_var, columns, *rows, swap(sides[0], "tcol", False), swap(sides[1], "tcol", True))
-    return tile, significance
+    met_sides = swap(sides[0], "tcol", False), swap(sides[1], "tcol", True)
+    held, part = row_pass(psf, tile_read, tile_var, columns, *rows)
+    *met_sides, part = lax.optimization_barrier((*met_sides, part))
+    return tile, side_pass(psf, held, part, *met_sides)
 
 
 def solution(mesh):

time: 63.3 us -> 61 us (0.964)
  waiting for transfers between devices: 14.9 us -> 10.2 us
  Pallas kernels: 31 us -> 32.9 us
    ppermute x12, waiting for transfers between devices: 14.9 us -> 10.2 us  [swap(): return lax.ppermute(value, ('trow', 'tcol'), pairs)]
    pallas_call x1 -> x2, Pallas kernels: 6.49 us -> 8.25 us  [the longest x1 5.73 us: row_pass(): pl.pallas_call(row_kernel, in_specs=[SMEM(), HBM, HBM] + [VMEM] * 5, out_...]
  transfers between devices with their start and end apart: 12 -> 12, of which waited for: 7 -> 5; matrix products, arithmetic and copies ran while one was open for 0% -> 0% of each run, Pallas kernels for 25% -> 36%
where the time goes in v4:
time: 61 us; the launch traced here: 60.3 us
  Pallas kernels  32.9 us (54%)
  starting transfers between devices  15.2 us (25%)
  waiting for transfers between devices  10.2 us (17%)
  between operations  0.97 us (2%)
  local copies, waits for them, and re-layouts  0.95 us (2%)
    ppermute x12, starting transfers between devices, swap(): return lax.ppermute(value, ('trow', 'tcol'), pairs)  15.2 us
    pallas_call x2, Pallas kernels, match(): pl.pallas_call(functools.partial(match_kernel, squared), in_specs=[HBM] *...  12.8 us
    ppermute x12, waiting for transfers between devices, swap(): return lax.ppermute(value, ('trow', 'tcol'), pairs)  10.2 us
    pallas_call x2, Pallas kernels, gather(): pl.pallas_call(functools.partial(gather_kernel, image), in_specs=[SMEM()]...  6.02 us
    pallas_call x1, Pallas kernels, row_pass(): pl.pallas_call(row_kernel, in_specs=[SMEM(), HBM, HBM] + [VMEM] * 5, out_...  5.73 us
    pallas_call x1, Pallas kernels, column_pass(): pl.pallas_call(column_kernel, in_specs=[SMEM(), HBM, HBM], out_specs=[VME...  4.32 us
    pallas_call x1, Pallas kernels, side_pass(): pl.pallas_call(side_kernel, in_specs=[SMEM(), HBM] + [VMEM] * 3, out_spec...  2.52 us
    pallas_call x1, Pallas kernels, own_sum(): pl.pallas_call(add_own, in_specs=[SMEM(), VMEM], out_specs=VMEM, out_shap...  1.37 us
  transfers between devices with their start and end apart: 12, of which 5 were waited for; matrix products, arithmetic and copies ran while one was open for 0% of the time, Pallas kernels for 36%

profile of v4, /device:TPU:7, one launch (start us, length us, event | category | flops | bytes accessed | tf_op | source)
XLA Modules:
  0.0 60.3 jit_solution(13783004939158323005)
XLA Ops:
  0.6 0.0 copy-start
  0.6 0.8 %reshape.28.taps = f32[252]{0:T(256)S(1)} reshape(bf16[6,2,21]{2,1,0:T(2,128)(2,1)} %param.11) | data formatting | bytes 1512 | tf_op jit(solution)/shard_map/reshape | solution.py:607
  1.4 6.4 %match_img.1 = (bf16[3,528,128]{2,1,0:T(8,128)(2,1)S(1)}, bf16[3,528,128]{2,1,0:T(8,128)(2,1)S(1)}, bf16[1,528,128]{2,1,0:T(8,128)(2,1)S(1)}, bf16[1,528,128]{2,1,0:T(8,128)(2,1)S(1)}, bf16[32,128,128]{2,1,0:T(8,128)(2,1)S(1)}) custom-call(f32[8,6]{1,0:T(8,128)} %table_in.3, s32[1,1,2]{2,1,0:T(1,128)} %pick_in.3, s32[1,1,2]{2,1,0:T(1,128)} %visit_in.3, ...), custom_call_target="tpu_custom_call" | custom-call | tf_op jit(solution)/shard_map/match_img/pallas_call | solution.py:183
  7.8 1.4 %collective-permute-start = (bf16[3,528,128]{2,1,0:T(8,128)(2,1)S(1)}, bf16[3,528,128]{2,1,0:T(8,128)(2,1)S(1)}, u32[]{:S(2)}, u32[]{:S(2)}) collective-permute-start(bf16[3,528,128]{2,1,0:T(8,128)(2,1)S(1)} %get-tuple-element.46), channel_id=1, source_target_pairs={{0,8},{1,9},{2,10},{3,11},{4,12},{5,13},{6,14},{7,15},{8,0},{9,1},... | collective-permute-start | bytes 1216520 | tf_op jit(solution)/shard_map/ppermute | solution.py:224
  9.2 2.2 %collective-permute-start.1 = (bf16[3,528,128]{2,1,0:T(8,128)(2,1)S(1)}, bf16[3,528,128]{2,1,0:T(8,128)(2,1)S(1)}, u32[]{:S(2)}, u32[]{:S(2)}) collective-permute-start(bf16[3,528,128]{2,1,0:T(8,128)(2,1)S(1)} %get-tuple-element.47), channel_id=1, source_target_pairs={{0,1},{1,0},{2,3},{3,2},{4,5},{5,4},{6,7},{7,6},{8,16},{9,17},{10,... | collective-permute-start | bytes 1216520 | tf_op jit(solution)/shard_map/ppermute | solution.py:224
  11.3 6.4 %match_var.1 = (bf16[3,528,128]{2,1,0:T(8,128)(2,1)S(1)}, bf16[3,528,128]{2,1,0:T(8,128)(2,1)S(1)}, bf16[1,528,128]{2,1,0:T(8,128)(2,1)S(1)}, bf16[1,528,128]{2,1,0:T(8,128)(2,1)S(1)}, bf16[32,128,128]{2,1,0:T(8,128)(2,1)S(1)}) custom-call(f32[8,6]{1,0:T(8,128)} %table_in.3, s32[1,1,2]{2,1,0:T(1,128)} %pick_in.3, s32[1,1,2]{2,1,0:T(1,128)} %visit_in.3, ...), custom_call_target="tpu_custom_call" | custom-call | tf_op jit(solution)/shard_map/match_var/pallas_call | solution.py:183
  17.8 0.2 collective-permute-start.2
  18.0 1.4 %collective-permute-start.3 = (bf16[3,528,128]{2,1,0:T(8,128)(2,1)S(1)}, bf16[3,528,128]{2,1,0:T(8,128)(2,1)S(1)}, u32[]{:S(2)}, u32[]{:S(2)}) collective-permute-start(bf16[3,528,128]{2,1,0:T(8,128)(2,1)S(1)} %get-tuple-element.53), channel_id=1, source_target_pairs={{0,1},{1,0},{2,3},{3,2},{4,5},{5,4},{6,7},{7,6},{8,16},{9,17},{10,... | collective-permute-start | bytes 1216520 | tf_op jit(solution)/shard_map/ppermute | solution.py:224
  19.4 0.0 copy-done
  19.4 1.4 %own_var.1.start_ref = f32[1024,1024]{1,0:T(8,128)S(1)} custom-call(s32[32]{0:T(128)S(1)} %bitcast.3, bf16[32,128,128]{2,1,0:T(8,128)(2,1)S(1)} %get-tuple-element.49.own_ref), custom_call_target="tpu_custom_call" | custom-call | tf_op jit(solution)/shard_map/own_var/pallas_call | solution.py:269
  20.8 0.0 collective-permute-done.below_ref
  20.8 0.4 collective-permute-done.1.above_ref
  21.2 0.1 fusion.2
  21.3 1.9 %collective-permute-start.4 = (bf16[3,528,128]{2,1,0:T(8,128)(2,1)S(1)}, bf16[3,528,128]{2,1,0:T(8,128)(2,1)S(1)}, u32[]{:S(2)}, u32[]{:S(2)}) collective-permute-start(bf16[3,528,128]{2,1,0:T(8,128)(2,1)S(1)} %pad_maximum_fusion), channel_id=1, source_target_pairs={{0,1},{1,0},{2,3},{3,2},{4,5},{5,4},{6,7},{7,6},{8,9},{9,8},{10,11... | collective-permute-start | bytes 1216520 | tf_op jit(solution)/shard_map/ppermute | solution.py:224
  23.3 1.6 %collective-permute-start.5 = (bf16[3,528,128]{2,1,0:T(8,128)(2,1)S(1)}, bf16[3,528,128]{2,1,0:T(8,128)(2,1)S(1)}, u32[]{:S(2)}, u32[]{:S(2)}) collective-permute-start(bf16[3,528,128]{2,1,0:T(8,128)(2,1)S(1)} %pad_maximum_fusion.1), channel_id=1, source_target_pairs={{0,8},{1,2},{2,1},{3,4},{4,3},{5,6},{6,5},{7,15},{8,0},{9,10},{10,... | collective-permute-start | bytes 1216520 | tf_op jit(solution)/shard_map/ppermute | solution.py:224
  24.9 2.6 %collective-permute-done.2.below_ref = bf16[3,528,128]{2,1,0:T(8,128)(2,1)S(1)} collective-permute-done((bf16[3,528,128]{2,1,0:T(8,128)(2,1)S(1)}, bf16[3,528,128]{2,1,0:T(8,128)(2,1)S(1)}, u32[]{:S(2)}, u32[]{:S(2)}) %collective-permute-start.2) | collective-permute-done | bytes 405536 | tf_op jit(solution)/shard_map/ppermute | solution.py:224
  27.5 2.0 %collective-permute-done.3.above_ref = bf16[3,528,128]{2,1,0:T(8,128)(2,1)S(1)} collective-permute-done((bf16[3,528,128]{2,1,0:T(8,128)(2,1)S(1)}, bf16[3,528,128]{2,1,0:T(8,128)(2,1)S(1)}, u32[]{:S(2)}, u32[]{:S(2)}) %collective-permute-start.3) | collective-permute-done | bytes 405536 | tf_op jit(solution)/shard_map/ppermute | solution.py:224
  29.5 0.0 collective-permute-done.4.east_ref
  29.5 1.5 %collective-permute-done.5.west_ref = bf16[3,528,128]{2,1,0:T(8,128)(2,1)S(1)} collective-permute-done((bf16[3,528,128]{2,1,0:T(8,128)(2,1)S(1)}, bf16[3,528,128]{2,1,0:T(8,128)(2,1)S(1)}, u32[]{:S(2)}, u32[]{:S(2)}) %collective-permute-start.5) | collective-permute-done | bytes 405536 | tf_op jit(solution)/shard_map/ppermute | solution.py:224
  31.1 3.1 %collective-permute-start.6 = (bf16[3,528,128]{2,1,0:T(8,128)(2,1)S(1)}, bf16[3,528,128]{2,1,0:T(8,128)(2,1)S(1)}, u32[]{:S(2)}, u32[]{:S(2)}) collective-permute-start(bf16[3,528,128]{2,1,0:T(8,128)(2,1)S(1)} %pad_maximum_fusion.2), channel_id=1, source_target_pairs={{0,1},{1,0},{2,3},{3,2},{4,5},{5,4},{6,7},{7,6},{8,9},{9,8},{10,11... | collective-permute-start | bytes 1216520 | tf_op jit(solution)/shard_map/ppermute | solution.py:224
  34.3 0.1 collective-permute-start.7
  34.3 3.9 %gather_img.1 = (f32[1024,1024]{1,0:T(8,128)}, bf16[32,1024]{1,0:T(8,128)(2,1)S(1)}, bf16[32,1024]{1,0:T(8,128)(2,1)S(1)}, bf16[256,128]{1,0:T(8,128)(2,1)S(1)}, bf16[256,128]{1,0:T(8,128)(2,1)S(1)}) custom-call(s32[32]{0:T(128)S(1)} %bitcast.4, bf16[32,128,128]{2,1,0:T(8,128)(2,1)S(1)} %get-tuple-element.45.start_ref, ...), custom_call_target="tpu_custom_call" | custom-call | tf_op jit(solution)/shard_map/gather_img/pallas_call | solution.py:322
  38.2 0.0 collective-permute-done.6.east_ref
  38.2 3.6 %collective-permute-done.7.west_ref = bf16[3,528,128]{2,1,0:T(8,128)(2,1)S(1)} collective-permute-done((bf16[3,528,128]{2,1,0:T(8,128)(2,1)S(1)}, bf16[3,528,128]{2,1,0:T(8,128)(2,1)S(1)}, u32[]{:S(2)}, u32[]{:S(2)}) %collective-permute-start.7) | collective-permute-done | bytes 405536 | tf_op jit(solution)/shard_map/ppermute | solution.py:224
  41.9 0.0 copy-start.1
  41.9 2.1 %gather_var.1 = (bf16[1024,1024]{1,0:T(8,128)(2,1)S(1)}, bf16[48,1024]{1,0:T(8,128)(2,1)S(1)}, bf16[48,1024]{1,0:T(8,128)(2,1)S(1)}, bf16[384,128]{1,0:T(8,128)(2,1)S(1)}, bf16[384,128]{1,0:T(8,128)(2,1)S(1)}) custom-call(s32[32]{0:T(128)S(1)} %bitcast.5, f32[1024,1024]{1,0:T(8,128)S(1)} %own_var.1.start_ref, ...), custom_call_target="tpu_custom_call" | custom-call | tf_op jit(solution)/shard_map/gather_var/pallas_call | solution.py:322
  44.0 0.3 collective-permute-start.8
  44.3 2.0 %collective-permute-start.9 = (bf16[48,1024]{1,0:T(8,128)(2,1)S(1)}, bf16[48,1024]{1,0:T(8,128)(2,1)S(1)}, u32[]{:S(2)}, u32[]{:S(2)}) collective-permute-start(bf16[48,1024]{1,0:T(8,128)(2,1)S(1)} %get-tuple-element.70), channel_id=1, source_target_pairs={{0,1},{1,0},{2,3},{3,2},{4,5},{5,4},{6,7},{7,6},{8,16},{9,17},{10,... | collective-permute-start | bytes 294920 | tf_op jit(solution)/shard_map/ppermute | solution.py:224
  46.3 0.0 copy-done.1
  46.3 0.1 reshape.26.psf
  46.4 4.3 %column.1 = (bf16[1024,1024]{1,0:T(8,128)(2,1)S(1)}, bf16[1024,1024]{1,0:T(8,128)(2,1)S(1)}, bf16[1024,1024]{1,0:T(8,128)(2,1)S(1)}) custom-call(f32[62]{0:T(128)S(1)} %reshape.26.psf, f32[1024,1024]{1,0:T(8,128)} %get-tuple-element.42.tile_ref, bf16[1024,1024]{1,0:T(8,128)(2,1)S(1)} %get-tuple-element.68.var_ref), custom_call_target="tpu_custom_call" | custom-call | tf_op jit(solution)/shard_map/column/pallas_call | solution.py:416
  50.7 0.0 collective-permute-done.8.row_even.even_first.even_last
  50.7 0.0 collective-permute-done.9.row_odd.odd_first.odd_last
  50.7 0.1 turn.1
  50.8 1.1 %collective-permute-start.10 = (bf16[480,128]{1,0:T(8,128)(2,1)S(1)}, bf16[480,128]{1,0:T(8,128)(2,1)S(1)}, u32[]{:S(2)}, u32[]{:S(2)}) collective-permute-start(bf16[480,128]{1,0:T(8,128)(2,1)S(1)} %get-tuple-element.80), channel_id=1, source_target_pairs={{0,1},{1,0},{2,3},{3,2},{4,5},{5,4},{6,7},{7,6},{8,9},{9,8},{10,11... | collective-permute-start | bytes 368648 | tf_op jit(solution)/shard_map/ppermute | solution.py:224
  51.9 0.0 collective-permute-start.11
  51.9 5.7 %row.1 = (f32[1024,1024]{1,0:T(8,128)}, f32[2,1024,256]{2,1,0:T(8,128)S(1)}) custom-call(f32[62]{0:T(128)S(1)} %reshape.26.psf, f32[1024,1024]{1,0:T(8,128)} %get-tuple-element.42.tile_ref, bf16[1024,1024]{1,0:T(8,128)(2,1)S(1)} %get-tuple-element.68.var_ref, bf16[1024,1024]{1,0:T(8,128)(2,1)S(1)} %get-tuple-element.72.v_high, ...), custom_call_target="tpu_custom_call" | custom-call | tf_op jit(solution)/shard_map/row/pallas_call | solution.py:521
  57.6 0.0 collective-permute-done.10.col_even
  57.6 0.0 collective-permute-done.11.col_odd
  57.6 2.5 %side.1 = f32[1024,1024]{1,0:T(8,128)} custom-call(f32[62]{0:T(128)S(1)} %reshape.26.psf, f32[1024,1024]{1,0:T(8,128)} %get-tuple-element.77.held, f32[2,1024,256]{2,1,0:T(8,128)S(1)} %get-tuple-element.83.part_ref, bf16[480,128]{1,0:T(8,128)(2,1)S(1)} %collective-permute-done.10.col_even, ...), custom_call_target="tpu_custom_call", output_to_operand_aliasing={{}: (1, {})} | custom-call | tf_op jit(solution)/shard_map/side/pallas_call | solution.py:586
  (6 shorter events, 0.2 us)
Async XLA Ops:
  0.6 18.8 %copy-start = (s32[1,1,32]{2,1,0:T(1,128)S(1)}, s32[1,1,32]{2,1,0:T(1,128)}, u32[]{:S(2)}) copy-start(s32[1,1,32]{2,1,0:T(1,128)} %place_in.3) | copy-start | bytes 388
  7.8 13.0 %collective-permute-start = (bf16[3,528,128]{2,1,0:T(8,128)(2,1)S(1)}, bf16[3,528,128]{2,1,0:T(8,128)(2,1)S(1)}, u32[]{:S(2)}, u32[]{:S(2)}) collective-permute-start(bf16[3,528,128]{2,1,0:T(8,128)(2,1)S(1)} %get-tuple-element.46), channel_id=1, source_target_pairs={{0,8},{1,9},{2,10},{3,11},{4,12},{5,13},{6,14},{7,15},{8,0},{9,1},... | collective-permute-start | bytes 1216520 | tf_op jit(solution)/shard_map/ppermute | solution.py:224
  9.2 12.0 %collective-permute-start.1 = (bf16[3,528,128]{2,1,0:T(8,128)(2,1)S(1)}, bf16[3,528,128]{2,1,0:T(8,128)(2,1)S(1)}, u32[]{:S(2)}, u32[]{:S(2)}) collective-permute-start(bf16[3,528,128]{2,1,0:T(8,128)(2,1)S(1)} %get-tuple-element.47), channel_id=1, source_target_pairs={{0,1},{1,0},{2,3},{3,2},{4,5},{5,4},{6,7},{7,6},{8,16},{9,17},{10,... | collective-permute-start | bytes 1216520 | tf_op jit(solution)/shard_map/ppermute | solution.py:224
  17.8 9.7 %collective-permute-start.2 = (bf16[3,528,128]{2,1,0:T(8,128)(2,1)S(1)}, bf16[3,528,128]{2,1,0:T(8,128)(2,1)S(1)}, u32[]{:S(2)}, u32[]{:S(2)}) collective-permute-start(bf16[3,528,128]{2,1,0:T(8,128)(2,1)S(1)} %get-tuple-element.52), channel_id=1, source_target_pairs={{0,8},{1,9},{2,10},{3,11},{4,12},{5,13},{6,14},{7,15},{8,0},{9,1},... | collective-permute-start | bytes 1216520 | tf_op jit(solution)/shard_map/ppermute | solution.py:224
  18.0 11.5 %collective-permute-start.3 = (bf16[3,528,128]{2,1,0:T(8,128)(2,1)S(1)}, bf16[3,528,128]{2,1,0:T(8,128)(2,1)S(1)}, u32[]{:S(2)}, u32[]{:S(2)}) collective-permute-start(bf16[3,528,128]{2,1,0:T(8,128)(2,1)S(1)} %get-tuple-element.53), channel_id=1, source_target_pairs={{0,1},{1,0},{2,3},{3,2},{4,5},{5,4},{6,7},{7,6},{8,16},{9,17},{10,... | collective-permute-start | bytes 1216520 | tf_op jit(solution)/shard_map/ppermute | solution.py:224
  21.3 8.2 %collective-permute-start.4 = (bf16[3,528,128]{2,1,0:T(8,128)(2,1)S(1)}, bf16[3,528,128]{2,1,0:T(8,128)(2,1)S(1)}, u32[]{:S(2)}, u32[]{:S(2)}) collective-permute-start(bf16[3,528,128]{2,1,0:T(8,128)(2,1)S(1)} %pad_maximum_fusion), channel_id=1, source_target_pairs={{0,1},{1,0},{2,3},{3,2},{4,5},{5,4},{6,7},{7,6},{8,9},{9,8},{10,11... | collective-permute-start | bytes 1216520 | tf_op jit(solution)/shard_map/ppermute | solution.py:224
  23.3 7.7 %collective-permute-start.5 = (bf16[3,528,128]{2,1,0:T(8,128)(2,1)S(1)}, bf16[3,528,128]{2,1,0:T(8,128)(2,1)S(1)}, u32[]{:S(2)}, u32[]{:S(2)}) collective-permute-start(bf16[3,528,128]{2,1,0:T(8,128)(2,1)S(1)} %pad_maximum_fusion.1), channel_id=1, source_target_pairs={{0,8},{1,2},{2,1},{3,4},{4,3},{5,6},{6,5},{7,15},{8,0},{9,10},{10,... | collective-permute-start | bytes 1216520 | tf_op jit(solution)/shard_map/ppermute | solution.py:224
  31.1 7.1 %collective-permute-start.6 = (bf16[3,528,128]{2,1,0:T(8,128)(2,1)S(1)}, bf16[3,528,128]{2,1,0:T(8,128)(2,1)S(1)}, u32[]{:S(2)}, u32[]{:S(2)}) collective-permute-start(bf16[3,528,128]{2,1,0:T(8,128)(2,1)S(1)} %pad_maximum_fusion.2), channel_id=1, source_target_pairs={{0,1},{1,0},{2,3},{3,2},{4,5},{5,4},{6,7},{7,6},{8,9},{9,8},{10,11... | collective-permute-start | bytes 1216520 | tf_op jit(solution)/shard_map/ppermute | solution.py:224
  34.3 7.6 %collective-permute-start.7 = (bf16[3,528,128]{2,1,0:T(8,128)(2,1)S(1)}, bf16[3,528,128]{2,1,0:T(8,128)(2,1)S(1)}, u32[]{:S(2)}, u32[]{:S(2)}) collective-permute-start(bf16[3,528,128]{2,1,0:T(8,128)(2,1)S(1)} %pad_maximum_fusion.3), channel_id=1, source_target_pairs={{0,8},{1,2},{2,1},{3,4},{4,3},{5,6},{6,5},{7,15},{8,0},{9,10},{10,... | collective-permute-start | bytes 1216520 | tf_op jit(solution)/shard_map/ppermute | solution.py:224
  41.9 4.4 %copy-start.1 = (f32[2,31]{1,0:T(2,128)S(1)}, f32[2,31]{1,0:T(2,128)}, u32[]{:S(2)}) copy-start(f32[2,31]{1,0:T(2,128)} %param.17) | copy-start | bytes 748
  44.0 6.7 %collective-permute-start.8 = (bf16[48,1024]{1,0:T(8,128)(2,1)S(1)}, bf16[48,1024]{1,0:T(8,128)(2,1)S(1)}, u32[]{:S(2)}, u32[]{:S(2)}) collective-permute-start(bf16[48,1024]{1,0:T(8,128)(2,1)S(1)} %get-tuple-element.69), channel_id=1, source_target_pairs={{0,8},{1,9},{2,10},{3,11},{4,12},{5,13},{6,14},{7,15},{8,0},{9,1},... | collective-permute-start | bytes 294920 | tf_op jit(solution)/shard_map/ppermute | solution.py:224
  44.3 6.4 %collective-permute-start.9 = (bf16[48,1024]{1,0:T(8,128)(2,1)S(1)}, bf16[48,1024]{1,0:T(8,128)(2,1)S(1)}, u32[]{:S(2)}, u32[]{:S(2)}) collective-permute-start(bf16[48,1024]{1,0:T(8,128)(2,1)S(1)} %get-tuple-element.70), channel_id=1, source_target_pairs={{0,1},{1,0},{2,3},{3,2},{4,5},{5,4},{6,7},{7,6},{8,16},{9,17},{10,... | collective-permute-start | bytes 294920 | tf_op jit(solution)/shard_map/ppermute | solution.py:224
  50.8 6.8 %collective-permute-start.10 = (bf16[480,128]{1,0:T(8,128)(2,1)S(1)}, bf16[480,128]{1,0:T(8,128)(2,1)S(1)}, u32[]{:S(2)}, u32[]{:S(2)}) collective-permute-start(bf16[480,128]{1,0:T(8,128)(2,1)S(1)} %get-tuple-element.80), channel_id=1, source_target_pairs={{0,1},{1,0},{2,3},{3,2},{4,5},{5,4},{6,7},{7,6},{8,9},{9,8},{10,11... | collective-permute-start | bytes 368648 | tf_op jit(solution)/shard_map/ppermute | solution.py:224
  51.9 5.8 %collective-permute-start.11 = (bf16[480,128]{1,0:T(8,128)(2,1)S(1)}, bf16[480,128]{1,0:T(8,128)(2,1)S(1)}, u32[]{:S(2)}, u32[]{:S(2)}) collective-permute-start(bf16[480,128]{1,0:T(8,128)(2,1)S(1)} %get-tuple-element.81), channel_id=1, source_target_pairs={{0,8},{1,2},{2,1},{3,4},{4,3},{5,6},{6,5},{7,15},{8,0},{9,10},{10,... | collective-permute-start | bytes 368648 | tf_op jit(solution)/shard_map/ppermute | solution.py:224

commit v5 on v4

--- a/solution.py
+++ b/solution.py
@@ -232,7 +232,8 @@
     _, _, left, right = parcels
     leftward = jnp.concatenate([left, below[0:1], above[0:1]], 0)
     rightward = jnp.concatenate([right, below[2:3], above[2:3]], 0)
-    return below, above, swap(leftward, "tcol", False), swap(rightward, "tcol", True)
+    east = swap(rightward, "tcol", True)
+    return below, above, east, swap(leftward, "tcol", False)
 
 
 def pack(read, first):
@@ -540,7 +541,7 @@
     )(psf, tile, tile_var, *columns, *rims)
 
 
-def side_kernel(psf, held, part_ref, col_even, col_odd, out_ref, sides, bands, ends, v_side, out, out_sems):
+def side_kernel(psf, held, part_ref, col_odd, col_even, out_ref, sides, bands, ends, v_side, out, out_sems):
     col, cols_n = lax.axis_index("tcol"), lax.axis_size("tcol")
     scale = largest(psf, 0) * largest(psf, 1)
     column_bands(psf, bands)
@@ -626,7 +627,7 @@
     columns = list(column_pass(psf, tile_read, tile_var))
     *rows, columns[0] = lax.optimization_barrier((*rows, columns[0]))
     sides = turn(first, last, *rows)
-    met_sides = swap(sides[0], "tcol", False), swap(sides[1], "tcol", True)
+    met_sides = swap(sides[1], "tcol", True), swap(sides[0], "tcol", False)
     held, part = row_pass(psf, tile_read, tile_var, columns, *rows)
     *met_sides, part = lax.optimization_barrier((*met_sides, part))
     return tile, side_pass(psf, held, part, *met_sides)

time: 61 us -> 61.5 us (level)
  starting transfers between devices: 15.2 us -> 18.4 us
  waiting for transfers between devices: 10.2 us -> 7.15 us
    ppermute x12, starting transfers between devices: 15.2 us -> 18.4 us  [swap(): return lax.ppermute(value, ('trow', 'tcol'), pairs)]
    ppermute x12, waiting for transfers between devices: 10.2 us -> 7.15 us  [swap(): return lax.ppermute(value, ('trow', 'tcol'), pairs)]
where the time goes in v5:
time: 61.5 us; the launch traced here: 60.4 us
  Pallas kernels  32.8 us (53%)
  starting transfers between devices  18.4 us (30%)
  waiting for transfers between devices  7.15 us (12%)
  between operations  0.96 us (2%)
  local copies, waits for them, and re-layouts  0.95 us (2%)
    ppermute x12, starting transfers between devices, swap(): return lax.ppermute(value, ('trow', 'tcol'), pairs)  18.4 us
    pallas_call x2, Pallas kernels, match(): pl.pallas_call(functools.partial(match_kernel, squared), in_specs=[HBM] *...  12.8 us
    ppermute x12, waiting for transfers between devices, swap(): return lax.ppermute(value, ('trow', 'tcol'), pairs)  7.15 us
    pallas_call x2, Pallas kernels, gather(): pl.pallas_call(functools.partial(gather_kernel, image), in_specs=[SMEM()]...  5.94 us
    pallas_call x1, Pallas kernels, row_pass(): pl.pallas_call(row_kernel, in_specs=[SMEM(), HBM, HBM] + [VMEM] * 5, out_...  5.73 us
    pallas_call x1, Pallas kernels, column_pass(): pl.pallas_call(column_kernel, in_specs=[SMEM(), HBM, HBM], out_specs=[VME...  4.32 us
    pallas_call x1, Pallas kernels, side_pass(): pl.pallas_call(side_kernel, in_specs=[SMEM(), HBM] + [VMEM] * 3, out_spec...  2.52 us
    pallas_call x1, Pallas kernels, own_sum(): pl.pallas_call(add_own, in_specs=[SMEM(), VMEM], out_specs=VMEM, out_shap...  1.35 us
  transfers between devices with their start and end apart: 12, of which 5 were waited for; matrix products, arithmetic and copies ran while one was open for 0% of the time, Pallas kernels for 36%

profile of v5, /device:TPU:7, one launch (start us, length us, event | category | flops | bytes accessed | tf_op | source)
XLA Modules:
  0.0 60.4 jit_solution(616275634278224674)
XLA Ops:
  0.6 0.0 copy-start
  0.6 0.8 %reshape.28.taps = f32[252]{0:T(256)S(1)} reshape(bf16[6,2,21]{2,1,0:T(2,128)(2,1)} %param.11) | data formatting | bytes 1512 | tf_op jit(solution)/shard_map/reshape | solution.py:608
  1.4 6.4 %match_img.1 = (bf16[3,528,128]{2,1,0:T(8,128)(2,1)S(1)}, bf16[3,528,128]{2,1,0:T(8,128)(2,1)S(1)}, bf16[1,528,128]{2,1,0:T(8,128)(2,1)S(1)}, bf16[1,528,128]{2,1,0:T(8,128)(2,1)S(1)}, bf16[32,128,128]{2,1,0:T(8,128)(2,1)S(1)}) custom-call(f32[8,6]{1,0:T(8,128)} %table_in.3, s32[1,1,2]{2,1,0:T(1,128)} %pick_in.3, s32[1,1,2]{2,1,0:T(1,128)} %visit_in.3, ...), custom_call_target="tpu_custom_call" | custom-call | tf_op jit(solution)/shard_map/match_img/pallas_call | solution.py:183
  7.8 1.4 %collective-permute-start = (bf16[3,528,128]{2,1,0:T(8,128)(2,1)S(1)}, bf16[3,528,128]{2,1,0:T(8,128)(2,1)S(1)}, u32[]{:S(2)}, u32[]{:S(2)}) collective-permute-start(bf16[3,528,128]{2,1,0:T(8,128)(2,1)S(1)} %get-tuple-element.46), channel_id=1, source_target_pairs={{0,8},{1,9},{2,10},{3,11},{4,12},{5,13},{6,14},{7,15},{8,0},{9,1},... | collective-permute-start | bytes 1216520 | tf_op jit(solution)/shard_map/ppermute | solution.py:224
  9.2 2.2 %collective-permute-start.1 = (bf16[3,528,128]{2,1,0:T(8,128)(2,1)S(1)}, bf16[3,528,128]{2,1,0:T(8,128)(2,1)S(1)}, u32[]{:S(2)}, u32[]{:S(2)}) collective-permute-start(bf16[3,528,128]{2,1,0:T(8,128)(2,1)S(1)} %get-tuple-element.47), channel_id=1, source_target_pairs={{0,1},{1,0},{2,3},{3,2},{4,5},{5,4},{6,7},{7,6},{8,16},{9,17},{10,... | collective-permute-start | bytes 1216520 | tf_op jit(solution)/shard_map/ppermute | solution.py:224
  11.3 6.4 %match_var.1 = (bf16[3,528,128]{2,1,0:T(8,128)(2,1)S(1)}, bf16[3,528,128]{2,1,0:T(8,128)(2,1)S(1)}, bf16[1,528,128]{2,1,0:T(8,128)(2,1)S(1)}, bf16[1,528,128]{2,1,0:T(8,128)(2,1)S(1)}, bf16[32,128,128]{2,1,0:T(8,128)(2,1)S(1)}) custom-call(f32[8,6]{1,0:T(8,128)} %table_in.3, s32[1,1,2]{2,1,0:T(1,128)} %pick_in.3, s32[1,1,2]{2,1,0:T(1,128)} %visit_in.3, ...), custom_call_target="tpu_custom_call" | custom-call | tf_op jit(solution)/shard_map/match_var/pallas_call | solution.py:183
  17.8 0.2 collective-permute-start.2
  18.0 1.4 %collective-permute-start.3 = (bf16[3,528,128]{2,1,0:T(8,128)(2,1)S(1)}, bf16[3,528,128]{2,1,0:T(8,128)(2,1)S(1)}, u32[]{:S(2)}, u32[]{:S(2)}) collective-permute-start(bf16[3,528,128]{2,1,0:T(8,128)(2,1)S(1)} %get-tuple-element.53), channel_id=1, source_target_pairs={{0,1},{1,0},{2,3},{3,2},{4,5},{5,4},{6,7},{7,6},{8,16},{9,17},{10,... | collective-permute-start | bytes 1216520 | tf_op jit(solution)/shard_map/ppermute | solution.py:224
  19.4 0.0 copy-done
  19.4 1.4 %own_var.1.start_ref = f32[1024,1024]{1,0:T(8,128)S(1)} custom-call(s32[32]{0:T(128)S(1)} %bitcast.3, bf16[32,128,128]{2,1,0:T(8,128)(2,1)S(1)} %get-tuple-element.49.own_ref), custom_call_target="tpu_custom_call" | custom-call | tf_op jit(solution)/shard_map/own_var/pallas_call | solution.py:270
  20.7 0.0 collective-permute-done.below_ref
  20.8 0.5 collective-permute-done.1.above_ref
  21.2 0.1 fusion.2
  21.3 3.5 %collective-permute-start.4 = (bf16[3,528,128]{2,1,0:T(8,128)(2,1)S(1)}, bf16[3,528,128]{2,1,0:T(8,128)(2,1)S(1)}, u32[]{:S(2)}, u32[]{:S(2)}) collective-permute-start(bf16[3,528,128]{2,1,0:T(8,128)(2,1)S(1)} %pad_maximum_fusion), channel_id=1, source_target_pairs={{0,8},{1,2},{2,1},{3,4},{4,3},{5,6},{6,5},{7,15},{8,0},{9,10},{10,... | collective-permute-start | bytes 1216520 | tf_op jit(solution)/shard_map/ppermute | solution.py:224
  24.8 0.1 collective-permute-start.5
  24.9 2.6 %collective-permute-done.2.below_ref = bf16[3,528,128]{2,1,0:T(8,128)(2,1)S(1)} collective-permute-done((bf16[3,528,128]{2,1,0:T(8,128)(2,1)S(1)}, bf16[3,528,128]{2,1,0:T(8,128)(2,1)S(1)}, u32[]{:S(2)}, u32[]{:S(2)}) %collective-permute-start.2) | collective-permute-done | bytes 405536 | tf_op jit(solution)/shard_map/ppermute | solution.py:224
  27.5 2.0 %collective-permute-done.3.above_ref = bf16[3,528,128]{2,1,0:T(8,128)(2,1)S(1)} collective-permute-done((bf16[3,528,128]{2,1,0:T(8,128)(2,1)S(1)}, bf16[3,528,128]{2,1,0:T(8,128)(2,1)S(1)}, u32[]{:S(2)}, u32[]{:S(2)}) %collective-permute-start.3) | collective-permute-done | bytes 405536 | tf_op jit(solution)/shard_map/ppermute | solution.py:224
  29.5 1.2 %collective-permute-done.4.east_ref = bf16[3,528,128]{2,1,0:T(8,128)(2,1)S(1)} collective-permute-done((bf16[3,528,128]{2,1,0:T(8,128)(2,1)S(1)}, bf16[3,528,128]{2,1,0:T(8,128)(2,1)S(1)}, u32[]{:S(2)}, u32[]{:S(2)}) %collective-permute-start.4) | collective-permute-done | bytes 405536 | tf_op jit(solution)/shard_map/ppermute | solution.py:224
  30.7 0.0 collective-permute-done.5.west_ref
  30.8 2.8 %collective-permute-start.6 = (bf16[3,528,128]{2,1,0:T(8,128)(2,1)S(1)}, bf16[3,528,128]{2,1,0:T(8,128)(2,1)S(1)}, u32[]{:S(2)}, u32[]{:S(2)}) collective-permute-start(bf16[3,528,128]{2,1,0:T(8,128)(2,1)S(1)} %pad_maximum_fusion.2), channel_id=1, source_target_pairs={{0,8},{1,2},{2,1},{3,4},{4,3},{5,6},{6,5},{7,15},{8,0},{9,10},{10,... | collective-permute-start | bytes 1216520 | tf_op jit(solution)/shard_map/ppermute | solution.py:224
  33.7 1.1 %collective-permute-start.7 = (bf16[3,528,128]{2,1,0:T(8,128)(2,1)S(1)}, bf16[3,528,128]{2,1,0:T(8,128)(2,1)S(1)}, u32[]{:S(2)}, u32[]{:S(2)}) collective-permute-start(bf16[3,528,128]{2,1,0:T(8,128)(2,1)S(1)} %pad_maximum_fusion.3), channel_id=1, source_target_pairs={{0,1},{1,0},{2,3},{3,2},{4,5},{5,4},{6,7},{7,6},{8,9},{9,8},{10,11... | collective-permute-start | bytes 1216520 | tf_op jit(solution)/shard_map/ppermute | solution.py:224
  34.8 3.8 %gather_img.1 = (f32[1024,1024]{1,0:T(8,128)}, bf16[32,1024]{1,0:T(8,128)(2,1)S(1)}, bf16[32,1024]{1,0:T(8,128)(2,1)S(1)}, bf16[256,128]{1,0:T(8,128)(2,1)S(1)}, bf16[256,128]{1,0:T(8,128)(2,1)S(1)}) custom-call(s32[32]{0:T(128)S(1)} %bitcast.4, bf16[32,128,128]{2,1,0:T(8,128)(2,1)S(1)} %get-tuple-element.45.start_ref, ...), custom_call_target="tpu_custom_call" | custom-call | tf_op jit(solution)/shard_map/gather_img/pallas_call | solution.py:323
  38.6 0.9 %collective-permute-done.6.east_ref = bf16[3,528,128]{2,1,0:T(8,128)(2,1)S(1)} collective-permute-done((bf16[3,528,128]{2,1,0:T(8,128)(2,1)S(1)}, bf16[3,528,128]{2,1,0:T(8,128)(2,1)S(1)}, u32[]{:S(2)}, u32[]{:S(2)}) %collective-permute-start.6) | collective-permute-done | bytes 405536 | tf_op jit(solution)/shard_map/ppermute | solution.py:224
  39.5 0.0 collective-permute-done.7.west_ref
  39.5 0.0 copy-start.1
  39.5 2.1 %gather_var.1 = (bf16[1024,1024]{1,0:T(8,128)(2,1)S(1)}, bf16[48,1024]{1,0:T(8,128)(2,1)S(1)}, bf16[48,1024]{1,0:T(8,128)(2,1)S(1)}, bf16[384,128]{1,0:T(8,128)(2,1)S(1)}, bf16[384,128]{1,0:T(8,128)(2,1)S(1)}) custom-call(s32[32]{0:T(128)S(1)} %bitcast.5, f32[1024,1024]{1,0:T(8,128)S(1)} %own_var.1.start_ref, ...), custom_call_target="tpu_custom_call" | custom-call | tf_op jit(solution)/shard_map/gather_var/pallas_call | solution.py:323
  41.7 0.6 %collective-permute-start.8 = (bf16[48,1024]{1,0:T(8,128)(2,1)S(1)}, bf16[48,1024]{1,0:T(8,128)(2,1)S(1)}, u32[]{:S(2)}, u32[]{:S(2)}) collective-permute-start(bf16[48,1024]{1,0:T(8,128)(2,1)S(1)} %get-tuple-element.69), channel_id=1, source_target_pairs={{0,8},{1,9},{2,10},{3,11},{4,12},{5,13},{6,14},{7,15},{8,0},{9,1},... | collective-permute-start | bytes 294920 | tf_op jit(solution)/shard_map/ppermute | solution.py:224
  42.3 1.8 %collective-permute-start.9 = (bf16[48,1024]{1,0:T(8,128)(2,1)S(1)}, bf16[48,1024]{1,0:T(8,128)(2,1)S(1)}, u32[]{:S(2)}, u32[]{:S(2)}) collective-permute-start(bf16[48,1024]{1,0:T(8,128)(2,1)S(1)} %get-tuple-element.70), channel_id=1, source_target_pairs={{0,1},{1,0},{2,3},{3,2},{4,5},{5,4},{6,7},{7,6},{8,16},{9,17},{10,... | collective-permute-start | bytes 294920 | tf_op jit(solution)/shard_map/ppermute | solution.py:224
  44.1 0.0 copy-done.1
  44.1 0.1 reshape.26.psf
  44.1 4.3 %column.1 = (bf16[1024,1024]{1,0:T(8,128)(2,1)S(1)}, bf16[1024,1024]{1,0:T(8,128)(2,1)S(1)}, bf16[1024,1024]{1,0:T(8,128)(2,1)S(1)}) custom-call(f32[62]{0:T(128)S(1)} %reshape.26.psf, f32[1024,1024]{1,0:T(8,128)} %get-tuple-element.42.tile_ref, bf16[1024,1024]{1,0:T(8,128)(2,1)S(1)} %get-tuple-element.68.var_ref), custom_call_target="tpu_custom_call" | custom-call | tf_op jit(solution)/shard_map/column/pallas_call | solution.py:417
  48.5 0.0 collective-permute-done.8.row_even.even_first.even_last
  48.5 0.0 collective-permute-done.9.row_odd.odd_first.odd_last
  48.5 0.1 turn.1
  48.6 2.2 %collective-permute-start.10 = (bf16[480,128]{1,0:T(8,128)(2,1)S(1)}, bf16[480,128]{1,0:T(8,128)(2,1)S(1)}, u32[]{:S(2)}, u32[]{:S(2)}) collective-permute-start(bf16[480,128]{1,0:T(8,128)(2,1)S(1)} %get-tuple-element.80), channel_id=1, source_target_pairs={{0,8},{1,2},{2,1},{3,4},{4,3},{5,6},{6,5},{7,15},{8,0},{9,10},{10,... | collective-permute-start | bytes 368648 | tf_op jit(solution)/shard_map/ppermute | solution.py:224
  50.8 1.2 %collective-permute-start.11 = (bf16[480,128]{1,0:T(8,128)(2,1)S(1)}, bf16[480,128]{1,0:T(8,128)(2,1)S(1)}, u32[]{:S(2)}, u32[]{:S(2)}) collective-permute-start(bf16[480,128]{1,0:T(8,128)(2,1)S(1)} %get-tuple-element.81), channel_id=1, source_target_pairs={{0,1},{1,0},{2,3},{3,2},{4,5},{5,4},{6,7},{7,6},{8,9},{9,8},{10,11... | collective-permute-start | bytes 368648 | tf_op jit(solution)/shard_map/ppermute | solution.py:224
  52.0 5.7 %row.1 = (f32[1024,1024]{1,0:T(8,128)}, f32[2,1024,256]{2,1,0:T(8,128)S(1)}) custom-call(f32[62]{0:T(128)S(1)} %reshape.26.psf, f32[1024,1024]{1,0:T(8,128)} %get-tuple-element.42.tile_ref, bf16[1024,1024]{1,0:T(8,128)(2,1)S(1)} %get-tuple-element.68.var_ref, bf16[1024,1024]{1,0:T(8,128)(2,1)S(1)} %get-tuple-element.72.v_high, ...), custom_call_target="tpu_custom_call" | custom-call | tf_op jit(solution)/shard_map/row/pallas_call | solution.py:522
  57.7 0.0 collective-permute-done.10.col_odd
  57.7 0.0 collective-permute-done.11.col_even
  57.7 2.5 %side.1 = f32[1024,1024]{1,0:T(8,128)} custom-call(f32[62]{0:T(128)S(1)} %reshape.26.psf, f32[1024,1024]{1,0:T(8,128)} %get-tuple-element.77.held, f32[2,1024,256]{2,1,0:T(8,128)S(1)} %get-tuple-element.83.part_ref, bf16[480,128]{1,0:T(8,128)(2,1)S(1)} %collective-permute-done.10.col_odd, ...), custom_call_target="tpu_custom_call", output_to_operand_aliasing={{}: (1, {})} | custom-call | tf_op jit(solution)/shard_map/side/pallas_call | solution.py:587
  (6 shorter events, 0.2 us)
Async XLA Ops:
  0.6 18.8 %copy-start = (s32[1,1,32]{2,1,0:T(1,128)S(1)}, s32[1,1,32]{2,1,0:T(1,128)}, u32[]{:S(2)}) copy-start(s32[1,1,32]{2,1,0:T(1,128)} %place_in.3) | copy-start | bytes 388
  7.8 13.0 %collective-permute-start = (bf16[3,528,128]{2,1,0:T(8,128)(2,1)S(1)}, bf16[3,528,128]{2,1,0:T(8,128)(2,1)S(1)}, u32[]{:S(2)}, u32[]{:S(2)}) collective-permute-start(bf16[3,528,128]{2,1,0:T(8,128)(2,1)S(1)} %get-tuple-element.46), channel_id=1, source_target_pairs={{0,8},{1,9},{2,10},{3,11},{4,12},{5,13},{6,14},{7,15},{8,0},{9,1},... | collective-permute-start | bytes 1216520 | tf_op jit(solution)/shard_map/ppermute | solution.py:224
  9.2 12.0 %collective-permute-start.1 = (bf16[3,528,128]{2,1,0:T(8,128)(2,1)S(1)}, bf16[3,528,128]{2,1,0:T(8,128)(2,1)S(1)}, u32[]{:S(2)}, u32[]{:S(2)}) collective-permute-start(bf16[3,528,128]{2,1,0:T(8,128)(2,1)S(1)} %get-tuple-element.47), channel_id=1, source_target_pairs={{0,1},{1,0},{2,3},{3,2},{4,5},{5,4},{6,7},{7,6},{8,16},{9,17},{10,... | collective-permute-start | bytes 1216520 | tf_op jit(solution)/shard_map/ppermute | solution.py:224
  17.8 9.7 %collective-permute-start.2 = (bf16[3,528,128]{2,1,0:T(8,128)(2,1)S(1)}, bf16[3,528,128]{2,1,0:T(8,128)(2,1)S(1)}, u32[]{:S(2)}, u32[]{:S(2)}) collective-permute-start(bf16[3,528,128]{2,1,0:T(8,128)(2,1)S(1)} %get-tuple-element.52), channel_id=1, source_target_pairs={{0,8},{1,9},{2,10},{3,11},{4,12},{5,13},{6,14},{7,15},{8,0},{9,1},... | collective-permute-start | bytes 1216520 | tf_op jit(solution)/shard_map/ppermute | solution.py:224
  18.0 11.5 %collective-permute-start.3 = (bf16[3,528,128]{2,1,0:T(8,128)(2,1)S(1)}, bf16[3,528,128]{2,1,0:T(8,128)(2,1)S(1)}, u32[]{:S(2)}, u32[]{:S(2)}) collective-permute-start(bf16[3,528,128]{2,1,0:T(8,128)(2,1)S(1)} %get-tuple-element.53), channel_id=1, source_target_pairs={{0,1},{1,0},{2,3},{3,2},{4,5},{5,4},{6,7},{7,6},{8,16},{9,17},{10,... | collective-permute-start | bytes 1216520 | tf_op jit(solution)/shard_map/ppermute | solution.py:224
  21.3 9.4 %collective-permute-start.4 = (bf16[3,528,128]{2,1,0:T(8,128)(2,1)S(1)}, bf16[3,528,128]{2,1,0:T(8,128)(2,1)S(1)}, u32[]{:S(2)}, u32[]{:S(2)}) collective-permute-start(bf16[3,528,128]{2,1,0:T(8,128)(2,1)S(1)} %pad_maximum_fusion), channel_id=1, source_target_pairs={{0,8},{1,2},{2,1},{3,4},{4,3},{5,6},{6,5},{7,15},{8,0},{9,10},{10,... | collective-permute-start | bytes 1216520 | tf_op jit(solution)/shard_map/ppermute | solution.py:224
  24.8 5.8 %collective-permute-start.5 = (bf16[3,528,128]{2,1,0:T(8,128)(2,1)S(1)}, bf16[3,528,128]{2,1,0:T(8,128)(2,1)S(1)}, u32[]{:S(2)}, u32[]{:S(2)}) collective-permute-start(bf16[3,528,128]{2,1,0:T(8,128)(2,1)S(1)} %pad_maximum_fusion.1), channel_id=1, source_target_pairs={{0,1},{1,0},{2,3},{3,2},{4,5},{5,4},{6,7},{7,6},{8,9},{9,8},{10,11... | collective-permute-start | bytes 1216520 | tf_op jit(solution)/shard_map/ppermute | solution.py:224
  30.8 8.7 %collective-permute-start.6 = (bf16[3,528,128]{2,1,0:T(8,128)(2,1)S(1)}, bf16[3,528,128]{2,1,0:T(8,128)(2,1)S(1)}, u32[]{:S(2)}, u32[]{:S(2)}) collective-permute-start(bf16[3,528,128]{2,1,0:T(8,128)(2,1)S(1)} %pad_maximum_fusion.2), channel_id=1, source_target_pairs={{0,8},{1,2},{2,1},{3,4},{4,3},{5,6},{6,5},{7,15},{8,0},{9,10},{10,... | collective-permute-start | bytes 1216520 | tf_op jit(solution)/shard_map/ppermute | solution.py:224
  33.7 5.8 %collective-permute-start.7 = (bf16[3,528,128]{2,1,0:T(8,128)(2,1)S(1)}, bf16[3,528,128]{2,1,0:T(8,128)(2,1)S(1)}, u32[]{:S(2)}, u32[]{:S(2)}) collective-permute-start(bf16[3,528,128]{2,1,0:T(8,128)(2,1)S(1)} %pad_maximum_fusion.3), channel_id=1, source_target_pairs={{0,1},{1,0},{2,3},{3,2},{4,5},{5,4},{6,7},{7,6},{8,9},{9,8},{10,11... | collective-permute-start | bytes 1216520 | tf_op jit(solution)/shard_map/ppermute | solution.py:224
  39.5 4.5 %copy-start.1 = (f32[2,31]{1,0:T(2,128)S(1)}, f32[2,31]{1,0:T(2,128)}, u32[]{:S(2)}) copy-start(f32[2,31]{1,0:T(2,128)} %param.17) | copy-start | bytes 748
  41.7 6.8 %collective-permute-start.8 = (bf16[48,1024]{1,0:T(8,128)(2,1)S(1)}, bf16[48,1024]{1,0:T(8,128)(2,1)S(1)}, u32[]{:S(2)}, u32[]{:S(2)}) collective-permute-start(bf16[48,1024]{1,0:T(8,128)(2,1)S(1)} %get-tuple-element.69), channel_id=1, source_target_pairs={{0,8},{1,9},{2,10},{3,11},{4,12},{5,13},{6,14},{7,15},{8,0},{9,1},... | collective-permute-start | bytes 294920 | tf_op jit(solution)/shard_map/ppermute | solution.py:224
  42.3 6.2 %collective-permute-start.9 = (bf16[48,1024]{1,0:T(8,128)(2,1)S(1)}, bf16[48,1024]{1,0:T(8,128)(2,1)S(1)}, u32[]{:S(2)}, u32[]{:S(2)}) collective-permute-start(bf16[48,1024]{1,0:T(8,128)(2,1)S(1)} %get-tuple-element.70), channel_id=1, source_target_pairs={{0,1},{1,0},{2,3},{3,2},{4,5},{5,4},{6,7},{7,6},{8,16},{9,17},{10,... | collective-permute-start | bytes 294920 | tf_op jit(solution)/shard_map/ppermute | solution.py:224
  48.6 9.1 %collective-permute-start.10 = (bf16[480,128]{1,0:T(8,128)(2,1)S(1)}, bf16[480,128]{1,0:T(8,128)(2,1)S(1)}, u32[]{:S(2)}, u32[]{:S(2)}) collective-permute-start(bf16[480,128]{1,0:T(8,128)(2,1)S(1)} %get-tuple-element.80), channel_id=1, source_target_pairs={{0,8},{1,2},{2,1},{3,4},{4,3},{5,6},{6,5},{7,15},{8,0},{9,10},{10,... | collective-permute-start | bytes 368648 | tf_op jit(solution)/shard_map/ppermute | solution.py:224
  50.8 7.0 %collective-permute-start.11 = (bf16[480,128]{1,0:T(8,128)(2,1)S(1)}, bf16[480,128]{1,0:T(8,128)(2,1)S(1)}, u32[]{:S(2)}, u32[]{:S(2)}) collective-permute-start(bf16[480,128]{1,0:T(8,128)(2,1)S(1)} %get-tuple-element.81), channel_id=1, source_target_pairs={{0,1},{1,0},{2,3},{3,2},{4,5},{5,4},{6,7},{7,6},{8,9},{9,8},{10,11... | collective-permute-start | bytes 368648 | tf_op jit(solution)/shard_map/ppermute | solution.py:224

commit v6 on v4

--- a/solution.py
+++ b/solution.py
@@ -607,6 +607,7 @@
     taps = basis_taps.astype(F32).reshape(-1)
     psf = psf_taps.reshape(-1)
     pin = lambda x: pltpu.with_memory_space_constraint(x, pltpu.HBM)
+    place, psf = pin(place), pin(psf)
     small = (*map(pin, (coef_table, coef_pick, block_visit, visit_weight, patch_place)), taps)
 
     *parcels, own_image = match(False, *small, pin(ccd_image.reshape(2, BLOCK, BLOCK)))

time: 61 us -> 62 us (1.016)
  transfers between devices with their start and end apart: 12 -> 12, of which waited for: 5 -> 5; matrix products, arithmetic and copies ran while one was open for 0% -> 1% of each run, Pallas kernels for 36% -> 36%
where the time goes in v6:
time: 62 us; the launch traced here: 61.1 us
  Pallas kernels  33.4 us (54%)
  starting transfers between devices  15 us (24%)
  waiting for transfers between devices  10 us (16%)
  local copies, waits for them, and re-layouts  1.48 us (2%)
  between operations  0.96 us (2%)
    ppermute x12, starting transfers between devices, swap(): return lax.ppermute(value, ('trow', 'tcol'), pairs)  15 us
    pallas_call x2, Pallas kernels, match(): pl.pallas_call(functools.partial(match_kernel, squared), in_specs=[HBM] *...  12.8 us
    ppermute x12, waiting for transfers between devices, swap(): return lax.ppermute(value, ('trow', 'tcol'), pairs)  10 us
    pallas_call x2, Pallas kernels, gather(): pl.pallas_call(functools.partial(gather_kernel, image), in_specs=[SMEM()]...  6.35 us
    pallas_call x1, Pallas kernels, row_pass(): pl.pallas_call(row_kernel, in_specs=[SMEM(), HBM, HBM] + [VMEM] * 5, out_...  5.64 us
    pallas_call x1, Pallas kernels, column_pass(): pl.pallas_call(column_kernel, in_specs=[SMEM(), HBM, HBM], out_specs=[VME...  4.44 us
    pallas_call x1, Pallas kernels, side_pass(): pl.pallas_call(side_kernel, in_specs=[SMEM(), HBM] + [VMEM] * 3, out_spec...  2.64 us
    pallas_call x1, Pallas kernels, own_sum(): pl.pallas_call(add_own, in_specs=[SMEM(), VMEM], out_specs=VMEM, out_shap...  1.45 us
  transfers between devices with their start and end apart: 12, of which 5 were waited for; matrix products, arithmetic and copies ran while one was open for 1% of the time, Pallas kernels for 36%

profile of v6, /device:TPU:7, one launch (start us, length us, event | category | flops | bytes accessed | tf_op | source)
XLA Modules:
  0.0 61.1 jit_solution(12148703514277733407)
XLA Ops:
  0.6 0.8 %reshape.28.taps = f32[252]{0:T(256)S(1)} reshape(bf16[6,2,21]{2,1,0:T(2,128)(2,1)} %param.11) | data formatting | bytes 1512 | tf_op jit(solution)/shard_map/reshape | solution.py:607
  1.4 6.4 %match_img.1 = (bf16[3,528,128]{2,1,0:T(8,128)(2,1)S(1)}, bf16[3,528,128]{2,1,0:T(8,128)(2,1)S(1)}, bf16[1,528,128]{2,1,0:T(8,128)(2,1)S(1)}, bf16[1,528,128]{2,1,0:T(8,128)(2,1)S(1)}, bf16[32,128,128]{2,1,0:T(8,128)(2,1)S(1)}) custom-call(f32[8,6]{1,0:T(8,128)} %table_in.3, s32[1,1,2]{2,1,0:T(1,128)} %pick_in.3, s32[1,1,2]{2,1,0:T(1,128)} %visit_in.3, ...), custom_call_target="tpu_custom_call" | custom-call | tf_op jit(solution)/shard_map/match_img/pallas_call | solution.py:183
  7.8 1.4 %collective-permute-start = (bf16[3,528,128]{2,1,0:T(8,128)(2,1)S(1)}, bf16[3,528,128]{2,1,0:T(8,128)(2,1)S(1)}, u32[]{:S(2)}, u32[]{:S(2)}) collective-permute-start(bf16[3,528,128]{2,1,0:T(8,128)(2,1)S(1)} %get-tuple-element.46), channel_id=1, source_target_pairs={{0,8},{1,9},{2,10},{3,11},{4,12},{5,13},{6,14},{7,15},{8,0},{9,1},... | collective-permute-start | bytes 1216520 | tf_op jit(solution)/shard_map/ppermute | solution.py:224
  9.2 2.2 %collective-permute-start.1 = (bf16[3,528,128]{2,1,0:T(8,128)(2,1)S(1)}, bf16[3,528,128]{2,1,0:T(8,128)(2,1)S(1)}, u32[]{:S(2)}, u32[]{:S(2)}) collective-permute-start(bf16[3,528,128]{2,1,0:T(8,128)(2,1)S(1)} %get-tuple-element.47), channel_id=1, source_target_pairs={{0,1},{1,0},{2,3},{3,2},{4,5},{5,4},{6,7},{7,6},{8,16},{9,17},{10,... | collective-permute-start | bytes 1216520 | tf_op jit(solution)/shard_map/ppermute | solution.py:224
  11.3 6.4 %match_var.1 = (bf16[3,528,128]{2,1,0:T(8,128)(2,1)S(1)}, bf16[3,528,128]{2,1,0:T(8,128)(2,1)S(1)}, bf16[1,528,128]{2,1,0:T(8,128)(2,1)S(1)}, bf16[1,528,128]{2,1,0:T(8,128)(2,1)S(1)}, bf16[32,128,128]{2,1,0:T(8,128)(2,1)S(1)}) custom-call(f32[8,6]{1,0:T(8,128)} %table_in.3, s32[1,1,2]{2,1,0:T(1,128)} %pick_in.3, s32[1,1,2]{2,1,0:T(1,128)} %visit_in.3, ...), custom_call_target="tpu_custom_call" | custom-call | tf_op jit(solution)/shard_map/match_var/pallas_call | solution.py:183
  17.8 0.2 collective-permute-start.2
  18.0 1.4 %collective-permute-start.3 = (bf16[3,528,128]{2,1,0:T(8,128)(2,1)S(1)}, bf16[3,528,128]{2,1,0:T(8,128)(2,1)S(1)}, u32[]{:S(2)}, u32[]{:S(2)}) collective-permute-start(bf16[3,528,128]{2,1,0:T(8,128)(2,1)S(1)} %get-tuple-element.53), channel_id=1, source_target_pairs={{0,1},{1,0},{2,3},{3,2},{4,5},{5,4},{6,7},{7,6},{8,16},{9,17},{10,... | collective-permute-start | bytes 1216520 | tf_op jit(solution)/shard_map/ppermute | solution.py:224
  19.4 1.4 %own_var.1.start_ref = f32[1024,1024]{1,0:T(8,128)S(1)} custom-call(s32[32]{0:T(128)} %bitcast.5, bf16[32,128,128]{2,1,0:T(8,128)(2,1)S(1)} %get-tuple-element.49.own_ref), custom_call_target="tpu_custom_call" | custom-call | tf_op jit(solution)/shard_map/own_var/pallas_call | solution.py:269
  20.8 0.0 collective-permute-done.below_ref
  20.8 0.4 collective-permute-done.1.above_ref
  21.2 0.1 fusion.2
  21.3 1.9 %collective-permute-start.4 = (bf16[3,528,128]{2,1,0:T(8,128)(2,1)S(1)}, bf16[3,528,128]{2,1,0:T(8,128)(2,1)S(1)}, u32[]{:S(2)}, u32[]{:S(2)}) collective-permute-start(bf16[3,528,128]{2,1,0:T(8,128)(2,1)S(1)} %pad_maximum_fusion), channel_id=1, source_target_pairs={{0,1},{1,0},{2,3},{3,2},{4,5},{5,4},{6,7},{7,6},{8,9},{9,8},{10,11... | collective-permute-start | bytes 1216520 | tf_op jit(solution)/shard_map/ppermute | solution.py:224
  23.3 1.6 %collective-permute-start.5 = (bf16[3,528,128]{2,1,0:T(8,128)(2,1)S(1)}, bf16[3,528,128]{2,1,0:T(8,128)(2,1)S(1)}, u32[]{:S(2)}, u32[]{:S(2)}) collective-permute-start(bf16[3,528,128]{2,1,0:T(8,128)(2,1)S(1)} %pad_maximum_fusion.1), channel_id=1, source_target_pairs={{0,8},{1,2},{2,1},{3,4},{4,3},{5,6},{6,5},{7,15},{8,0},{9,10},{10,... | collective-permute-start | bytes 1216520 | tf_op jit(solution)/shard_map/ppermute | solution.py:224
  24.9 2.6 %collective-permute-done.2.below_ref = bf16[3,528,128]{2,1,0:T(8,128)(2,1)S(1)} collective-permute-done((bf16[3,528,128]{2,1,0:T(8,128)(2,1)S(1)}, bf16[3,528,128]{2,1,0:T(8,128)(2,1)S(1)}, u32[]{:S(2)}, u32[]{:S(2)}) %collective-permute-start.2) | collective-permute-done | bytes 405536 | tf_op jit(solution)/shard_map/ppermute | solution.py:224
  27.5 2.0 %collective-permute-done.3.above_ref = bf16[3,528,128]{2,1,0:T(8,128)(2,1)S(1)} collective-permute-done((bf16[3,528,128]{2,1,0:T(8,128)(2,1)S(1)}, bf16[3,528,128]{2,1,0:T(8,128)(2,1)S(1)}, u32[]{:S(2)}, u32[]{:S(2)}) %collective-permute-start.3) | collective-permute-done | bytes 405536 | tf_op jit(solution)/shard_map/ppermute | solution.py:224
  29.5 0.0 collective-permute-done.4.east_ref
  29.5 1.5 %collective-permute-done.5.west_ref = bf16[3,528,128]{2,1,0:T(8,128)(2,1)S(1)} collective-permute-done((bf16[3,528,128]{2,1,0:T(8,128)(2,1)S(1)}, bf16[3,528,128]{2,1,0:T(8,128)(2,1)S(1)}, u32[]{:S(2)}, u32[]{:S(2)}) %collective-permute-start.5) | collective-permute-done | bytes 405536 | tf_op jit(solution)/shard_map/ppermute | solution.py:224
  31.1 3.1 %collective-permute-start.6 = (bf16[3,528,128]{2,1,0:T(8,128)(2,1)S(1)}, bf16[3,528,128]{2,1,0:T(8,128)(2,1)S(1)}, u32[]{:S(2)}, u32[]{:S(2)}) collective-permute-start(bf16[3,528,128]{2,1,0:T(8,128)(2,1)S(1)} %pad_maximum_fusion.2), channel_id=1, source_target_pairs={{0,1},{1,0},{2,3},{3,2},{4,5},{5,4},{6,7},{7,6},{8,9},{9,8},{10,11... | collective-permute-start | bytes 1216520 | tf_op jit(solution)/shard_map/ppermute | solution.py:224
  34.2 0.1 collective-permute-start.7
  34.3 4.0 %gather_img.1 = (f32[1024,1024]{1,0:T(8,128)}, bf16[32,1024]{1,0:T(8,128)(2,1)S(1)}, bf16[32,1024]{1,0:T(8,128)(2,1)S(1)}, bf16[256,128]{1,0:T(8,128)(2,1)S(1)}, bf16[256,128]{1,0:T(8,128)(2,1)S(1)}) custom-call(s32[32]{0:T(128)} %bitcast.6, bf16[32,128,128]{2,1,0:T(8,128)(2,1)S(1)} %get-tuple-element.45.start_ref, ...), custom_call_target="tpu_custom_call" | custom-call | tf_op jit(solution)/shard_map/gather_img/pallas_call | solution.py:322
  38.3 0.0 collective-permute-done.6.east_ref
  38.3 3.5 %collective-permute-done.7.west_ref = bf16[3,528,128]{2,1,0:T(8,128)(2,1)S(1)} collective-permute-done((bf16[3,528,128]{2,1,0:T(8,128)(2,1)S(1)}, bf16[3,528,128]{2,1,0:T(8,128)(2,1)S(1)}, u32[]{:S(2)}, u32[]{:S(2)}) %collective-permute-start.7) | collective-permute-done | bytes 405536 | tf_op jit(solution)/shard_map/ppermute | solution.py:224
  41.9 0.0 copy-start
  41.9 2.4 %gather_var.1 = (bf16[1024,1024]{1,0:T(8,128)(2,1)S(1)}, bf16[48,1024]{1,0:T(8,128)(2,1)S(1)}, bf16[48,1024]{1,0:T(8,128)(2,1)S(1)}, bf16[384,128]{1,0:T(8,128)(2,1)S(1)}, bf16[384,128]{1,0:T(8,128)(2,1)S(1)}) custom-call(s32[32]{0:T(128)} %bitcast.7, f32[1024,1024]{1,0:T(8,128)S(1)} %own_var.1.start_ref, ...), custom_call_target="tpu_custom_call" | custom-call | tf_op jit(solution)/shard_map/gather_var/pallas_call | solution.py:322
  44.3 0.2 collective-permute-start.8
  44.5 2.0 %collective-permute-start.9 = (bf16[48,1024]{1,0:T(8,128)(2,1)S(1)}, bf16[48,1024]{1,0:T(8,128)(2,1)S(1)}, u32[]{:S(2)}, u32[]{:S(2)}) collective-permute-start(bf16[48,1024]{1,0:T(8,128)(2,1)S(1)} %get-tuple-element.70), channel_id=1, source_target_pairs={{0,1},{1,0},{2,3},{3,2},{4,5},{5,4},{6,7},{7,6},{8,16},{9,17},{10,... | collective-permute-start | bytes 294920 | tf_op jit(solution)/shard_map/ppermute | solution.py:224
  46.5 0.0 copy-done
  46.5 0.6 %reshape.26.psf = f32[62]{0:T(128)} reshape(f32[2,31]{1,0:T(2,128)S(1)} %copy-done) | data formatting | bytes 496 | tf_op jit(solution)/shard_map/reshape | solution.py:608
  47.1 4.4 %column.1 = (bf16[1024,1024]{1,0:T(8,128)(2,1)S(1)}, bf16[1024,1024]{1,0:T(8,128)(2,1)S(1)}, bf16[1024,1024]{1,0:T(8,128)(2,1)S(1)}) custom-call(f32[62]{0:T(128)} %reshape.26.psf, f32[1024,1024]{1,0:T(8,128)} %get-tuple-element.42.tile_ref, bf16[1024,1024]{1,0:T(8,128)(2,1)S(1)} %get-tuple-element.68.var_ref), custom_call_target="tpu_custom_call" | custom-call | tf_op jit(solution)/shard_map/column/pallas_call | solution.py:416
  51.6 0.0 collective-permute-done.8.row_even.even_first.even_last
  51.6 0.0 collective-permute-done.9.row_odd.odd_first.odd_last
  51.6 0.1 turn.1
  51.7 0.9 %collective-permute-start.10 = (bf16[480,128]{1,0:T(8,128)(2,1)S(1)}, bf16[480,128]{1,0:T(8,128)(2,1)S(1)}, u32[]{:S(2)}, u32[]{:S(2)}) collective-permute-start(bf16[480,128]{1,0:T(8,128)(2,1)S(1)} %get-tuple-element.80), channel_id=1, source_target_pairs={{0,1},{1,0},{2,3},{3,2},{4,5},{5,4},{6,7},{7,6},{8,9},{9,8},{10,11... | collective-permute-start | bytes 368648 | tf_op jit(solution)/shard_map/ppermute | solution.py:224
  52.6 0.0 collective-permute-start.11
  52.6 5.6 %row.1 = (f32[1024,1024]{1,0:T(8,128)}, f32[2,1024,256]{2,1,0:T(8,128)S(1)}) custom-call(f32[62]{0:T(128)} %reshape.26.psf, f32[1024,1024]{1,0:T(8,128)} %get-tuple-element.42.tile_ref, bf16[1024,1024]{1,0:T(8,128)(2,1)S(1)} %get-tuple-element.68.var_ref, bf16[1024,1024]{1,0:T(8,128)(2,1)S(1)} %get-tuple-element.72.v_high, ...), custom_call_target="tpu_custom_call" | custom-call | tf_op jit(solution)/shard_map/row/pallas_call | solution.py:521
  58.3 0.0 collective-permute-done.10.col_even
  58.3 0.0 collective-permute-done.11.col_odd
  58.3 2.6 %side.1 = f32[1024,1024]{1,0:T(8,128)} custom-call(f32[62]{0:T(128)} %reshape.26.psf, f32[1024,1024]{1,0:T(8,128)} %get-tuple-element.77.held, f32[2,1024,256]{2,1,0:T(8,128)S(1)} %get-tuple-element.83.part_ref, bf16[480,128]{1,0:T(8,128)(2,1)S(1)} %collective-permute-done.10.col_even, ...), custom_call_target="tpu_custom_call", output_to_operand_aliasing={{}: (1, {})} | custom-call | tf_op jit(solution)/shard_map/side/pallas_call | solution.py:586
  (6 shorter events, 0.2 us)
Async XLA Ops:
  7.8 13.0 %collective-permute-start = (bf16[3,528,128]{2,1,0:T(8,128)(2,1)S(1)}, bf16[3,528,128]{2,1,0:T(8,128)(2,1)S(1)}, u32[]{:S(2)}, u32[]{:S(2)}) collective-permute-start(bf16[3,528,128]{2,1,0:T(8,128)(2,1)S(1)} %get-tuple-element.46), channel_id=1, source_target_pairs={{0,8},{1,9},{2,10},{3,11},{4,12},{5,13},{6,14},{7,15},{8,0},{9,1},... | collective-permute-start | bytes 1216520 | tf_op jit(solution)/shard_map/ppermute | solution.py:224
  9.2 12.0 %collective-permute-start.1 = (bf16[3,528,128]{2,1,0:T(8,128)(2,1)S(1)}, bf16[3,528,128]{2,1,0:T(8,128)(2,1)S(1)}, u32[]{:S(2)}, u32[]{:S(2)}) collective-permute-start(bf16[3,528,128]{2,1,0:T(8,128)(2,1)S(1)} %get-tuple-element.47), channel_id=1, source_target_pairs={{0,1},{1,0},{2,3},{3,2},{4,5},{5,4},{6,7},{7,6},{8,16},{9,17},{10,... | collective-permute-start | bytes 1216520 | tf_op jit(solution)/shard_map/ppermute | solution.py:224
  17.8 9.7 %collective-permute-start.2 = (bf16[3,528,128]{2,1,0:T(8,128)(2,1)S(1)}, bf16[3,528,128]{2,1,0:T(8,128)(2,1)S(1)}, u32[]{:S(2)}, u32[]{:S(2)}) collective-permute-start(bf16[3,528,128]{2,1,0:T(8,128)(2,1)S(1)} %get-tuple-element.52), channel_id=1, source_target_pairs={{0,8},{1,9},{2,10},{3,11},{4,12},{5,13},{6,14},{7,15},{8,0},{9,1},... | collective-permute-start | bytes 1216520 | tf_op jit(solution)/shard_map/ppermute | solution.py:224
  18.0 11.5 %collective-permute-start.3 = (bf16[3,528,128]{2,1,0:T(8,128)(2,1)S(1)}, bf16[3,528,128]{2,1,0:T(8,128)(2,1)S(1)}, u32[]{:S(2)}, u32[]{:S(2)}) collective-permute-start(bf16[3,528,128]{2,1,0:T(8,128)(2,1)S(1)} %get-tuple-element.53), channel_id=1, source_target_pairs={{0,1},{1,0},{2,3},{3,2},{4,5},{5,4},{6,7},{7,6},{8,16},{9,17},{10,... | collective-permute-start | bytes 1216520 | tf_op jit(solution)/shard_map/ppermute | solution.py:224
  21.3 8.2 %collective-permute-start.4 = (bf16[3,528,128]{2,1,0:T(8,128)(2,1)S(1)}, bf16[3,528,128]{2,1,0:T(8,128)(2,1)S(1)}, u32[]{:S(2)}, u32[]{:S(2)}) collective-permute-start(bf16[3,528,128]{2,1,0:T(8,128)(2,1)S(1)} %pad_maximum_fusion), channel_id=1, source_target_pairs={{0,1},{1,0},{2,3},{3,2},{4,5},{5,4},{6,7},{7,6},{8,9},{9,8},{10,11... | collective-permute-start | bytes 1216520 | tf_op jit(solution)/shard_map/ppermute | solution.py:224
  23.3 7.7 %collective-permute-start.5 = (bf16[3,528,128]{2,1,0:T(8,128)(2,1)S(1)}, bf16[3,528,128]{2,1,0:T(8,128)(2,1)S(1)}, u32[]{:S(2)}, u32[]{:S(2)}) collective-permute-start(bf16[3,528,128]{2,1,0:T(8,128)(2,1)S(1)} %pad_maximum_fusion.1), channel_id=1, source_target_pairs={{0,8},{1,2},{2,1},{3,4},{4,3},{5,6},{6,5},{7,15},{8,0},{9,10},{10,... | collective-permute-start | bytes 1216520 | tf_op jit(solution)/shard_map/ppermute | solution.py:224
  31.1 7.2 %collective-permute-start.6 = (bf16[3,528,128]{2,1,0:T(8,128)(2,1)S(1)}, bf16[3,528,128]{2,1,0:T(8,128)(2,1)S(1)}, u32[]{:S(2)}, u32[]{:S(2)}) collective-permute-start(bf16[3,528,128]{2,1,0:T(8,128)(2,1)S(1)} %pad_maximum_fusion.2), channel_id=1, source_target_pairs={{0,1},{1,0},{2,3},{3,2},{4,5},{5,4},{6,7},{7,6},{8,9},{9,8},{10,11... | collective-permute-start | bytes 1216520 | tf_op jit(solution)/shard_map/ppermute | solution.py:224
  34.2 7.6 %collective-permute-start.7 = (bf16[3,528,128]{2,1,0:T(8,128)(2,1)S(1)}, bf16[3,528,128]{2,1,0:T(8,128)(2,1)S(1)}, u32[]{:S(2)}, u32[]{:S(2)}) collective-permute-start(bf16[3,528,128]{2,1,0:T(8,128)(2,1)S(1)} %pad_maximum_fusion.3), channel_id=1, source_target_pairs={{0,8},{1,2},{2,1},{3,4},{4,3},{5,6},{6,5},{7,15},{8,0},{9,10},{10,... | collective-permute-start | bytes 1216520 | tf_op jit(solution)/shard_map/ppermute | solution.py:224
  41.9 4.7 %copy-start = (f32[2,31]{1,0:T(2,128)S(1)}, f32[2,31]{1,0:T(2,128)}, u32[]{:S(2)}) copy-start(f32[2,31]{1,0:T(2,128)} %param.17) | copy-start | bytes 748
  44.3 7.3 %collective-permute-start.8 = (bf16[48,1024]{1,0:T(8,128)(2,1)S(1)}, bf16[48,1024]{1,0:T(8,128)(2,1)S(1)}, u32[]{:S(2)}, u32[]{:S(2)}) collective-permute-start(bf16[48,1024]{1,0:T(8,128)(2,1)S(1)} %get-tuple-element.69), channel_id=1, source_target_pairs={{0,8},{1,9},{2,10},{3,11},{4,12},{5,13},{6,14},{7,15},{8,0},{9,1},... | collective-permute-start | bytes 294920 | tf_op jit(solution)/shard_map/ppermute | solution.py:224
  44.5 7.1 %collective-permute-start.9 = (bf16[48,1024]{1,0:T(8,128)(2,1)S(1)}, bf16[48,1024]{1,0:T(8,128)(2,1)S(1)}, u32[]{:S(2)}, u32[]{:S(2)}) collective-permute-start(bf16[48,1024]{1,0:T(8,128)(2,1)S(1)} %get-tuple-element.70), channel_id=1, source_target_pairs={{0,1},{1,0},{2,3},{3,2},{4,5},{5,4},{6,7},{7,6},{8,16},{9,17},{10,... | collective-permute-start | bytes 294920 | tf_op jit(solution)/shard_map/ppermute | solution.py:224
  51.7 6.6 %collective-permute-start.10 = (bf16[480,128]{1,0:T(8,128)(2,1)S(1)}, bf16[480,128]{1,0:T(8,128)(2,1)S(1)}, u32[]{:S(2)}, u32[]{:S(2)}) collective-permute-start(bf16[480,128]{1,0:T(8,128)(2,1)S(1)} %get-tuple-element.80), channel_id=1, source_target_pairs={{0,1},{1,0},{2,3},{3,2},{4,5},{5,4},{6,7},{7,6},{8,9},{9,8},{10,11... | collective-permute-start | bytes 368648 | tf_op jit(solution)/shard_map/ppermute | solution.py:224
  52.6 5.7 %collective-permute-start.11 = (bf16[480,128]{1,0:T(8,128)(2,1)S(1)}, bf16[480,128]{1,0:T(8,128)(2,1)S(1)}, u32[]{:S(2)}, u32[]{:S(2)}) collective-permute-start(bf16[480,128]{1,0:T(8,128)(2,1)S(1)} %get-tuple-element.81), channel_id=1, source_target_pairs={{0,8},{1,2},{2,1},{3,4},{4,3},{5,6},{6,5},{7,15},{8,0},{9,10},{10,... | collective-permute-start | bytes 368648 | tf_op jit(solution)/shard_map/ppermute | solution.py:224
